TPU v7x, 32 devices: a whole 2x2x4 slice. The times are simulated.
32 devices in a mesh: ka: 4 (over y, x), band: 8 (over z, core).
Axes of the slice: x: 2, y: 2, z: 4, core: 2. Of those that a mesh axis runs over, the one named last changes fastest.
Arguments:
- targets: float32 [32, 2, 24, 576], P(('ka', 'band')), may hold values from -6 to 6
- occupied: bfloat16 [32, 2, 24, 576], P(('ka', 'band')), may hold values from -3 to 3
- kernels: float32 [16, 24, 576], replicated, may hold values from 0.1 to 2
- partner: int32 [4], replicated, may hold values from 0 to 3, as said below
- kernel_index: int32 [8, 8], replicated, may hold values from 0 to 15
Outputs:
- exchange: float32 [32, 2, 24, 576], P(('ka', 'band'))
Inputs may be any that keep to these rules, and one draw needn't show every extreme that they name: partner is a permutation of the groups.
All inputs are finite; a program needn't handle non-finite values.
Results may differ from a plain program's by a relative error of at most 0.0003.
Values may be sent and summed in bfloat16 or wider, within the bound.
No kernel may reach another device: no remote copies, remote signals or barrier semaphores. Data moves between devices by JAX's collectives and lax.ppermute only.
A program may use at most 64 MiB of HBM per device.

v0:
```python
import jax
import jax.numpy as jnp
from jax import lax
from jax.sharding import PartitionSpec as P

GRID = 24
KPT_DEV = 2


def passed_along(array, axis, by):
    peers = lax.axis_size(axis)
    return lax.ppermute(array, axis, [(i, (i + by) % peers) for i in range(peers)])


def spectral_tables(grid_size):
    positions = jnp.arange(grid_size, dtype=jnp.int32)
    products = positions[:, None] * positions[None, :] % grid_size
    angles = products.astype(jnp.float32) * (2.0 * jnp.pi / grid_size)
    factor = 1.0 / jnp.sqrt(jnp.float32(grid_size))
    return (jnp.cos(angles) * factor, jnp.sin(angles) * factor)


def rotate_apply(source_field, matrix):
    batch_count, grid_size, plane_size = source_field.shape
    result = lax.dot_general(
        source_field,
        matrix,
        (((1,), (1,)), ((), ())),
        precision=lax.Precision.HIGHEST,
        preferred_element_type=jnp.float32,
    )
    return result.reshape(batch_count, grid_size, plane_size)


def transform(real_part, imag_part, cosine_table, sine_table, direction):
    for repeat in range(3):
        real_part, imag_part = (
            rotate_apply(real_part, cosine_table) - direction * rotate_apply(imag_part, sine_table),
            rotate_apply(imag_part, cosine_table) + direction * rotate_apply(real_part, sine_table),
        )
    return (real_part, imag_part)


def pair_term(orbital, target_real, target_imag, kernel, cosine_table, sine_table):
    orbital_values = orbital.astype(jnp.float32)
    orbital_real = orbital_values[0, 0]
    orbital_imag = orbital_values[0, 1]
    dens_real = orbital_real * target_real + orbital_imag * target_imag
    dens_imag = orbital_real * target_imag - orbital_imag * target_real
    spec_real, spec_imag = transform(dens_real, dens_imag, cosine_table, sine_table, -1.0)
    pot_real, pot_imag = transform(
        kernel * spec_real, kernel * spec_imag, cosine_table, sine_table, 1.0
    )
    return (
        orbital_real * pot_real - orbital_imag * pot_imag,
        orbital_real * pot_imag + orbital_imag * pot_real,
    )


def shards(targets, occupied, kernels, partner, kernel_index):
    band_count = lax.axis_size("band")
    per_kpoint = band_count // KPT_DEV
    my_group = lax.axis_index("ka")
    position = lax.axis_index("band")
    kpoint = my_group * KPT_DEV + position // per_kpoint
    cosine_table, sine_table = spectral_tables(GRID)
    target_real = targets[:, 0]
    target_imag = targets[:, 1]
    everyone = lax.all_gather(occupied, "ka", axis=0, tiled=True)
    partner_group = partner[my_group]
    visitor = lax.dynamic_slice_in_dim(everyone, partner_group, 1, 0)

    def contribute(totals, orbital, source_band):
        source_k = partner_group * KPT_DEV + source_band // per_kpoint
        table_row = kernel_index[kpoint, source_k]
        kernel = lax.dynamic_index_in_dim(kernels, table_row, 0, keepdims=False)
        more_real, more_imag = pair_term(
            orbital, target_real, target_imag, kernel, cosine_table, sine_table
        )
        return (totals[0] - more_real, totals[1] - more_imag)

    empty_field = jnp.zeros_like(target_real)
    totals = contribute((empty_field, empty_field), visitor, position)
    halfway = band_count // 2

    def both_sides(number, carried):
        ahead, behind, summed = carried
        ahead = passed_along(ahead, "band", 1)
        behind = passed_along(behind, "band", -1)
        summed = contribute(summed, ahead, (position - number) % band_count)
        summed = contribute(summed, behind, (position + number) % band_count)
        return (ahead, behind, summed)

    ahead, behind, totals = lax.fori_loop(1, halfway, both_sides, (visitor, visitor, totals))
    arrived = passed_along(ahead, "band", 1)
    totals = contribute(totals, arrived, (position - halfway) % band_count)
    return jnp.stack(totals, axis=1)


def solution(mesh):
    return jax.shard_map(
        shards,
        mesh=mesh,
        in_specs=(
            P(("ka", "band"), None, None, None),
            P(("ka", "band"), None, None, None),
            P(),
            P(),
            P(),
        ),
        out_specs=P(("ka", "band"), None, None, None),
        check_vma=False,
    )
```

profile of v0, /device:TPU:0, one launch (start us, length us, event | category | flops | bytes accessed | tf_op | source)
XLA Modules:
  0.0 129.7 jit_solution(3527982354289120434)
XLA Ops:
  0.0 0.7 copy-done.5
  0.7 0.6 dynamic_slice.63
  3.0 10.4 %all_gather.3 = bf16[4,2,24,576]{3,2,1,0:T(8,128)(2,1)S(1)} all-gather(bf16[1,2,24,576]{3,2,1,0:T(8,128)(2,1)S(1)} %copy-done.2), channel_id=1, replica_groups=mesh['ka'=4,'band'=8] {'ka'}, dimensions={0}, use_global_device_ids=true | all-gather | bytes 276480 | tf_op jit(solution)/shard_map/all_gather | solution.py:69
  14.1 0.9 copy-done.1
  17.1 0.3 fusion.265
  19.4 0.7 copy-done.3
  20.1 0.6 fusion.518
  23.2 0.3 fusion.291
  23.4 0.3 fusion.295
  23.7 0.3 convolution_add_fusion.11
  24.6 0.3 convolution_subtract_fusion.11
  28.2 85.2 %while.24 = (s32[]{:T(128)}, bf16[1,2,24,576]{3,2,1,0:T(8,128)(2,1)S(1)}, bf16[1,2,24,576]{3,2,1,0:T(8,128)(2,1)S(1)}, f32[1,24,576]{2,1,0:T(8,128)S(1)}, f32[1,...) while((s32[]{:T(128)}, ...), condition=%wide.region_1.2_spmd.clone.clone, body=%wide.region_0.1_spmd.clone.clone.sunk | while | flops 192430080 | bytes 14722047 | solution.py:94
  28.5 3.5 %collective-permute-start.1 = (bf16[1,2,24,576]{3,2,1,0:T(8,128)(2,1)S(1)}, bf16[1,2,24,576]{3,2,1,0:T(8,128)(2,1)S(1)}, u32[]{:S(2)}, u32[]{:S(2)}) collective-permute-start(bf16[1,2,24,576]{3,2,1,0:T(8,128)(2,1)S(1)} %get-tuple-element.801), channel_id=1, source_target_pairs={{0,7},{1,0},{2,1},{3,2},{4,3},{5,4},{6,5},{7,6},{8,15},{9,8},{10,9... | collective-permute-start | bytes 165896 | tf_op jit(solution)/shard_map/while/body/eval_jaxpr/ppermute | solution.py:12
  32.0 0.7 fusion.737
  41.5 0.3 fusion.760
  41.8 0.3 fusion.756
  42.1 0.3 convolution_add_fusion.21
  42.9 0.3 convolution_subtract_fusion.21
  51.6 0.3 fusion.742
  51.8 0.3 fusion.738
  52.1 0.3 convolution_add_fusion.18
  52.9 0.3 convolution_subtract_fusion.18
  56.8 3.5 %collective-permute-start.1 = (bf16[1,2,24,576]{3,2,1,0:T(8,128)(2,1)S(1)}, bf16[1,2,24,576]{3,2,1,0:T(8,128)(2,1)S(1)}, u32[]{:S(2)}, u32[]{:S(2)}) collective-permute-start(bf16[1,2,24,576]{3,2,1,0:T(8,128)(2,1)S(1)} %get-tuple-element.801), channel_id=1, source_target_pairs={{0,7},{1,0},{2,1},{3,2},{4,3},{5,4},{6,5},{7,6},{8,15},{9,8},{10,9... | collective-permute-start | bytes 165896 | tf_op jit(solution)/shard_map/while/body/eval_jaxpr/ppermute | solution.py:12
  60.3 0.7 fusion.737
  69.8 0.3 fusion.760
  70.1 0.3 fusion.756
  70.4 0.3 convolution_add_fusion.21
  71.2 0.3 convolution_subtract_fusion.21
  79.8 0.3 fusion.742
  80.1 0.3 fusion.738
  80.4 0.3 convolution_add_fusion.18
  81.2 0.3 convolution_subtract_fusion.18
  85.0 3.5 %collective-permute-start.1 = (bf16[1,2,24,576]{3,2,1,0:T(8,128)(2,1)S(1)}, bf16[1,2,24,576]{3,2,1,0:T(8,128)(2,1)S(1)}, u32[]{:S(2)}, u32[]{:S(2)}) collective-permute-start(bf16[1,2,24,576]{3,2,1,0:T(8,128)(2,1)S(1)} %get-tuple-element.801), channel_id=1, source_target_pairs={{0,7},{1,0},{2,1},{3,2},{4,3},{5,4},{6,5},{7,6},{8,15},{9,8},{10,9... | collective-permute-start | bytes 165896 | tf_op jit(solution)/shard_map/while/body/eval_jaxpr/ppermute | solution.py:12
  88.6 0.7 fusion.737
  98.1 0.3 fusion.760
  98.3 0.3 fusion.756
  98.6 0.3 convolution_add_fusion.21
  99.5 0.3 convolution_subtract_fusion.21
  108.1 0.3 fusion.742
  108.4 0.3 fusion.738
  108.6 0.3 convolution_add_fusion.18
  109.5 0.3 convolution_subtract_fusion.18
  115.4 3.5 %collective-permute-done.2 = bf16[1,2,24,576]{3,2,1,0:T(8,128)(2,1)S(1)} collective-permute-done((bf16[1,2,24,576]{3,2,1,0:T(8,128)(2,1)S(1)}, bf16[1,2,24,576]{3,2,1,0:T(8,128)(2,1)S(1)}, u32[]{:S(2)}, u32[]{:S(2)}) %collective-permute-start.2) | collective-permute-done | bytes 55328 | tf_op jit(solution)/shard_map/ppermute | solution.py:12
  124.0 0.3 fusion.279
  124.3 0.3 fusion.275
  124.5 0.3 convolution_subtract_fusion.8
  125.4 0.3 convolution_add_fusion.8
  129.1 0.6 copy-done.4
  (395 shorter events, 69.5 us)
Async XLA Ops:
  0.0 0.7 copy-start.5
  0.0 3.0 %copy-start.2 = (bf16[1,2,24,576]{3,2,1,0:T(8,128)(2,1)S(1)}, bf16[1,2,24,576]{3,2,1,0:T(8,128)(2,1)}, u32[]{:S(2)}) copy-start(bf16[1,2,24,576]{3,2,1,0:T(8,128)(2,1)} %param.8) | copy-start | bytes 165892
  14.0 0.9 copy-start.1
  18.5 4.6 %copy-start = (f32[16,24,576]{2,1,0:T(8,128)S(1)}, f32[16,24,576]{2,1,0:T(8,128)}, u32[]{:S(2)}) copy-start(f32[16,24,576]{2,1,0:T(8,128)} %param.9) | copy-start | bytes 2654212
  19.4 0.7 copy-start.3
  28.4 8.0 %collective-permute-start = (bf16[1,2,24,576]{3,2,1,0:T(8,128)(2,1)S(1)}, bf16[1,2,24,576]{3,2,1,0:T(8,128)(2,1)S(1)}, u32[]{:S(2)}, u32[]{:S(2)}) collective-permute-start(bf16[1,2,24,576]{3,2,1,0:T(8,128)(2,1)S(1)} %get-tuple-element.800), channel_id=1, source_target_pairs={{0,1},{1,2},{2,3},{3,4},{4,5},{5,6},{6,7},{7,0},{8,9},{9,10},{10,1... | collective-permute-start | bytes 165896 | tf_op jit(solution)/shard_map/while/body/eval_jaxpr/ppermute | solution.py:12
  28.5 8.0 %collective-permute-start.1 = (bf16[1,2,24,576]{3,2,1,0:T(8,128)(2,1)S(1)}, bf16[1,2,24,576]{3,2,1,0:T(8,128)(2,1)S(1)}, u32[]{:S(2)}, u32[]{:S(2)}) collective-permute-start(bf16[1,2,24,576]{3,2,1,0:T(8,128)(2,1)S(1)} %get-tuple-element.801), channel_id=1, source_target_pairs={{0,7},{1,0},{2,1},{3,2},{4,3},{5,4},{6,5},{7,6},{8,15},{9,8},{10,9... | collective-permute-start | bytes 165896 | tf_op jit(solution)/shard_map/while/body/eval_jaxpr/ppermute | solution.py:12
  56.7 8.0 %collective-permute-start = (bf16[1,2,24,576]{3,2,1,0:T(8,128)(2,1)S(1)}, bf16[1,2,24,576]{3,2,1,0:T(8,128)(2,1)S(1)}, u32[]{:S(2)}, u32[]{:S(2)}) collective-permute-start(bf16[1,2,24,576]{3,2,1,0:T(8,128)(2,1)S(1)} %get-tuple-element.800), channel_id=1, source_target_pairs={{0,1},{1,2},{2,3},{3,4},{4,5},{5,6},{6,7},{7,0},{8,9},{9,10},{10,1... | collective-permute-start | bytes 165896 | tf_op jit(solution)/shard_map/while/body/eval_jaxpr/ppermute | solution.py:12
  56.8 8.0 %collective-permute-start.1 = (bf16[1,2,24,576]{3,2,1,0:T(8,128)(2,1)S(1)}, bf16[1,2,24,576]{3,2,1,0:T(8,128)(2,1)S(1)}, u32[]{:S(2)}, u32[]{:S(2)}) collective-permute-start(bf16[1,2,24,576]{3,2,1,0:T(8,128)(2,1)S(1)} %get-tuple-element.801), channel_id=1, source_target_pairs={{0,7},{1,0},{2,1},{3,2},{4,3},{5,4},{6,5},{7,6},{8,15},{9,8},{10,9... | collective-permute-start | bytes 165896 | tf_op jit(solution)/shard_map/while/body/eval_jaxpr/ppermute | solution.py:12
  85.0 8.0 %collective-permute-start = (bf16[1,2,24,576]{3,2,1,0:T(8,128)(2,1)S(1)}, bf16[1,2,24,576]{3,2,1,0:T(8,128)(2,1)S(1)}, u32[]{:S(2)}, u32[]{:S(2)}) collective-permute-start(bf16[1,2,24,576]{3,2,1,0:T(8,128)(2,1)S(1)} %get-tuple-element.800), channel_id=1, source_target_pairs={{0,1},{1,2},{2,3},{3,4},{4,5},{5,6},{6,7},{7,0},{8,9},{9,10},{10,1... | collective-permute-start | bytes 165896 | tf_op jit(solution)/shard_map/while/body/eval_jaxpr/ppermute | solution.py:12
  85.0 8.0 %collective-permute-start.1 = (bf16[1,2,24,576]{3,2,1,0:T(8,128)(2,1)S(1)}, bf16[1,2,24,576]{3,2,1,0:T(8,128)(2,1)S(1)}, u32[]{:S(2)}, u32[]{:S(2)}) collective-permute-start(bf16[1,2,24,576]{3,2,1,0:T(8,128)(2,1)S(1)} %get-tuple-element.801), channel_id=1, source_target_pairs={{0,7},{1,0},{2,1},{3,2},{4,3},{5,4},{6,5},{7,6},{8,15},{9,8},{10,9... | collective-permute-start | bytes 165896 | tf_op jit(solution)/shard_map/while/body/eval_jaxpr/ppermute | solution.py:12
  113.5 5.5 %collective-permute-start.2 = (bf16[1,2,24,576]{3,2,1,0:T(8,128)(2,1)S(1)}, bf16[1,2,24,576]{3,2,1,0:T(8,128)(2,1)S(1)}, u32[]{:S(2)}, u32[]{:S(2)}) collective-permute-start(bf16[1,2,24,576]{3,2,1,0:T(8,128)(2,1)S(1)} %get-tuple-element.533), channel_id=1, source_target_pairs={{0,1},{1,2},{2,3},{3,4},{4,5},{5,6},{6,7},{7,0},{8,9},{9,10},{10,1... | collective-permute-start | bytes 165896 | tf_op jit(solution)/shard_map/ppermute | solution.py:12
  129.1 0.7 copy-start.4
where the time goes:
time: 130 us
  matrix products  49.9 us (38%)
  local copies, waits for them, and re-layouts  33.6 us (26%)
  loops' own time  13.9 us (11%)
  starting transfers between devices  10.8 us (8%)
  blocking collectives  10.4 us (8%)
  between operations  6.9 us (5%)
  waiting for transfers between devices  3.56 us (3%)
    dot_general x192, matrix products, rotate_apply(): lax.dot_general(source_field, matrix, (((1,), (1,)), ((), ())), precision...  49.9 us
    another operation x1, loops' own time, shards(): lax.fori_loop(1, halfway, both_sides, (visitor, visitor, totals))  13.9 us
    sub x96, local copies, waits for them, and re-layouts, transform(): rotate_apply(real_part, cosine_table)  13.8 us
    add x96, local copies, waits for them, and re-layouts, transform(): rotate_apply(imag_part, cosine_table)  13.8 us
    ppermute x7, starting transfers between devices, passed_along(): lax.ppermute(array, axis, [(i, (i + by) % peers) for i in range(peers)])  10.8 us
    all_gather x1, blocking collectives, shards(): everyone = lax.all_gather(occupied, 'ka', axis=0, tiled=True)  10.4 us
    ppermute x7, waiting for transfers between devices, passed_along(): lax.ppermute(array, axis, [(i, (i + by) % peers) for i in range(peers)])  3.56 us
    unnamed x13, local copies, waits for them, and re-layouts  2.85 us
  transfers between devices with their start and end apart: 7, of which 1 were waited for; matrix products, arithmetic and copies ran while one was open for 2% of the time, Pallas kernels for 0%

commit v1 on v0

v1 whole, which is shorter than its diff:
```python
import functools
import math

import jax
import jax.numpy as jnp
import ml_dtypes
import numpy as np
from jax import lax
from jax.experimental import pallas as pl
from jax.experimental.pallas import tpu as pltpu
from jax.sharding import PartitionSpec as P

KPT_DEV = 2
RADIX = 3
CHUNK = 8
BF16 = jnp.bfloat16
F32 = jnp.float32


def split_table(table):
    high = table.astype(ml_dtypes.bfloat16)
    low = (table - high.astype(np.float64)).astype(ml_dtypes.bfloat16)
    return high, low


def plane_tables(grid_size):
    inner = grid_size // RADIX
    b, c = np.divmod(np.arange(inner * grid_size), grid_size)
    found = []
    for residue in range(RADIX):
        turns = b[:, None] * (RADIX * b[None, :] + residue) + c[:, None] * c[None, :]
        angles = (turns % grid_size) * (2.0 * np.pi / grid_size)
        found.append([split_table(np.cos(angles)), split_table(np.sin(angles))])
    forward = np.array(found)
    return np.stack([forward, np.swapaxes(forward, -1, -2)])


def line_tables(grid_size):
    positions = np.arange(grid_size)
    angles = (positions[:, None] * positions[None, :] % grid_size) * (2.0 * np.pi / grid_size)
    found = []
    for sign in (1.0, -1.0):
        full = np.block(
            [
                [np.cos(angles), sign * np.sin(angles)],
                [-sign * np.sin(angles), np.cos(angles)],
            ]
        )
        high, low = split_table(full)
        found.append(np.concatenate([high, high, low], axis=1))
    return np.stack(found)


def halves(values):
    high = values.astype(BF16)
    return high, (values - high.astype(F32)).astype(BF16)


def dot(left, right):
    return jnp.dot(left, right, preferred_element_type=F32)


def line_transform(values, table):
    high, low = halves(values)
    return dot(table, jnp.concatenate([high, low, high], axis=0))


def plane_transform(batch, tables, sign):
    rows = batch[0].shape[0]
    half = rows // 2
    high, low = halves(jnp.concatenate(batch, axis=0))
    parts = []
    for which in range(2):
        table_high, table_low = tables[which]
        parts.append(dot(high, table_high) + dot(low, table_high) + dot(high, table_low))
    found = []
    for number in range(len(batch)):
        at = number * rows
        cosine = parts[0][at : at + rows]
        sine = parts[1][at : at + rows]
        found.append(
            jnp.concatenate(
                [
                    cosine[:half] + sign * sine[half:],
                    cosine[half:] - sign * sine[:half],
                ],
                axis=0,
            )
        )
    return found


def butterfly(first, second, third, sign):
    half = first.shape[0] // 2
    total = second + third
    turned = (second - third) * (math.sqrt(3.0) / 2.0)
    middle = first - 0.5 * total
    turned = jnp.concatenate([sign * turned[half:], -sign * turned[:half]], axis=0)
    return first + total, middle + turned, middle - turned


def prepare_body(partner_ref, index_ref, kernels_ref, out_ref, held, sems):
    group = lax.axis_index("ka")
    per_kpoint = lax.axis_size("band") // KPT_DEV
    kpoint = group * KPT_DEV + lax.axis_index("band") // per_kpoint
    grid_size = kernels_ref.shape[1]
    inner = grid_size // RADIX
    copies = []
    for local in range(KPT_DEV):
        row = index_ref[kpoint, partner_ref[group] * KPT_DEV + local]
        copy = pltpu.make_async_copy(kernels_ref.at[row], held.at[local], sems.at[local])
        copy.start()
        copies.append(copy)
    for copy in copies:
        copy.wait()
    scale = 1.0 / grid_size**3
    for local in range(KPT_DEV):
        values = held[local] * scale
        for residue in range(RADIX):
            blocks = []
            for q in range(inner):
                at = (RADIX * q + residue) * grid_size
                blocks.append(values[:, at : at + grid_size])
            out_ref[local, residue] = jnp.concatenate(blocks, axis=1)


def prepare(partner, kernel_index, kernels):
    grid_size, plane = kernels.shape[1:]
    return pl.pallas_call(
        prepare_body,
        out_shape=jax.ShapeDtypeStruct((KPT_DEV, RADIX, grid_size, plane // RADIX), F32),
        in_specs=[
            pl.BlockSpec(memory_space=pltpu.SMEM),
            pl.BlockSpec(memory_space=pltpu.SMEM),
            pl.BlockSpec(memory_space=pl.ANY),
        ],
        out_specs=pl.BlockSpec(memory_space=pltpu.VMEM),
        scratch_shapes=[
            pltpu.VMEM((KPT_DEV, grid_size, plane), F32),
            pltpu.SemaphoreType.DMA((KPT_DEV,)),
        ],
    )(partner, kernel_index, kernels)


def exchange_body(sources, target_ref, orbital_ref, kernel_ref, line_ref, plane_ref, out_ref):
    grid_size, plane = target_ref.shape[2:]
    width = plane // RADIX
    per_kpoint = lax.axis_size("band") // KPT_DEV
    position = lax.axis_index("band")
    lanes = [slice(block * width, (block + 1) * width) for block in range(RADIX)]
    target = [(target_ref[0, 0][:, at], target_ref[0, 1][:, at]) for at in lanes]

    def orbital_of(number):
        return [
            (orbital_ref[number, 0][:, at].astype(F32), orbital_ref[number, 1][:, at].astype(F32))
            for at in lanes
        ]

    def some(numbers, totals):
        fields = [[] for _ in range(RADIX)]
        for number in numbers:
            blocks = []
            for (real, imag), (target_real, target_imag) in zip(orbital_of(number), target):
                blocks.append(
                    jnp.concatenate(
                        [
                            real * target_real + imag * target_imag,
                            real * target_imag - imag * target_real,
                        ],
                        axis=0,
                    )
                )
            for residue, block in enumerate(butterfly(*blocks, 1.0)):
                fields[residue].append(block)
        for residue in range(RADIX):
            tables = [[plane_ref[0, residue, i, j] for j in range(2)] for i in range(2)]
            batch = plane_transform(fields[residue], tables, 1.0)
            for place, number in enumerate(numbers):
                local = sources(position, number) // per_kpoint
                kernel = kernel_ref[local, residue]
                values = line_transform(batch[place], line_ref[0])
                values = values * jnp.concatenate([kernel, kernel], axis=0)
                batch[place] = line_transform(values, line_ref[1])
            tables = [[plane_ref[1, residue, i, j] for j in range(2)] for i in range(2)]
            fields[residue] = plane_transform(batch, tables, -1.0)
        for place, number in enumerate(numbers):
            blocks = butterfly(*[fields[residue][place] for residue in range(RADIX)], -1.0)
            for block, (real, imag) in enumerate(orbital_of(number)):
                pot_real, pot_imag = blocks[block][:grid_size], blocks[block][grid_size:]
                totals[block] = (
                    totals[block][0] - (real * pot_real - imag * pot_imag),
                    totals[block][1] - (real * pot_imag + imag * pot_real),
                )
        return totals

    blank = jnp.zeros((grid_size, width), F32)
    totals = [(blank, blank) for _ in range(RADIX)]
    count = orbital_ref.shape[0]
    for start in range(0, count, CHUNK):
        totals = some(range(start, min(start + CHUNK, count)), totals)
    for part in range(2):
        out_ref[0, part] = jnp.concatenate([totals[block][part] for block in range(RADIX)], axis=1)


def exchange(sources, target, orbitals, kernels):
    grid_size = target.shape[2]
    return pl.pallas_call(
        functools.partial(exchange_body, sources),
        out_shape=jax.ShapeDtypeStruct(target.shape, F32),
        in_specs=[pl.BlockSpec(memory_space=pltpu.VMEM)] * 5,
        out_specs=pl.BlockSpec(memory_space=pltpu.VMEM),
        compiler_params=pltpu.CompilerParams(vmem_limit_bytes=32 * 1024 * 1024),
    )(target, orbitals, kernels, jnp.asarray(line_tables(grid_size)), jnp.asarray(plane_tables(grid_size)))


def shards(targets, occupied, kernels, partner, kernel_index):
    groups = lax.axis_size("ka")
    band_count = lax.axis_size("band")
    my_group = lax.axis_index("ka")
    kernel_blocks = prepare(partner, kernel_index, kernels)

    shift = (partner[my_group] - my_group) % groups
    visitor = occupied
    for by in range(1, groups):
        came = lax.ppermute(occupied, "ka", [((i + by) % groups, i) for i in range(groups)])
        visitor = jnp.where(shift == by, came, visitor)

    chips = band_count // 2
    visitors = [visitor]
    for step in range(1, chips):
        visitors.append(lax.ppermute(visitor, "band", [(i, i ^ (2 * step)) for i in range(band_count)]))
    stacked = jnp.concatenate(visitors, axis=0)
    others = lax.ppermute(stacked, "band", [(i, i ^ 1) for i in range(band_count)])
    orbitals = jnp.concatenate([stacked, others], axis=0)

    def sources(position, number):
        return position ^ (2 * (number % chips)) ^ (number // chips)

    return exchange(sources, targets, orbitals, kernel_blocks)


def solution(mesh):
    return jax.shard_map(
        shards,
        mesh=mesh,
        in_specs=(
            P(("ka", "band"), None, None, None),
            P(("ka", "band"), None, None, None),
            P(),
            P(),
            P(),
        ),
        out_specs=P(("ka", "band"), None, None, None),
        check_vma=False,
    )
```

time: 130 us -> 27.2 us (0.21)
  matrix products: 49.9 us -> 0 us
  local copies, waits for them, and re-layouts: 33.6 us -> 2.22 us
  loops' own time: 13.9 us -> 0 us
  blocking collectives: 10.4 us -> 0 us
  Pallas kernels: 0 us -> 6.67 us
  between operations: 6.9 us -> 0.77 us
  waiting for transfers between devices: 3.56 us -> 5.84 us
    dot_general x192 -> x0, matrix products: 49.9 us -> none  [rotate_apply(): lax.dot_general(source_field, matrix, (((1,), (1,)), ((), ())), precision...]
    another operation x1 -> x0, loops' own time: 13.9 us -> none  [shards(): lax.fori_loop(1, halfway, both_sides, (visitor, visitor, totals))]
    sub x96 -> x0, local copies, waits for them, and re-layouts: 13.8 us -> none  [transform(): rotate_apply(real_part, cosine_table)]
    add x96 -> x0, local copies, waits for them, and re-layouts: 13.8 us -> none  [transform(): rotate_apply(imag_part, cosine_table)]
    all_gather x1 -> x0, blocking collectives: 10.4 us -> none  [shards(): everyone = lax.all_gather(occupied, 'ka', axis=0, tiled=True)]
    pallas_call x0 -> x2, Pallas kernels: none -> 6.67 us  [the longest x1 4.21 us: exchange(): pl.pallas_call(functools.partial(exchange_body, sources), out_shape=jax.S...]
    ppermute x7, waiting for transfers between devices: 3.56 us -> 5.84 us  [the longest x3 3.32 us: shards(): lax.ppermute(visitor, 'band', [(i, i ^ 2 * step) for i in range(band_coun...]
    dynamic_slice x5 -> x1, local copies, waits for them, and re-layouts: 3.15 us -> 1.24 us  [shards(): shift = (partner[my_group] - my_group) % groups]
  transfers between devices with their start and end apart: 7 -> 7, of which waited for: 1 -> 4; matrix products, arithmetic and copies ran while one was open for 2% -> 5% of each run, Pallas kernels for 0% -> 9%
where the time goes in v1:
time: 27.2 us; the launch traced here: 26.9 us
  starting transfers between devices  10.5 us (39%)
  Pallas kernels  6.67 us (25%)
  waiting for transfers between devices  5.84 us (21%)
  local copies, waits for them, and re-layouts  2.22 us (8%)
  other arithmetic  0.92 us (3%)
  between operations  0.77 us (3%)
    ppermute x3, starting transfers between devices, shards(): lax.ppermute(occupied, 'ka', [((i + by) % groups, i) for i in range(group...  5.95 us
    ppermute x3, starting transfers between devices, shards(): lax.ppermute(visitor, 'band', [(i, i ^ 2 * step) for i in range(band_coun...  4.45 us
    pallas_call x1, Pallas kernels, exchange(): pl.pallas_call(functools.partial(exchange_body, sources), out_shape=jax.S...  4.21 us
    ppermute x3, waiting for transfers between devices, shards(): lax.ppermute(visitor, 'band', [(i, i ^ 2 * step) for i in range(band_coun...  3.32 us
    pallas_call x1, Pallas kernels, prepare(): pl.pallas_call(prepare_body, out_shape=jax.ShapeDtypeStruct((KPT_DEV, RAD...  2.46 us
    ppermute x1, waiting for transfers between devices, shards(): lax.ppermute(stacked, 'band', [(i, i ^ 1) for i in range(band_count)])  1.44 us
    dynamic_slice x1, local copies, waits for them, and re-layouts, shards(): shift = (partner[my_group] - my_group) % groups  1.24 us
    ppermute x3, waiting for transfers between devices, shards(): lax.ppermute(occupied, 'ka', [((i + by) % groups, i) for i in range(group...  1.07 us
  transfers between devices with their start and end apart: 7, of which 4 were waited for; matrix products, arithmetic and copies ran while one was open for 5% of the time, Pallas kernels for 9%

profile of v1, /device:TPU:0, one launch (start us, length us, event | category | flops | bytes accessed | tf_op | source)
XLA Modules:
  0.0 26.9 jit_solution(4983743468418602634)
XLA Ops:
  0.0 0.0 copy-start.3
  0.0 0.0 copy-start
  0.0 0.0 copy-start.2
  0.0 3.0 %collective-permute-start = (bf16[1,2,24,576]{3,2,1,0:T(8,128)(2,1)}, bf16[1,2,24,576]{3,2,1,0:T(8,128)(2,1)S(1)}, u32[]{:S(2)}, u32[]{:S(2)}) collective-permute-start(bf16[1,2,24,576]{3,2,1,0:T(8,128)(2,1)} %param.8), channel_id=1, source_target_pairs={{24,0},{0,8},{8,16},{16,24},{25,1},{1,9},{9,17},{17,25},{26,2},{2,... | collective-permute-start | bytes 165896 | tf_op jit(solution)/shard_map/ppermute | solution.py:225
  3.0 1.5 %collective-permute-start.1 = (bf16[1,2,24,576]{3,2,1,0:T(8,128)(2,1)}, bf16[1,2,24,576]{3,2,1,0:T(8,128)(2,1)S(1)}, u32[]{:S(2)}, u32[]{:S(2)}) collective-permute-start(bf16[1,2,24,576]{3,2,1,0:T(8,128)(2,1)} %param.8), channel_id=1, source_target_pairs={{16,0},{24,8},{0,16},{8,24},{17,1},{25,9},{1,17},{9,25},{18,2},{26... | collective-permute-start | bytes 165896 | tf_op jit(solution)/shard_map/ppermute | solution.py:225
  4.5 1.4 %collective-permute-start.2 = (bf16[1,2,24,576]{3,2,1,0:T(8,128)(2,1)}, bf16[1,2,24,576]{3,2,1,0:T(8,128)(2,1)S(1)}, u32[]{:S(2)}, u32[]{:S(2)}) collective-permute-start(bf16[1,2,24,576]{3,2,1,0:T(8,128)(2,1)} %param.8), channel_id=1, source_target_pairs={{8,0},{16,8},{24,16},{0,24},{9,1},{17,9},{25,17},{1,25},{10,2},{18... | collective-permute-start | bytes 165896 | tf_op jit(solution)/shard_map/ppermute | solution.py:225
  6.0 1.2 %dynamic_slice.3 = s32[1]{0:T(128)} dynamic-slice(s32[4]{0:T(128)} %partner_ref.1, s32[]{:T(128)S(6)} %select_n.30), dynamic_slice_sizes={1} | dynamic-slice | bytes 12 | tf_op jit(solution)/shard_map/dynamic_slice | solution.py:222
  7.9 0.0 collective-permute-done
  7.9 0.0 collective-permute-done.1
  7.9 1.1 %collective-permute-done.2 = bf16[1,2,24,576]{3,2,1,0:T(8,128)(2,1)S(1)} collective-permute-done((bf16[1,2,24,576]{3,2,1,0:T(8,128)(2,1)}, bf16[1,2,24,576]{3,2,1,0:T(8,128)(2,1)S(1)}, u32[]{:S(2)}, u32[]{:S(2)}) %collective-permute-start.2) | collective-permute-done | bytes 55328 | tf_op jit(solution)/shard_map/ppermute | solution.py:225
  9.0 0.9 %constant_dynamic-update-slice_fusion.4 = (bf16[8,2,24,576]{3,2,1,0:T(8,128)(2,1)S(1)}, bf16[1,2,24,576]{3,2,1,0:T(8,128)(2,1)S(1)}) fusion(bf16[1,2,24,576]{3,2,1,0:T(8,128)(2,1)S(1)} %collective-permute-done, bf16[1,2,24,576]{3,2,1,0:T(8,128)(2,1)S(1)} %collective-permute-done.1, bf16[1,2,24,576]{3,2,1,0:T(8,128)(2,1)S(1)} %collective-permute-done.2, ...), kind=kLoop, calls=%fused_computation.6 | loop fusion | flops 82943 | bytes 344067
  9.8 1.6 %collective-permute-start.3 = (bf16[1,2,24,576]{3,2,1,0:T(8,128)(2,1)S(1)}, bf16[1,2,24,576]{3,2,1,0:T(8,128)(2,1)S(1)}, u32[]{:S(2)}, u32[]{:S(2)}) collective-permute-start(bf16[1,2,24,576]{3,2,1,0:T(8,128)(2,1)S(1)} %get-tuple-element.6), channel_id=1, source_target_pairs={{0,2},{1,3},{2,0},{3,1},{4,6},{5,7},{6,4},{7,5},{8,10},{9,11},{10,... | collective-permute-start | bytes 165896 | tf_op jit(solution)/shard_map/ppermute | solution.py:231
  11.5 2.6 %collective-permute-start.4 = (bf16[1,2,24,576]{3,2,1,0:T(8,128)(2,1)S(1)}, bf16[1,2,24,576]{3,2,1,0:T(8,128)(2,1)S(1)}, u32[]{:S(2)}, u32[]{:S(2)}) collective-permute-start(bf16[1,2,24,576]{3,2,1,0:T(8,128)(2,1)S(1)} %get-tuple-element.6), channel_id=1, source_target_pairs={{0,4},{1,5},{2,6},{3,7},{4,0},{5,1},{6,2},{7,3},{8,12},{9,13},{10,... | collective-permute-start | bytes 165896 | tf_op jit(solution)/shard_map/ppermute | solution.py:231
  14.1 0.2 collective-permute-start.5
  14.3 2.5 %shard_map.73.kernel_ref = f32[2,3,24,192]{3,2,1,0:T(8,128)} custom-call(s32[4]{0:T(128)} %partner_ref.1, s32[8,8]{1,0:T(8,128)} %index_ref.1, f32[16,24,576]{2,1,0:T(8,128)} %kernels_ref.1), custom_call_target="tpu_custom_call" | custom-call | tf_op jit(solution)/shard_map/pallas_call | solution.py:129
  16.7 0.0 collective-permute-done.3
  16.8 1.1 %collective-permute-done.4 = bf16[1,2,24,576]{3,2,1,0:T(8,128)(2,1)S(1)} collective-permute-done((bf16[1,2,24,576]{3,2,1,0:T(8,128)(2,1)S(1)}, bf16[1,2,24,576]{3,2,1,0:T(8,128)(2,1)S(1)}, u32[]{:S(2)}, u32[]{:S(2)}) %collective-permute-start.4) | collective-permute-done | bytes 55328 | tf_op jit(solution)/shard_map/ppermute | solution.py:231
  17.9 2.2 %collective-permute-done.5 = bf16[1,2,24,576]{3,2,1,0:T(8,128)(2,1)S(1)} collective-permute-done((bf16[1,2,24,576]{3,2,1,0:T(8,128)(2,1)S(1)}, bf16[1,2,24,576]{3,2,1,0:T(8,128)(2,1)S(1)}, u32[]{:S(2)}, u32[]{:S(2)}) %collective-permute-start.5) | collective-permute-done | bytes 55328 | tf_op jit(solution)/shard_map/ppermute | solution.py:231
  20.1 0.1 pad_maximum_fusion
  20.1 0.1 collective-permute-start.6
  20.3 1.4 %collective-permute-done.6 = bf16[4,2,24,576]{3,2,1,0:T(8,128)(2,1)S(1)} collective-permute-done((bf16[4,2,24,576]{3,2,1,0:T(8,128)(2,1)S(1)}, bf16[4,2,24,576]{3,2,1,0:T(8,128)(2,1)S(1)}, u32[]{:S(2)}, u32[]{:S(2)}) %collective-permute-start.6) | collective-permute-done | bytes 221216 | tf_op jit(solution)/shard_map/ppermute | solution.py:233
  21.7 0.0 copy-done.3
  21.8 0.0 copy-done
  21.8 0.0 copy-done.2
  21.8 0.0 copy-start.1
  21.8 0.9 %copy-done.1 = f32[2,3,24,192]{3,2,1,0:T(8,128)S(1)} copy-done((f32[2,3,24,192]{3,2,1,0:T(8,128)S(1)}, f32[2,3,24,192]{3,2,1,0:T(8,128)}, u32[]{:S(2)}) %copy-start.1) | copy-done | bytes 110616
  22.7 4.2 %shard_map.74 = f32[1,2,24,576]{3,2,1,0:T(8,128)} custom-call(f32[1,2,24,576]{3,2,1,0:T(8,128)S(1)} %copy-done.2, bf16[8,2,24,576]{3,2,1,0:T(8,128)(2,1)S(1)} %constant_dynamic-update-slice_fusion.orbital_ref, f32[2,3,24,192]{3,2,1,0:T(8,128)S(1)} %copy-done.1, bf16[2,48,144]{2,1,0:T(8,128)(2,1)S(1)} %copy-done.3, bf16[2,3,2,2,192,192]{5,4,3,2,1,0:T(8,128)(2,1)S(1)} %copy-done), custom_call_target="tpu_custom_call" | custom-call | tf_op jit(solution)/shard_map/pallas_call | solution.py:207
  (4 shorter events, 0.1 us)
Async XLA Ops:
  0.0 21.7 %copy-start.3 = (bf16[2,48,144]{2,1,0:T(8,128)(2,1)S(1)}, bf16[2,48,144]{2,1,0:T(8,128)(2,1)}, u32[]{:S(2)}) copy-start(bf16[2,48,144]{2,1,0:T(8,128)(2,1)} %constant.28.clone.line_ref) | copy-start | bytes 82948
  0.0 21.8 %copy-start = (bf16[2,3,2,2,192,192]{5,4,3,2,1,0:T(8,128)(2,1)S(1)}, bf16[2,3,2,2,192,192]{5,4,3,2,1,0:T(8,128)(2,1)}, u32[]{:S(2)}) copy-start(bf16[2,3,2,2,192,192]{5,4,3,2,1,0:T(8,128)(2,1)} %constant.29.clone.plane_ref) | copy-start | bytes 5308420
  0.0 21.8 %copy-start.2 = (f32[1,2,24,576]{3,2,1,0:T(8,128)S(1)}, f32[1,2,24,576]{3,2,1,0:T(8,128)}, u32[]{:S(2)}) copy-start(f32[1,2,24,576]{3,2,1,0:T(8,128)} %target_ref.1) | copy-start | bytes 331780
  0.0 7.9 %collective-permute-start = (bf16[1,2,24,576]{3,2,1,0:T(8,128)(2,1)}, bf16[1,2,24,576]{3,2,1,0:T(8,128)(2,1)S(1)}, u32[]{:S(2)}, u32[]{:S(2)}) collective-permute-start(bf16[1,2,24,576]{3,2,1,0:T(8,128)(2,1)} %param.8), channel_id=1, source_target_pairs={{24,0},{0,8},{8,16},{16,24},{25,1},{1,9},{9,17},{17,25},{26,2},{2,... | collective-permute-start | bytes 165896 | tf_op jit(solution)/shard_map/ppermute | solution.py:225
  3.0 4.9 %collective-permute-start.1 = (bf16[1,2,24,576]{3,2,1,0:T(8,128)(2,1)}, bf16[1,2,24,576]{3,2,1,0:T(8,128)(2,1)S(1)}, u32[]{:S(2)}, u32[]{:S(2)}) collective-permute-start(bf16[1,2,24,576]{3,2,1,0:T(8,128)(2,1)} %param.8), channel_id=1, source_target_pairs={{16,0},{24,8},{0,16},{8,24},{17,1},{25,9},{1,17},{9,25},{18,2},{26... | collective-permute-start | bytes 165896 | tf_op jit(solution)/shard_map/ppermute | solution.py:225
  4.5 4.4 %collective-permute-start.2 = (bf16[1,2,24,576]{3,2,1,0:T(8,128)(2,1)}, bf16[1,2,24,576]{3,2,1,0:T(8,128)(2,1)S(1)}, u32[]{:S(2)}, u32[]{:S(2)}) collective-permute-start(bf16[1,2,24,576]{3,2,1,0:T(8,128)(2,1)} %param.8), channel_id=1, source_target_pairs={{8,0},{16,8},{24,16},{0,24},{9,1},{17,9},{25,17},{1,25},{10,2},{18... | collective-permute-start | bytes 165896 | tf_op jit(solution)/shard_map/ppermute | solution.py:225
  9.8 6.9 %collective-permute-start.3 = (bf16[1,2,24,576]{3,2,1,0:T(8,128)(2,1)S(1)}, bf16[1,2,24,576]{3,2,1,0:T(8,128)(2,1)S(1)}, u32[]{:S(2)}, u32[]{:S(2)}) collective-permute-start(bf16[1,2,24,576]{3,2,1,0:T(8,128)(2,1)S(1)} %get-tuple-element.6), channel_id=1, source_target_pairs={{0,2},{1,3},{2,0},{3,1},{4,6},{5,7},{6,4},{7,5},{8,10},{9,11},{10,... | collective-permute-start | bytes 165896 | tf_op jit(solution)/shard_map/ppermute | solution.py:231
  11.5 6.4 %collective-permute-start.4 = (bf16[1,2,24,576]{3,2,1,0:T(8,128)(2,1)S(1)}, bf16[1,2,24,576]{3,2,1,0:T(8,128)(2,1)S(1)}, u32[]{:S(2)}, u32[]{:S(2)}) collective-permute-start(bf16[1,2,24,576]{3,2,1,0:T(8,128)(2,1)S(1)} %get-tuple-element.6), channel_id=1, source_target_pairs={{0,4},{1,5},{2,6},{3,7},{4,0},{5,1},{6,2},{7,3},{8,12},{9,13},{10,... | collective-permute-start | bytes 165896 | tf_op jit(solution)/shard_map/ppermute | solution.py:231
  14.1 6.0 %collective-permute-start.5 = (bf16[1,2,24,576]{3,2,1,0:T(8,128)(2,1)S(1)}, bf16[1,2,24,576]{3,2,1,0:T(8,128)(2,1)S(1)}, u32[]{:S(2)}, u32[]{:S(2)}) collective-permute-start(bf16[1,2,24,576]{3,2,1,0:T(8,128)(2,1)S(1)} %get-tuple-element.6), channel_id=1, source_target_pairs={{0,6},{1,7},{2,4},{3,5},{4,2},{5,3},{6,0},{7,1},{8,14},{9,15},{10,... | collective-permute-start | bytes 165896 | tf_op jit(solution)/shard_map/ppermute | solution.py:231
  20.1 1.6 %collective-permute-start.6 = (bf16[4,2,24,576]{3,2,1,0:T(8,128)(2,1)S(1)}, bf16[4,2,24,576]{3,2,1,0:T(8,128)(2,1)S(1)}, u32[]{:S(2)}, u32[]{:S(2)}) collective-permute-start(bf16[4,2,24,576]{3,2,1,0:T(8,128)(2,1)S(1)} %pad_maximum_fusion), channel_id=1, source_target_pairs={{0,1},{1,0},{2,3},{3,2},{4,5},{5,4},{6,7},{7,6},{8,9},{9,8},{10,11... | collective-permute-start | bytes 663560 | tf_op jit(solution)/shard_map/ppermute | solution.py:233
  21.8 0.9 %copy-start.1 = (f32[2,3,24,192]{3,2,1,0:T(8,128)S(1)}, f32[2,3,24,192]{3,2,1,0:T(8,128)}, u32[]{:S(2)}) copy-start(f32[2,3,24,192]{3,2,1,0:T(8,128)} %shard_map.73.kernel_ref) | copy-start | bytes 331780

commit v2 on v0

v2 whole, which is shorter than its diff:
```python
import functools
import math

import jax
import jax.numpy as jnp
import ml_dtypes
import numpy as np
from jax import lax
from jax.experimental import pallas as pl
from jax.experimental.pallas import tpu as pltpu
from jax.sharding import PartitionSpec as P

KPT_DEV = 2
RADIX = 6
CHUNK = 8
LANES = 128
PITCH_GAP = 0
CARRIED = 3
SCOPED_BYTES = 16 * 1024 * 1024
BF16 = jnp.bfloat16
F32 = jnp.float32


def split_table(table):
    high = table.astype(ml_dtypes.bfloat16)
    low = (table - high.astype(np.float64)).astype(ml_dtypes.bfloat16)
    return high, low


def padded(width):
    return -(-width // LANES) * LANES


def plane_tables(grid_size):
    inner = grid_size // RADIX
    width = inner * grid_size
    room = padded(width) - width
    b, c = np.divmod(np.arange(width), grid_size)
    found = []
    for sign in (1.0, -1.0):
        for residue in range(RADIX):
            turns = b[:, None] * (RADIX * b[None, :] + residue) + c[:, None] * c[None, :]
            angles = (turns % grid_size) * (2.0 * np.pi / grid_size)
            if sign < 0:
                angles = angles.T
            cosine = np.pad(np.cos(angles), [(0, room)] * 2)
            sine = np.pad(sign * np.sin(angles), [(0, room)] * 2)
            found.append(split_table(np.block([[cosine, -sine], [sine, cosine]])))
    found = np.array(found)
    return found.reshape((2, RADIX) + found.shape[1:])


def halves(values):
    high = values.astype(BF16)
    return high, (values - high.astype(F32)).astype(BF16)


def plane_transform(real, imag, tables):
    high, low = halves(jnp.concatenate([jnp.concatenate(real, axis=0), jnp.concatenate(imag, axis=0)], axis=1))
    left = jnp.concatenate([high, low, high], axis=1)
    right = jnp.concatenate([tables[0], tables[0], tables[1]], axis=0)
    found = jnp.dot(left, right, preferred_element_type=F32)
    half = found.shape[1] // 2
    return found[:, :half], found[:, half:]


def turn(value, angle):
    real, imag = value
    eighths = angle * 8
    if eighths == int(eighths):
        eighth = int(eighths) % 8
        if eighth % 2:
            half = math.sqrt(0.5)
            real, imag = (real + imag) * half, (imag - real) * half
        for _ in range(eighth // 2):
            real, imag = imag, -real
        return real, imag
    cosine, sine = math.cos(2 * math.pi * angle), math.sin(2 * math.pi * angle)
    return real * cosine + imag * sine, imag * cosine - real * sine


def plus(left, right):
    return left[0] + right[0], left[1] + right[1]


def minus(left, right):
    return left[0] - right[0], left[1] - right[1]


def three_points(first, second, third, sign):
    total = plus(second, third)
    apart = minus(second, third)
    factor = sign * math.sqrt(3.0) / 2.0
    turned = (apart[1] * factor, apart[0] * -factor)
    middle = (first[0] - 0.5 * total[0], first[1] - 0.5 * total[1])
    return [plus(first, total), plus(middle, turned), minus(middle, turned)]


def line_transform(values, sign):
    size = len(values)
    if size == 1:
        return values
    if size == 3:
        return three_points(*values, sign)
    odd = size
    while odd % 2 == 0:
        odd //= 2
    if odd == 1:
        even = line_transform(values[0::2], sign)
        other = line_transform(values[1::2], sign)
        other = [turn(value, sign * k / size) for k, value in enumerate(other)]
        return [plus(*both) for both in zip(even, other)] + [minus(*both) for both in zip(even, other)]
    if odd == size:
        found = []
        for k in range(size):
            total = values[0]
            for n in range(1, size):
                total = plus(total, turn(values[n], sign * (k * n % size) / size))
            found.append(total)
        return found
    twos = size // odd
    rows = []
    for i in range(odd):
        rows.append(line_transform([values[(twos * i + odd * j) % size] for j in range(twos)], sign))
    columns = [line_transform([row[j] for row in rows], sign) for j in range(twos)]
    return [columns[k % twos][k % odd] for k in range(size)]


def prepare_body(steps, partner_ref, index_ref, kernels_ref, *refs):
    carried, (out_ref, shift_ref), refs = refs[:CARRIED], refs[CARRIED : CARRIED + 2], refs[CARRIED + 2 :]
    copied, (partner, index, held, sems) = refs[:CARRIED], refs[CARRIED:]
    copies = []
    moves = [(partner_ref, partner), (index_ref, index), (kernels_ref, held), *zip(carried, copied)]
    for number, (source, target) in enumerate(moves):
        copy = pltpu.make_async_copy(source, target, sems.at[number])
        copy.start()
        copies.append(copy)
    group = lax.axis_index("ka")
    position = lax.axis_index("band")
    per_kpoint = lax.axis_size("band") // KPT_DEV
    kpoint = group * KPT_DEV + position // per_kpoint
    grid_size = kernels_ref.shape[1]
    inner = grid_size // RADIX
    width = inner * grid_size
    slots = lax.broadcasted_iota(jnp.int32, (CHUNK, LANES), 0)
    chosen = []
    for start in range(0, len(steps), CHUNK):
        local_of = jnp.zeros((CHUNK, LANES), jnp.int32)
        for slot, step in enumerate(steps[start : start + CHUNK]):
            local = (position ^ (2 * step)) // per_kpoint
            local_of = jnp.where(slots == slot, local, local_of)
        chosen.append([local_of == local for local in range(KPT_DEV)])
    for copy in copies[:3]:
        copy.wait()
    groups = lax.axis_size("ka")
    shift_ref[0] = lax.rem(partner[group] + groups - group, groups)
    numbers = [index[kpoint, partner[group] * KPT_DEV + local] for local in range(KPT_DEV)]
    scale = 1.0 / grid_size**3
    for residue in range(RADIX):
        arranged = []
        for number in numbers:
            blocks = []
            for q in range(inner):
                at = (RADIX * q + residue) * grid_size
                blocks.append(held[number, :, at : at + grid_size])
            blocks.append(jnp.zeros((grid_size, padded(width) - width), F32))
            arranged.append(jnp.concatenate(blocks, axis=1) * scale)
        for lane in range(padded(width) // LANES):
            at = slice(lane * LANES, (lane + 1) * LANES)
            for p in range(grid_size):
                rows = [jnp.broadcast_to(values[p : p + 1, at], (CHUNK, LANES)) for values in arranged]
                for number, masks in enumerate(chosen):
                    found = rows[0]
                    for local in range(1, KPT_DEV):
                        found = jnp.where(masks[local], rows[local], found)
                    out_ref[number, residue, lane, p] = found
    for copy in copies[3:]:
        copy.wait()


def in_hbm(array):
    return pltpu.with_memory_space_constraint(array, pltpu.HBM)


def prepare(steps, partner, kernel_index, kernels, *carried):
    grid_size, plane = kernels.shape[1:]
    chunks = -(-len(steps) // CHUNK)
    lanes = padded(plane // RADIX) // LANES
    given = [partner, kernel_index, kernels, *carried]
    return pl.pallas_call(
        functools.partial(prepare_body, steps),
        out_shape=[
            pltpu.VMEM((chunks, RADIX, lanes, grid_size, CHUNK, LANES), F32),
            pltpu.SMEM((1,), jnp.int32),
            *[pltpu.VMEM(array.shape, array.dtype) for array in carried],
        ],
        in_specs=[pl.BlockSpec(memory_space=pltpu.HBM)] * len(given),
        out_specs=[
            pl.BlockSpec(memory_space=pltpu.VMEM),
            pl.BlockSpec(memory_space=pltpu.SMEM),
            *[pl.BlockSpec(memory_space=pltpu.VMEM)] * len(carried),
        ],
        scratch_shapes=[
            pltpu.SMEM(partner.shape, jnp.int32),
            pltpu.SMEM(kernel_index.shape, jnp.int32),
            pltpu.VMEM(kernels.shape, F32),
            pltpu.SemaphoreType.DMA((len(given),)),
        ],
        compiler_params=pltpu.CompilerParams(vmem_limit_bytes=SCOPED_BYTES),
    )(*[in_hbm(array) for array in given])


def choose_body(shift_ref, *refs):
    for by, ref in enumerate(refs[:-1]):

        @pl.when(shift_ref[0] == by)
        def _(ref=ref):
            refs[-1][...] = ref[...]


def choose(shift, arrays):
    whole = pl.BlockSpec(memory_space=pltpu.VMEM)
    return pl.pallas_call(
        choose_body,
        out_shape=pltpu.VMEM(arrays[0].shape, arrays[0].dtype),
        in_specs=[pl.BlockSpec(memory_space=pltpu.SMEM), *[whole] * len(arrays)],
        out_specs=whole,
        compiler_params=pltpu.CompilerParams(vmem_limit_bytes=SCOPED_BYTES),
    )(shift, *arrays)


def lane_blocks(values, width):
    rows, plane = values.shape
    found = []
    for block in range(RADIX):
        at, room = block * width, padded(width)
        if at + room <= plane:
            found.append(values[:, at : at + room])
        else:
            blank = jnp.zeros((rows, at + room - plane), values.dtype)
            found.append(jnp.concatenate([values[:, at:], blank], axis=1))
    return found


def forward(members, first, target_ref, plane_ref, field_ref, held_ref):
    grid_size, plane = target_ref.shape[2:]
    lanes = field_ref.shape[3]
    pitch = field_ref.shape[4] // CHUNK
    target = [lane_blocks(target_ref[0, part], plane // RADIX) for part in range(2)]
    taken = 0
    while taken < len(members):
        chunk, slot = divmod(first + taken, CHUNK)
        batch = members[taken : taken + CHUNK - slot]
        taken += len(batch)
        fields = [([], []) for _ in range(RADIX)]
        for place, (ref, row) in enumerate(batch):
            orbital = [
                [values.astype(F32) for values in lane_blocks(ref[row, part], plane // RADIX)] for part in range(2)
            ]
            blocks = []
            for block in range(RADIX):
                real, imag = orbital[0][block], orbital[1][block]
                target_real, target_imag = target[0][block], target[1][block]
                held_ref[chunk, slot + place, 0, block] = real
                held_ref[chunk, slot + place, 1, block] = imag
                blocks.append(
                    (
                        real * target_real + imag * target_imag,
                        real * target_imag - imag * target_real,
                    )
                )
            for residue, value in enumerate(line_transform(blocks, 1.0)):
                for part in range(2):
                    fields[residue][part].append(value[part])
        for residue in range(RADIX):
            parts = plane_transform(*fields[residue], [plane_ref[0, residue, j] for j in range(2)])
            for part in range(2):
                for place in range(len(batch)):
                    found = parts[part][place * grid_size : (place + 1) * grid_size]
                    for lane in range(lanes):
                        at = (slot + place) * pitch
                        field_ref[chunk, residue, part, lane, at : at + grid_size] = found[
                            :, lane * LANES : (lane + 1) * LANES
                        ]


def early_body(count, *refs):
    orbital_refs, (target_ref, plane_ref, field_ref, held_ref) = refs[:count], refs[count:]
    members = [(ref, row) for ref in orbital_refs for row in range(ref.shape[0])]
    forward(members, 0, target_ref, plane_ref, field_ref, held_ref)


def late_body(count, first, *refs):
    orbital_refs, refs = refs[:count], refs[count:]
    target_ref, plane_ref, kernel_ref, _, _, out_ref, field_ref, held_ref = refs
    grid_size, plane = target_ref.shape[2:]
    width = plane // RADIX
    chunks, _, _, lanes, rows = field_ref.shape[:5]
    pitch = rows // CHUNK
    members = [(ref, row) for ref in orbital_refs for row in range(ref.shape[0])]
    forward(members, first, target_ref, plane_ref, field_ref, held_ref)
    totals = [[0.0, 0.0] for _ in range(RADIX)]
    for chunk in range(chunks):
        potentials = []
        for residue in range(RADIX):
            for lane in range(lanes):
                values = [
                    tuple(field_ref[chunk, residue, part, lane, pl.ds(a, CHUNK, stride=pitch)] for part in range(2))
                    for a in range(grid_size)
                ]
                scaled = []
                for p, (real, imag) in enumerate(line_transform(values, 1.0)):
                    kernel = kernel_ref[chunk, residue, lane, p]
                    scaled.append((real * kernel, imag * kernel))
                for a, value in enumerate(line_transform(scaled, -1.0)):
                    for part in range(2):
                        field_ref[chunk, residue, part, lane, pl.ds(a, CHUNK, stride=pitch)] = value[part]
        for residue in range(RADIX):
            parts = []
            for part in range(2):
                parts.append([])
                for place in range(CHUNK):
                    at = slice(place * pitch, place * pitch + grid_size)
                    found = [field_ref[chunk, residue, part, lane, at] for lane in range(lanes)]
                    parts[part].append(jnp.concatenate(found, axis=1))
            potentials.append(plane_transform(*parts, [plane_ref[1, residue, j] for j in range(2)]))
        for place in range(CHUNK):
            at = slice(place * grid_size, (place + 1) * grid_size)
            blocks = line_transform([(real[at], imag[at]) for real, imag in potentials], -1.0)
            for block, (pot_real, pot_imag) in enumerate(blocks):
                real, imag = (held_ref[chunk, place, part, block] for part in range(2))
                totals[block][0] -= real * pot_real - imag * pot_imag
                totals[block][1] -= real * pot_imag + imag * pot_real
    for part in range(2):
        out_ref[0, part] = jnp.concatenate([totals[block][part][:, :width] for block in range(RADIX)], axis=1)


def exchange(early, late, target, kernels, tables):
    grid_size, plane = target.shape[2:]
    lanes = padded(plane // RADIX) // LANES
    chunks = kernels.shape[0]
    known = sum(array.shape[0] for array in early)
    carried = [
        pltpu.VMEM((chunks, RADIX, 2, lanes, CHUNK * (grid_size + PITCH_GAP), LANES), F32),
        pltpu.VMEM((chunks, CHUNK, 2, RADIX, grid_size, lanes * LANES), F32),
    ]
    whole = pl.BlockSpec(memory_space=pltpu.VMEM)
    params = pltpu.CompilerParams(vmem_limit_bytes=SCOPED_BYTES)
    given = [*early, target, tables]
    field, held = pl.pallas_call(
        functools.partial(early_body, len(early)),
        out_shape=carried,
        in_specs=[whole] * len(given),
        out_specs=[whole] * 2,
        compiler_params=params,
    )(*given)
    given = [*late, target, tables, kernels, field, held]
    return pl.pallas_call(
        functools.partial(late_body, len(late), known),
        out_shape=[jax.ShapeDtypeStruct(target.shape, F32), *carried],
        in_specs=[whole] * len(given),
        out_specs=[whole] * 3,
        input_output_aliases={len(given) - 2: 1, len(given) - 1: 2},
        compiler_params=params,
    )(*given)[0]


def shards(targets, occupied, kernels, partner, kernel_index):
    groups = lax.axis_size("ka")
    band_count = lax.axis_size("band")
    chips = band_count // 2

    steps = [0, *range(2, chips), 1] * 2
    tables = jnp.asarray(plane_tables(targets.shape[2]))
    kernel_blocks, shift, own, target, tables = prepare(
        steps, partner, kernel_index, kernels, occupied, targets, tables
    )
    came = [
        lax.ppermute(occupied, "ka", [((i + by) % groups, i) for i in range(groups)]) for by in range(1, groups)
    ]
    visitor = choose(shift, [own, *came])

    def along(array, by):
        return lax.ppermute(array, "band", [(i, i ^ by) for i in range(band_count)])

    mine = jnp.concatenate([visitor, *[along(visitor, 2 * step) for step in steps[1:chips]]], axis=0)
    others = along(mine, 1)
    return exchange([mine], [others], target, kernel_blocks, tables)


def solution(mesh):
    return jax.shard_map(
        shards,
        mesh=mesh,
        in_specs=(
            P(("ka", "band"), None, None, None),
            P(("ka", "band"), None, None, None),
            P(),
            P(),
            P(),
        ),
        out_specs=P(("ka", "band"), None, None, None),
        check_vma=False,
    )
```

time: 130 us -> 24 us (0.18)
  matrix products: 49.9 us -> 0 us
  local copies, waits for them, and re-layouts: 33.6 us -> 0 us
  loops' own time: 13.9 us -> 0 us
  blocking collectives: 10.4 us -> 0 us
  between operations: 6.9 us -> 0.04 us
  Pallas kernels: 0 us -> 6.12 us
  waiting for transfers between devices: 3.56 us -> 8.3 us
  starting transfers between devices: 10.8 us -> 9.3 us
    dot_general x192 -> x0, matrix products: 49.9 us -> none  [rotate_apply(): lax.dot_general(source_field, matrix, (((1,), (1,)), ((), ())), precision...]
    another operation x1 -> x0, loops' own time: 13.9 us -> none  [shards(): lax.fori_loop(1, halfway, both_sides, (visitor, visitor, totals))]
    sub x96 -> x0, local copies, waits for them, and re-layouts: 13.8 us -> none  [transform(): rotate_apply(real_part, cosine_table)]
    add x96 -> x0, local copies, waits for them, and re-layouts: 13.8 us -> none  [transform(): rotate_apply(imag_part, cosine_table)]
    all_gather x1 -> x0, blocking collectives: 10.4 us -> none  [shards(): everyone = lax.all_gather(occupied, 'ka', axis=0, tiled=True)]
    pallas_call x0 -> x4, Pallas kernels: none -> 6.12 us  [the longest x1 3.02 us: exchange(): pl.pallas_call(functools.partial(late_body, len(late), known), out_shape=...]
    ppermute x7, waiting for transfers between devices: 3.56 us -> 8.3 us  [the longest x4 6.38 us: along(): return lax.ppermute(array, 'band', [(i, i ^ by) for i in range(band_count)])]
    dynamic_slice x5 -> x0, local copies, waits for them, and re-layouts: 3.15 us -> none  [the longest x4 2.57 us: contribute(): table_row = kernel_index[kpoint, source_k]]
  transfers between devices with their start and end apart: 7 -> 7, of which waited for: 1 -> 5; matrix products, arithmetic and copies ran while one was open for 2% -> 0% of each run, Pallas kernels for 0% -> 13%
where the time goes in v2:
time: 24 us; the launch traced here: 23.8 us
  starting transfers between devices  9.3 us (39%)
  waiting for transfers between devices  8.3 us (35%)
  Pallas kernels  6.12 us (26%)
    ppermute x4, waiting for transfers between devices, along(): return lax.ppermute(array, 'band', [(i, i ^ by) for i in range(band_count)])  6.38 us
    ppermute x3, starting transfers between devices, shards(): lax.ppermute(occupied, 'ka', [((i + by) % groups, i) for i in range(group...  4.99 us
    ppermute x4, starting transfers between devices, along(): return lax.ppermute(array, 'band', [(i, i ^ by) for i in range(band_count)])  4.3 us
    pallas_call x1, Pallas kernels, exchange(): pl.pallas_call(functools.partial(late_body, len(late), known), out_shape=...  3.02 us
    pallas_call x1, Pallas kernels, prepare(): pl.pallas_call(functools.partial(prepare_body, steps), out_shape=[pltpu.V...  2.3 us
    ppermute x3, waiting for transfers between devices, shards(): lax.ppermute(occupied, 'ka', [((i + by) % groups, i) for i in range(group...  1.91 us
    pallas_call x1, Pallas kernels, exchange(): pl.pallas_call(functools.partial(early_body, len(early)), out_shape=carri...  0.78 us
  transfers between devices with their start and end apart: 7, of which 5 were waited for; matrix products, arithmetic and copies ran while one was open for 0% of the time, Pallas kernels for 13%

profile of v2, /device:TPU:0, one launch (start us, length us, event | category | flops | bytes accessed | tf_op | source)
XLA Modules:
  0.0 23.8 jit_solution(1654842025450158176)
XLA Ops:
  0.0 3.9 %collective-permute-start = (bf16[1,2,24,576]{3,2,1,0:T(8,128)(2,1)}, bf16[1,2,24,576]{3,2,1,0:T(8,128)(2,1)S(1)}, u32[]{:S(2)}, u32[]{:S(2)}) collective-permute-start(bf16[1,2,24,576]{3,2,1,0:T(8,128)(2,1)} %refs_0_.1), channel_id=1, source_target_pairs={{8,0},{16,8},{24,16},{0,24},{9,1},{17,9},{25,17},{1,25},{10,2},{18... | collective-permute-start | bytes 165896 | tf_op jit(solution)/shard_map/ppermute | solution.py:379
  3.9 0.0 collective-permute-start.2
  3.9 1.1 %collective-permute-start.1 = (bf16[1,2,24,576]{3,2,1,0:T(8,128)(2,1)}, bf16[1,2,24,576]{3,2,1,0:T(8,128)(2,1)S(1)}, u32[]{:S(2)}, u32[]{:S(2)}) collective-permute-start(bf16[1,2,24,576]{3,2,1,0:T(8,128)(2,1)} %refs_0_.1), channel_id=1, source_target_pairs={{16,0},{24,8},{0,16},{8,24},{17,1},{25,9},{1,17},{9,25},{18,2},{26... | collective-permute-start | bytes 165896 | tf_op jit(solution)/shard_map/ppermute | solution.py:379
  5.0 2.3 %shard_map.64 = (f32[1,6,1,24,8,128]{5,4,3,2,1,0:T(8,128)S(1)}, s32[1]{0:T(128)S(4)}, bf16[1,2,24,576]{3,2,1,0:T(8,128)(2,1)S(1)}, f32[1,2,24,576]{3,2,1,0:T(8,128)S(1)}, bf16[2,6,2,256,256]{4,3,2,1,0:T(8,128)(2,1)S(1)}) custom-call(s32[4]{0:T(128)} %partner_ref.1, s32[8,8]{1,0:T(8,128)} %index_ref.1, f32[16,24,576]{2,1,0:T(8,128)} %kernels_ref.1, ...), custom_call_target="tpu_custom_call" | custom-call | tf_op jit(solution)/shard_map/pallas_call | solution.py:190
  7.3 0.0 collective-permute-done.refs_1_
  7.3 1.9 %collective-permute-done.2.refs_3_ = bf16[1,2,24,576]{3,2,1,0:T(8,128)(2,1)S(1)} collective-permute-done((bf16[1,2,24,576]{3,2,1,0:T(8,128)(2,1)}, bf16[1,2,24,576]{3,2,1,0:T(8,128)(2,1)S(1)}, u32[]{:S(2)}, u32[]{:S(2)}) %collective-permute-start.2) | collective-permute-done | bytes 55328 | tf_op jit(solution)/shard_map/ppermute | solution.py:379
  9.2 0.0 collective-permute-done.1.refs_2_
  9.3 1.6 %collective-permute-start.5 = (bf16[1,2,24,576]{3,2,1,0:T(8,128)(2,1)S(1)}, bf16[1,2,24,576]{3,2,1,0:T(8,128)(2,1)S(1)}, u32[]{:S(2)}, u32[]{:S(2)}) collective-permute-start(bf16[1,2,24,576]{3,2,1,0:T(8,128)(2,1)S(1)} %shard_map.65), channel_id=1, source_target_pairs={{0,2},{1,3},{2,0},{3,1},{4,6},{5,7},{6,4},{7,5},{8,10},{9,11},{10,... | collective-permute-start | bytes 165896 | tf_op jit(solution)/shard_map/ppermute | solution.py:384
  10.9 2.5 %collective-permute-start.4 = (bf16[1,2,24,576]{3,2,1,0:T(8,128)(2,1)S(1)}, bf16[1,2,24,576]{3,2,1,0:T(8,128)(2,1)S(1)}, u32[]{:S(2)}, u32[]{:S(2)}) collective-permute-start(bf16[1,2,24,576]{3,2,1,0:T(8,128)(2,1)S(1)} %shard_map.65), channel_id=1, source_target_pairs={{0,6},{1,7},{2,4},{3,5},{4,2},{5,3},{6,0},{7,1},{8,14},{9,15},{10,... | collective-permute-start | bytes 165896 | tf_op jit(solution)/shard_map/ppermute | solution.py:384
  13.4 0.1 collective-permute-start.3
  13.5 0.7 %collective-permute-done.5 = bf16[1,2,24,576]{3,2,1,0:T(8,128)(2,1)S(1)} collective-permute-done((bf16[1,2,24,576]{3,2,1,0:T(8,128)(2,1)S(1)}, bf16[1,2,24,576]{3,2,1,0:T(8,128)(2,1)S(1)}, u32[]{:S(2)}, u32[]{:S(2)}) %collective-permute-start.5) | collective-permute-done | bytes 55328 | tf_op jit(solution)/shard_map/ppermute | solution.py:384
  14.2 2.7 %collective-permute-done.4 = bf16[1,2,24,576]{3,2,1,0:T(8,128)(2,1)S(1)} collective-permute-done((bf16[1,2,24,576]{3,2,1,0:T(8,128)(2,1)S(1)}, bf16[1,2,24,576]{3,2,1,0:T(8,128)(2,1)S(1)}, u32[]{:S(2)}, u32[]{:S(2)}) %collective-permute-start.4) | collective-permute-done | bytes 55328 | tf_op jit(solution)/shard_map/ppermute | solution.py:384
  16.9 2.2 %collective-permute-done.3 = bf16[1,2,24,576]{3,2,1,0:T(8,128)(2,1)S(1)} collective-permute-done((bf16[1,2,24,576]{3,2,1,0:T(8,128)(2,1)S(1)}, bf16[1,2,24,576]{3,2,1,0:T(8,128)(2,1)S(1)}, u32[]{:S(2)}, u32[]{:S(2)}) %collective-permute-start.3) | collective-permute-done | bytes 55328 | tf_op jit(solution)/shard_map/ppermute | solution.py:384
  19.2 0.1 pad_maximum_fusion.refs_0_
  19.2 0.1 collective-permute-start.6
  19.3 0.8 %shard_map.66 = (f32[1,6,2,1,192,128]{5,4,3,2,1,0:T(8,128)S(1)}, f32[1,8,2,6,24,128]{5,4,3,2,1,0:T(8,128)S(1)}) custom-call(bf16[4,2,24,576]{3,2,1,0:T(8,128)(2,1)S(1)} %pad_maximum_fusion.refs_0_, f32[1,2,24,576]{3,2,1,0:T(8,128)S(1)} %get-tuple-element.15.refs_1_, bf16[2,6,2,256,256]{4,3,2,1,0:T(8,128)(2,1)S(1)} %get-tuple-element.16.refs_2_), custom_call_target="tpu_custom_call" | custom-call | tf_op jit(solution)/shard_map/pallas_call | solution.py:350
  20.1 0.7 %collective-permute-done.6.refs_0_ = bf16[4,2,24,576]{3,2,1,0:T(8,128)(2,1)S(1)} collective-permute-done((bf16[4,2,24,576]{3,2,1,0:T(8,128)(2,1)S(1)}, bf16[4,2,24,576]{3,2,1,0:T(8,128)(2,1)S(1)}, u32[]{:S(2)}, u32[]{:S(2)}) %collective-permute-start.6) | collective-permute-done | bytes 221216 | tf_op jit(solution)/shard_map/ppermute | solution.py:384
  20.8 3.0 %shard_map.67 = (f32[1,2,24,576]{3,2,1,0:T(8,128)}, f32[1,6,2,1,192,128]{5,4,3,2,1,0:T(8,128)S(1)}, f32[1,8,2,6,24,128]{5,4,3,2,1,0:T(8,128)S(1)}) custom-call(bf16[4,2,24,576]{3,2,1,0:T(8,128)(2,1)S(1)} %collective-permute-done.6.refs_0_, f32[1,2,24,576]{3,2,1,0:T(8,128)S(1)} %get-tuple-element.15.refs_1_, ...), custom_call_target="tpu_custom_call", output_to_operand_aliasing={{1}: (4, {}), {2}: (5, {})} | custom-call | tf_op jit(solution)/shard_map/pallas_call | solution.py:358
  (1 shorter events, 0.0 us)
Async XLA Ops:
  0.0 7.3 %collective-permute-start = (bf16[1,2,24,576]{3,2,1,0:T(8,128)(2,1)}, bf16[1,2,24,576]{3,2,1,0:T(8,128)(2,1)S(1)}, u32[]{:S(2)}, u32[]{:S(2)}) collective-permute-start(bf16[1,2,24,576]{3,2,1,0:T(8,128)(2,1)} %refs_0_.1), channel_id=1, source_target_pairs={{8,0},{16,8},{24,16},{0,24},{9,1},{17,9},{25,17},{1,25},{10,2},{18... | collective-permute-start | bytes 165896 | tf_op jit(solution)/shard_map/ppermute | solution.py:379
  3.9 5.3 %collective-permute-start.2 = (bf16[1,2,24,576]{3,2,1,0:T(8,128)(2,1)}, bf16[1,2,24,576]{3,2,1,0:T(8,128)(2,1)S(1)}, u32[]{:S(2)}, u32[]{:S(2)}) collective-permute-start(bf16[1,2,24,576]{3,2,1,0:T(8,128)(2,1)} %refs_0_.1), channel_id=1, source_target_pairs={{24,0},{0,8},{8,16},{16,24},{25,1},{1,9},{9,17},{17,25},{26,2},{2,... | collective-permute-start | bytes 165896 | tf_op jit(solution)/shard_map/ppermute | solution.py:379
  3.9 5.3 %collective-permute-start.1 = (bf16[1,2,24,576]{3,2,1,0:T(8,128)(2,1)}, bf16[1,2,24,576]{3,2,1,0:T(8,128)(2,1)S(1)}, u32[]{:S(2)}, u32[]{:S(2)}) collective-permute-start(bf16[1,2,24,576]{3,2,1,0:T(8,128)(2,1)} %refs_0_.1), channel_id=1, source_target_pairs={{16,0},{24,8},{0,16},{8,24},{17,1},{25,9},{1,17},{9,25},{18,2},{26... | collective-permute-start | bytes 165896 | tf_op jit(solution)/shard_map/ppermute | solution.py:379
  9.3 4.9 %collective-permute-start.5 = (bf16[1,2,24,576]{3,2,1,0:T(8,128)(2,1)S(1)}, bf16[1,2,24,576]{3,2,1,0:T(8,128)(2,1)S(1)}, u32[]{:S(2)}, u32[]{:S(2)}) collective-permute-start(bf16[1,2,24,576]{3,2,1,0:T(8,128)(2,1)S(1)} %shard_map.65), channel_id=1, source_target_pairs={{0,2},{1,3},{2,0},{3,1},{4,6},{5,7},{6,4},{7,5},{8,10},{9,11},{10,... | collective-permute-start | bytes 165896 | tf_op jit(solution)/shard_map/ppermute | solution.py:384
  10.9 6.0 %collective-permute-start.4 = (bf16[1,2,24,576]{3,2,1,0:T(8,128)(2,1)S(1)}, bf16[1,2,24,576]{3,2,1,0:T(8,128)(2,1)S(1)}, u32[]{:S(2)}, u32[]{:S(2)}) collective-permute-start(bf16[1,2,24,576]{3,2,1,0:T(8,128)(2,1)S(1)} %shard_map.65), channel_id=1, source_target_pairs={{0,6},{1,7},{2,4},{3,5},{4,2},{5,3},{6,0},{7,1},{8,14},{9,15},{10,... | collective-permute-start | bytes 165896 | tf_op jit(solution)/shard_map/ppermute | solution.py:384
  13.4 5.8 %collective-permute-start.3 = (bf16[1,2,24,576]{3,2,1,0:T(8,128)(2,1)S(1)}, bf16[1,2,24,576]{3,2,1,0:T(8,128)(2,1)S(1)}, u32[]{:S(2)}, u32[]{:S(2)}) collective-permute-start(bf16[1,2,24,576]{3,2,1,0:T(8,128)(2,1)S(1)} %shard_map.65), channel_id=1, source_target_pairs={{0,4},{1,5},{2,6},{3,7},{4,0},{5,1},{6,2},{7,3},{8,12},{9,13},{10,... | collective-permute-start | bytes 165896 | tf_op jit(solution)/shard_map/ppermute | solution.py:384
  19.2 1.6 %collective-permute-start.6 = (bf16[4,2,24,576]{3,2,1,0:T(8,128)(2,1)S(1)}, bf16[4,2,24,576]{3,2,1,0:T(8,128)(2,1)S(1)}, u32[]{:S(2)}, u32[]{:S(2)}) collective-permute-start(bf16[4,2,24,576]{3,2,1,0:T(8,128)(2,1)S(1)} %pad_maximum_fusion.refs_0_), channel_id=1, source_target_pairs={{0,1},{1,0},{2,3},{3,2},{4,5},{5,4},{6,7},{7,6},{8,9},{9,8},{10,11... | collective-permute-start | bytes 663560 | tf_op jit(solution)/shard_map/ppermute | solution.py:384

commit v3 on v2

--- a/solution.py
+++ b/solution.py
@@ -12,9 +12,10 @@
 
 KPT_DEV = 2
 RADIX = 6
-CHUNK = 8
+BATCH = 4
 LANES = 128
-PITCH_GAP = 0
+SUBLANES = 8
+FOLD = SUBLANES // BATCH
 CARRIED = 3
 SCOPED_BYTES = 16 * 1024 * 1024
 BF16 = jnp.bfloat16
@@ -56,10 +57,10 @@
 
 
 def plane_transform(real, imag, tables):
-    high, low = halves(jnp.concatenate([jnp.concatenate(real, axis=0), jnp.concatenate(imag, axis=0)], axis=1))
-    left = jnp.concatenate([high, low, high], axis=1)
-    right = jnp.concatenate([tables[0], tables[0], tables[1]], axis=0)
-    found = jnp.dot(left, right, preferred_element_type=F32)
+    high, low = halves(jnp.concatenate([real, imag], axis=1))
+    count = high.shape[0]
+    both = jnp.dot(jnp.concatenate([high, low], axis=0), tables[0], preferred_element_type=F32)
+    found = both[:count] + (both[count:] + jnp.dot(high, tables[1], preferred_element_type=F32))
     half = found.shape[1] // 2
     return found[:, :half], found[:, half:]
 
@@ -142,38 +143,39 @@
     grid_size = kernels_ref.shape[1]
     inner = grid_size // RADIX
     width = inner * grid_size
-    slots = lax.broadcasted_iota(jnp.int32, (CHUNK, LANES), 0)
+    slots = lax.broadcasted_iota(jnp.int32, (SUBLANES, LANES), 0)
     chosen = []
-    for start in range(0, len(steps), CHUNK):
-        local_of = jnp.zeros((CHUNK, LANES), jnp.int32)
-        for slot, step in enumerate(steps[start : start + CHUNK]):
+    for start in range(0, len(steps), BATCH):
+        local_of = jnp.zeros((SUBLANES, LANES), jnp.int32)
+        for slot, step in enumerate(steps[start : start + BATCH] * FOLD):
             local = (position ^ (2 * step)) // per_kpoint
             local_of = jnp.where(slots == slot, local, local_of)
         chosen.append([local_of == local for local in range(KPT_DEV)])
     for copy in copies[:3]:
         copy.wait()
-    groups = lax.axis_size("ka")
-    shift_ref[0] = lax.rem(partner[group] + groups - group, groups)
+    shift_ref[0] = partner[group] ^ group
     numbers = [index[kpoint, partner[group] * KPT_DEV + local] for local in range(KPT_DEV)]
     scale = 1.0 / grid_size**3
+    room = jnp.zeros((grid_size, padded(width) - width), F32)
     for residue in range(RADIX):
+        fold, upper = divmod(residue, FOLD)
         arranged = []
         for number in numbers:
             blocks = []
             for q in range(inner):
                 at = (RADIX * q + residue) * grid_size
                 blocks.append(held[number, :, at : at + grid_size])
-            blocks.append(jnp.zeros((grid_size, padded(width) - width), F32))
-            arranged.append(jnp.concatenate(blocks, axis=1) * scale)
+            arranged.append(jnp.concatenate([*blocks, room], axis=1) * scale)
+        rows = slice(upper * BATCH, (upper + 1) * BATCH)
         for lane in range(padded(width) // LANES):
             at = slice(lane * LANES, (lane + 1) * LANES)
             for p in range(grid_size):
-                rows = [jnp.broadcast_to(values[p : p + 1, at], (CHUNK, LANES)) for values in arranged]
-                for number, masks in enumerate(chosen):
-                    found = rows[0]
+                values = [jnp.broadcast_to(value[p : p + 1, at], (SUBLANES, LANES)) for value in arranged]
+                for batch, masks in enumerate(chosen):
+                    found = values[0]
                     for local in range(1, KPT_DEV):
-                        found = jnp.where(masks[local], rows[local], found)
-                    out_ref[number, residue, lane, p] = found
+                        found = jnp.where(masks[local], values[local], found)
+                    out_ref[batch, fold, lane, p, rows] = found[rows]
     for copy in copies[3:]:
         copy.wait()
 
@@ -184,13 +186,13 @@
 
 def prepare(steps, partner, kernel_index, kernels, *carried):
     grid_size, plane = kernels.shape[1:]
-    chunks = -(-len(steps) // CHUNK)
+    batches = len(steps) // BATCH
     lanes = padded(plane // RADIX) // LANES
     given = [partner, kernel_index, kernels, *carried]
     return pl.pallas_call(
         functools.partial(prepare_body, steps),
         out_shape=[
-            pltpu.VMEM((chunks, RADIX, lanes, grid_size, CHUNK, LANES), F32),
+            pltpu.VMEM((batches, RADIX // FOLD, lanes, grid_size, SUBLANES, LANES), F32),
             pltpu.SMEM((1,), jnp.int32),
             *[pltpu.VMEM(array.shape, array.dtype) for array in carried],
         ],
@@ -242,116 +244,118 @@
     return found
 
 
-def forward(members, first, target_ref, plane_ref, field_ref, held_ref):
+def forward(refs, first, target_ref, plane_ref, kernel_ref, field_ref, held_ref, work_ref):
     grid_size, plane = target_ref.shape[2:]
-    lanes = field_ref.shape[3]
-    pitch = field_ref.shape[4] // CHUNK
-    target = [lane_blocks(target_ref[0, part], plane // RADIX) for part in range(2)]
-    taken = 0
-    while taken < len(members):
-        chunk, slot = divmod(first + taken, CHUNK)
-        batch = members[taken : taken + CHUNK - slot]
-        taken += len(batch)
-        fields = [([], []) for _ in range(RADIX)]
-        for place, (ref, row) in enumerate(batch):
-            orbital = [
-                [values.astype(F32) for values in lane_blocks(ref[row, part], plane // RADIX)] for part in range(2)
-            ]
-            blocks = []
-            for block in range(RADIX):
-                real, imag = orbital[0][block], orbital[1][block]
-                target_real, target_imag = target[0][block], target[1][block]
-                held_ref[chunk, slot + place, 0, block] = real
-                held_ref[chunk, slot + place, 1, block] = imag
-                blocks.append(
-                    (
-                        real * target_real + imag * target_imag,
-                        real * target_imag - imag * target_real,
+    members = [(ref, row) for ref in refs for row in range(ref.shape[0])]
+    lanes = field_ref.shape[4] // LANES
+    count = BATCH * grid_size
+    for start in range(0, len(members), BATCH):
+        batch = (first + start) // BATCH
+        for place, (ref, row) in enumerate(members[start : start + BATCH]):
+            for part in range(2):
+                for block, values in enumerate(lane_blocks(ref[row, part], plane // RADIX)):
+                    held_ref[batch, place, part, block] = values.astype(F32)
+        for tile in range(0, grid_size, SUBLANES):
+            rows = slice(tile, tile + SUBLANES)
+            target = [lane_blocks(target_ref[0, part, rows], plane // RADIX) for part in range(2)]
+            for place in range(BATCH):
+                blocks = []
+                for block in range(RADIX):
+                    real, imag = (held_ref[batch, place, part, block, rows] for part in range(2))
+                    target_real, target_imag = target[0][block], target[1][block]
+                    blocks.append(
+                        (
+                            real * target_real + imag * target_imag,
+                            real * target_imag - imag * target_real,
+                        )
                     )
-                )
-            for residue, value in enumerate(line_transform(blocks, 1.0)):
+                at = place * grid_size + tile
+                for residue, value in enumerate(line_transform(blocks, 1.0)):
+                    for part in range(2):
+                        work_ref[residue, part, at : at + SUBLANES] = value[part]
+        for fold in range(RADIX // FOLD):
+            for upper in range(FOLD):
+                residue = fold * FOLD + upper
+                parts = [work_ref[residue, part, :count] for part in range(2)]
+                parts = plane_transform(*parts, [plane_ref[0, residue, j] for j in range(2)])
                 for part in range(2):
-                    fields[residue][part].append(value[part])
-        for residue in range(RADIX):
-            parts = plane_transform(*fields[residue], [plane_ref[0, residue, j] for j in range(2)])
-            for part in range(2):
-                for place in range(len(batch)):
-                    found = parts[part][place * grid_size : (place + 1) * grid_size]
-                    for lane in range(lanes):
-                        at = (slot + place) * pitch
-                        field_ref[chunk, residue, part, lane, at : at + grid_size] = found[
-                            :, lane * LANES : (lane + 1) * LANES
-                        ]
-
-
-def early_body(count, *refs):
-    orbital_refs, (target_ref, plane_ref, field_ref, held_ref) = refs[:count], refs[count:]
-    members = [(ref, row) for ref in orbital_refs for row in range(ref.shape[0])]
-    forward(members, 0, target_ref, plane_ref, field_ref, held_ref)
-
-
-def late_body(count, first, *refs):
-    orbital_refs, refs = refs[:count], refs[count:]
-    target_ref, plane_ref, kernel_ref, _, _, out_ref, field_ref, held_ref = refs
-    grid_size, plane = target_ref.shape[2:]
-    width = plane // RADIX
-    chunks, _, _, lanes, rows = field_ref.shape[:5]
-    pitch = rows // CHUNK
-    members = [(ref, row) for ref in orbital_refs for row in range(ref.shape[0])]
-    forward(members, first, target_ref, plane_ref, field_ref, held_ref)
-    totals = [[0.0, 0.0] for _ in range(RADIX)]
-    for chunk in range(chunks):
-        potentials = []
-        for residue in range(RADIX):
+                    field_ref[batch, fold, part, upper * count : (upper + 1) * count] = parts[part]
             for lane in range(lanes):
+                at = slice(lane * LANES, (lane + 1) * LANES)
                 values = [
-                    tuple(field_ref[chunk, residue, part, lane, pl.ds(a, CHUNK, stride=pitch)] for part in range(2))
+                    tuple(field_ref[batch, fold, part, pl.ds(a, SUBLANES, stride=grid_size), at] for part in range(2))
                     for a in range(grid_size)
                 ]
                 scaled = []
                 for p, (real, imag) in enumerate(line_transform(values, 1.0)):
-                    kernel = kernel_ref[chunk, residue, lane, p]
+                    kernel = kernel_ref[batch, fold, lane, p]
                     scaled.append((real * kernel, imag * kernel))
                 for a, value in enumerate(line_transform(scaled, -1.0)):
                     for part in range(2):
-                        field_ref[chunk, residue, part, lane, pl.ds(a, CHUNK, stride=pitch)] = value[part]
+                        field_ref[batch, fold, part, pl.ds(a, SUBLANES, stride=grid_size), at] = value[part]
+
+
+def early_body(count, *refs):
+    forward(refs[:count], 0, *refs[count:])
+
+
+def late_body(count, first, *refs):
+    orbital_refs, refs = refs[:count], refs[count:]
+    target_ref, plane_ref, kernel_ref, _, _, out_ref, field_ref, held_ref, work_ref = refs
+    forward(orbital_refs, first, target_ref, plane_ref, kernel_ref, field_ref, held_ref, work_ref)
+    grid_size, plane = target_ref.shape[2:]
+    width = plane // RADIX
+    batches = field_ref.shape[0]
+    count = BATCH * grid_size
+    for start in range(0, batches, 2):
+        pair = range(start, min(start + 2, batches))
         for residue in range(RADIX):
-            parts = []
+            fold, upper = divmod(residue, FOLD)
+            rows = slice(upper * count, (upper + 1) * count)
+            parts = [
+                jnp.concatenate([field_ref[batch, fold, part, rows] for batch in pair], axis=0) for part in range(2)
+            ]
+            parts = plane_transform(*parts, [plane_ref[1, residue, j] for j in range(2)])
             for part in range(2):
-                parts.append([])
-                for place in range(CHUNK):
-                    at = slice(place * pitch, place * pitch + grid_size)
-                    found = [field_ref[chunk, residue, part, lane, at] for lane in range(lanes)]
-                    parts[part].append(jnp.concatenate(found, axis=1))
-            potentials.append(plane_transform(*parts, [plane_ref[1, residue, j] for j in range(2)]))
-        for place in range(CHUNK):
-            at = slice(place * grid_size, (place + 1) * grid_size)
-            blocks = line_transform([(real[at], imag[at]) for real, imag in potentials], -1.0)
-            for block, (pot_real, pot_imag) in enumerate(blocks):
-                real, imag = (held_ref[chunk, place, part, block] for part in range(2))
-                totals[block][0] -= real * pot_real - imag * pot_imag
-                totals[block][1] -= real * pot_imag + imag * pot_real
-    for part in range(2):
-        out_ref[0, part] = jnp.concatenate([totals[block][part][:, :width] for block in range(RADIX)], axis=1)
+                work_ref[residue, part, : len(pair) * count] = parts[part]
+        for tile in range(0, grid_size, SUBLANES):
+            rows = slice(tile, tile + SUBLANES)
+            totals = [[0.0, 0.0] for _ in range(RADIX)]
+            for batch in pair:
+                for place in range(BATCH):
+                    at = (batch - start) * count + place * grid_size + tile
+                    at = slice(at, at + SUBLANES)
+                    blocks = line_transform(
+                        [tuple(work_ref[residue, part, at] for part in range(2)) for residue in range(RADIX)], -1.0
+                    )
+                    for block, (pot_real, pot_imag) in enumerate(blocks):
+                        real, imag = (held_ref[batch, place, part, block, rows] for part in range(2))
+                        totals[block][0] -= real * pot_real - imag * pot_imag
+                        totals[block][1] -= real * pot_imag + imag * pot_real
+            for part in range(2):
+                found = jnp.concatenate([totals[block][part][:, :width] for block in range(RADIX)], axis=1)
+                out_ref[0, part, rows] = found if start == 0 else out_ref[0, part, rows] + found
 
 
 def exchange(early, late, target, kernels, tables):
     grid_size, plane = target.shape[2:]
-    lanes = padded(plane // RADIX) // LANES
-    chunks = kernels.shape[0]
+    room = padded(plane // RADIX)
+    batches = kernels.shape[0]
     known = sum(array.shape[0] for array in early)
     carried = [
-        pltpu.VMEM((chunks, RADIX, 2, lanes, CHUNK * (grid_size + PITCH_GAP), LANES), F32),
-        pltpu.VMEM((chunks, CHUNK, 2, RADIX, grid_size, lanes * LANES), F32),
+        pltpu.VMEM((batches, RADIX // FOLD, 2, SUBLANES * grid_size, room), F32),
+        pltpu.VMEM((batches, BATCH, 2, RADIX, grid_size, room), F32),
     ]
+    work = pltpu.VMEM((RADIX, 2, 2 * BATCH * grid_size, room), F32)
     whole = pl.BlockSpec(memory_space=pltpu.VMEM)
     params = pltpu.CompilerParams(vmem_limit_bytes=SCOPED_BYTES)
-    given = [*early, target, tables]
+    given = [*early, target, tables, kernels]
     field, held = pl.pallas_call(
         functools.partial(early_body, len(early)),
         out_shape=carried,
         in_specs=[whole] * len(given),
         out_specs=[whole] * 2,
+        scratch_shapes=[work],
         compiler_params=params,
     )(*given)
     given = [*late, target, tables, kernels, field, held]
@@ -360,6 +364,7 @@
         out_shape=[jax.ShapeDtypeStruct(target.shape, F32), *carried],
         in_specs=[whole] * len(given),
         out_specs=[whole] * 3,
+        scratch_shapes=[work],
         input_output_aliases={len(given) - 2: 1, len(given) - 1: 2},
         compiler_params=params,
     )(*given)[0]
@@ -370,13 +375,13 @@
     band_count = lax.axis_size("band")
     chips = band_count // 2
 
-    steps = [0, *range(2, chips), 1] * 2
+    steps = list(range(chips)) * 2
     tables = jnp.asarray(plane_tables(targets.shape[2]))
     kernel_blocks, shift, own, target, tables = prepare(
         steps, partner, kernel_index, kernels, occupied, targets, tables
     )
     came = [
-        lax.ppermute(occupied, "ka", [((i + by) % groups, i) for i in range(groups)]) for by in range(1, groups)
+        lax.ppermute(occupied, "ka", [(i ^ by, i) for i in range(groups)]) for by in range(1, groups)
     ]
     visitor = choose(shift, [own, *came])
 

time: 24 us -> 22 us (0.917)
  waiting for transfers between devices: 8.3 us -> 7.07 us
  starting transfers between devices: 9.3 us -> 8.92 us
  Pallas kernels: 6.12 us -> 5.8 us
    ppermute x4, waiting for transfers between devices: 6.38 us -> 4.87 us  [along(): return lax.ppermute(array, 'band', [(i, i ^ by) for i in range(band_count)])]
    ppermute x3, starting transfers between devices: 4.99 us -> 4.46 us  [shards(): lax.ppermute(occupied, 'ka', [(i ^ by, i) for i in range(groups)])]
    pallas_call x1, Pallas kernels: 3.02 us -> 2.54 us  [exchange(): pl.pallas_call(functools.partial(late_body, len(late), known), out_shape=...]
    ppermute x3, waiting for transfers between devices: 1.91 us -> 2.2 us  [shards(): lax.ppermute(occupied, 'ka', [(i ^ by, i) for i in range(groups)])]
  transfers between devices with their start and end apart: 7 -> 7, of which waited for: 5 -> 5; matrix products, arithmetic and copies ran while one was open for 0% -> 0% of each run, Pallas kernels for 13% -> 15%
where the time goes in v3:
time: 22 us; the launch traced here: 21.9 us
  starting transfers between devices  8.92 us (41%)
  waiting for transfers between devices  7.07 us (32%)
  Pallas kernels  5.8 us (26%)
    ppermute x4, waiting for transfers between devices, along(): return lax.ppermute(array, 'band', [(i, i ^ by) for i in range(band_count)])  4.87 us
    ppermute x3, starting transfers between devices, shards(): lax.ppermute(occupied, 'ka', [(i ^ by, i) for i in range(groups)])  4.46 us
    ppermute x4, starting transfers between devices, along(): return lax.ppermute(array, 'band', [(i, i ^ by) for i in range(band_count)])  4.46 us
    pallas_call x1, Pallas kernels, exchange(): pl.pallas_call(functools.partial(late_body, len(late), known), out_shape=...  2.54 us
    pallas_call x1, Pallas kernels, prepare(): pl.pallas_call(functools.partial(prepare_body, steps), out_shape=[pltpu.V...  2.3 us
    ppermute x3, waiting for transfers between devices, shards(): lax.ppermute(occupied, 'ka', [(i ^ by, i) for i in range(groups)])  2.2 us
    pallas_call x1, Pallas kernels, exchange(): pl.pallas_call(functools.partial(early_body, len(early)), out_shape=carri...  0.96 us
  transfers between devices with their start and end apart: 7, of which 5 were waited for; matrix products, arithmetic and copies ran while one was open for 0% of the time, Pallas kernels for 15%

profile of v3, /device:TPU:0, one launch (start us, length us, event | category | flops | bytes accessed | tf_op | source)
XLA Modules:
  0.0 21.9 jit_solution(1725397911409907981)
XLA Ops:
  0.0 2.9 %collective-permute-start = (bf16[1,2,24,576]{3,2,1,0:T(8,128)(2,1)}, bf16[1,2,24,576]{3,2,1,0:T(8,128)(2,1)S(1)}, u32[]{:S(2)}, u32[]{:S(2)}) collective-permute-start(bf16[1,2,24,576]{3,2,1,0:T(8,128)(2,1)} %refs_0_.1), channel_id=1, source_target_pairs={{8,0},{0,8},{24,16},{16,24},{9,1},{1,9},{25,17},{17,25},{10,2},{2,... | collective-permute-start | bytes 165896 | tf_op jit(solution)/shard_map/ppermute | solution.py:384
  2.9 1.5 %collective-permute-start.2 = (bf16[1,2,24,576]{3,2,1,0:T(8,128)(2,1)}, bf16[1,2,24,576]{3,2,1,0:T(8,128)(2,1)S(1)}, u32[]{:S(2)}, u32[]{:S(2)}) collective-permute-start(bf16[1,2,24,576]{3,2,1,0:T(8,128)(2,1)} %refs_0_.1), channel_id=1, source_target_pairs={{24,0},{16,8},{8,16},{0,24},{25,1},{17,9},{9,17},{1,25},{26,2},{18... | collective-permute-start | bytes 165896 | tf_op jit(solution)/shard_map/ppermute | solution.py:384
  4.4 0.0 collective-permute-start.1
  4.5 2.3 %shard_map.64 = (f32[2,3,1,24,8,128]{5,4,3,2,1,0:T(8,128)S(1)}, s32[1]{0:T(128)S(4)}, bf16[1,2,24,576]{3,2,1,0:T(8,128)(2,1)S(1)}, f32[1,2,24,576]{3,2,1,0:T(8,128)S(1)}, bf16[2,6,2,256,256]{4,3,2,1,0:T(8,128)(2,1)S(1)}) custom-call(s32[4]{0:T(128)} %partner_ref.1, s32[8,8]{1,0:T(8,128)} %index_ref.1, f32[16,24,576]{2,1,0:T(8,128)} %kernels_ref.1, ...), custom_call_target="tpu_custom_call" | custom-call | tf_op jit(solution)/shard_map/pallas_call | solution.py:192
  6.8 0.0 collective-permute-done.refs_1_
  6.8 1.5 %collective-permute-done.2.refs_3_ = bf16[1,2,24,576]{3,2,1,0:T(8,128)(2,1)S(1)} collective-permute-done((bf16[1,2,24,576]{3,2,1,0:T(8,128)(2,1)}, bf16[1,2,24,576]{3,2,1,0:T(8,128)(2,1)S(1)}, u32[]{:S(2)}, u32[]{:S(2)}) %collective-permute-start.2) | collective-permute-done | bytes 55328 | tf_op jit(solution)/shard_map/ppermute | solution.py:384
  8.3 0.7 %collective-permute-done.1.refs_2_ = bf16[1,2,24,576]{3,2,1,0:T(8,128)(2,1)S(1)} collective-permute-done((bf16[1,2,24,576]{3,2,1,0:T(8,128)(2,1)}, bf16[1,2,24,576]{3,2,1,0:T(8,128)(2,1)S(1)}, u32[]{:S(2)}, u32[]{:S(2)}) %collective-permute-start.1) | collective-permute-done | bytes 55328 | tf_op jit(solution)/shard_map/ppermute | solution.py:384
  9.0 3.6 %collective-permute-start.5 = (bf16[1,2,24,576]{3,2,1,0:T(8,128)(2,1)S(1)}, bf16[1,2,24,576]{3,2,1,0:T(8,128)(2,1)S(1)}, u32[]{:S(2)}, u32[]{:S(2)}) collective-permute-start(bf16[1,2,24,576]{3,2,1,0:T(8,128)(2,1)S(1)} %shard_map.65), channel_id=1, source_target_pairs={{0,6},{1,7},{2,4},{3,5},{4,2},{5,3},{6,0},{7,1},{8,14},{9,15},{10,... | collective-permute-start | bytes 165896 | tf_op jit(solution)/shard_map/ppermute | solution.py:389
  12.6 0.0 collective-permute-start.4
  12.6 0.8 %collective-permute-start.3 = (bf16[1,2,24,576]{3,2,1,0:T(8,128)(2,1)S(1)}, bf16[1,2,24,576]{3,2,1,0:T(8,128)(2,1)S(1)}, u32[]{:S(2)}, u32[]{:S(2)}) collective-permute-start(bf16[1,2,24,576]{3,2,1,0:T(8,128)(2,1)S(1)} %shard_map.65), channel_id=1, source_target_pairs={{0,2},{1,3},{2,0},{3,1},{4,6},{5,7},{6,4},{7,5},{8,10},{9,11},{10,... | collective-permute-start | bytes 165896 | tf_op jit(solution)/shard_map/ppermute | solution.py:389
  13.4 2.2 %collective-permute-done.5 = bf16[1,2,24,576]{3,2,1,0:T(8,128)(2,1)S(1)} collective-permute-done((bf16[1,2,24,576]{3,2,1,0:T(8,128)(2,1)S(1)}, bf16[1,2,24,576]{3,2,1,0:T(8,128)(2,1)S(1)}, u32[]{:S(2)}, u32[]{:S(2)}) %collective-permute-start.5) | collective-permute-done | bytes 55328 | tf_op jit(solution)/shard_map/ppermute | solution.py:389
  15.6 2.1 %collective-permute-done.4 = bf16[1,2,24,576]{3,2,1,0:T(8,128)(2,1)S(1)} collective-permute-done((bf16[1,2,24,576]{3,2,1,0:T(8,128)(2,1)S(1)}, bf16[1,2,24,576]{3,2,1,0:T(8,128)(2,1)S(1)}, u32[]{:S(2)}, u32[]{:S(2)}) %collective-permute-start.4) | collective-permute-done | bytes 55328 | tf_op jit(solution)/shard_map/ppermute | solution.py:389
  17.7 0.0 collective-permute-done.3
  17.7 0.1 pad_maximum_fusion.refs_0_
  17.8 0.1 collective-permute-start.6
  17.9 1.0 %shard_map.66 = (f32[2,3,2,192,128]{4,3,2,1,0:T(8,128)S(1)}, f32[2,4,2,6,24,128]{5,4,3,2,1,0:T(8,128)S(1)}) custom-call(bf16[4,2,24,576]{3,2,1,0:T(8,128)(2,1)S(1)} %pad_maximum_fusion.refs_0_, f32[1,2,24,576]{3,2,1,0:T(8,128)S(1)} %get-tuple-element.15.refs_1_, bf16[2,6,2,256,256]{4,3,2,1,0:T(8,128)(2,1)S(1)} %get-tuple-element.16.refs_2_, ...), custom_call_target="tpu_custom_call" | custom-call | tf_op jit(solution)/shard_map/pallas_call | solution.py:353
  18.8 0.5 %collective-permute-done.6.refs_0_ = bf16[4,2,24,576]{3,2,1,0:T(8,128)(2,1)S(1)} collective-permute-done((bf16[4,2,24,576]{3,2,1,0:T(8,128)(2,1)S(1)}, bf16[4,2,24,576]{3,2,1,0:T(8,128)(2,1)S(1)}, u32[]{:S(2)}, u32[]{:S(2)}) %collective-permute-start.6) | collective-permute-done | bytes 221216 | tf_op jit(solution)/shard_map/ppermute | solution.py:389
  19.4 2.5 %shard_map.67 = (f32[1,2,24,576]{3,2,1,0:T(8,128)}, f32[2,3,2,192,128]{4,3,2,1,0:T(8,128)S(1)}, f32[2,4,2,6,24,128]{5,4,3,2,1,0:T(8,128)S(1)}) custom-call(bf16[4,2,24,576]{3,2,1,0:T(8,128)(2,1)S(1)} %collective-permute-done.6.refs_0_, f32[1,2,24,576]{3,2,1,0:T(8,128)S(1)} %get-tuple-element.15.refs_1_, ...), custom_call_target="tpu_custom_call", output_to_operand_aliasing={{1}: (4, {}), {2}: (5, {})} | custom-call | tf_op jit(solution)/shard_map/pallas_call | solution.py:362
  (1 shorter events, 0.0 us)
Async XLA Ops:
  0.0 6.8 %collective-permute-start = (bf16[1,2,24,576]{3,2,1,0:T(8,128)(2,1)}, bf16[1,2,24,576]{3,2,1,0:T(8,128)(2,1)S(1)}, u32[]{:S(2)}, u32[]{:S(2)}) collective-permute-start(bf16[1,2,24,576]{3,2,1,0:T(8,128)(2,1)} %refs_0_.1), channel_id=1, source_target_pairs={{8,0},{0,8},{24,16},{16,24},{9,1},{1,9},{25,17},{17,25},{10,2},{2,... | collective-permute-start | bytes 165896 | tf_op jit(solution)/shard_map/ppermute | solution.py:384
  2.9 5.4 %collective-permute-start.2 = (bf16[1,2,24,576]{3,2,1,0:T(8,128)(2,1)}, bf16[1,2,24,576]{3,2,1,0:T(8,128)(2,1)S(1)}, u32[]{:S(2)}, u32[]{:S(2)}) collective-permute-start(bf16[1,2,24,576]{3,2,1,0:T(8,128)(2,1)} %refs_0_.1), channel_id=1, source_target_pairs={{24,0},{16,8},{8,16},{0,24},{25,1},{17,9},{9,17},{1,25},{26,2},{18... | collective-permute-start | bytes 165896 | tf_op jit(solution)/shard_map/ppermute | solution.py:384
  4.4 4.6 %collective-permute-start.1 = (bf16[1,2,24,576]{3,2,1,0:T(8,128)(2,1)}, bf16[1,2,24,576]{3,2,1,0:T(8,128)(2,1)S(1)}, u32[]{:S(2)}, u32[]{:S(2)}) collective-permute-start(bf16[1,2,24,576]{3,2,1,0:T(8,128)(2,1)} %refs_0_.1), channel_id=1, source_target_pairs={{16,0},{24,8},{0,16},{8,24},{17,1},{25,9},{1,17},{9,25},{18,2},{26... | collective-permute-start | bytes 165896 | tf_op jit(solution)/shard_map/ppermute | solution.py:384
  9.0 6.6 %collective-permute-start.5 = (bf16[1,2,24,576]{3,2,1,0:T(8,128)(2,1)S(1)}, bf16[1,2,24,576]{3,2,1,0:T(8,128)(2,1)S(1)}, u32[]{:S(2)}, u32[]{:S(2)}) collective-permute-start(bf16[1,2,24,576]{3,2,1,0:T(8,128)(2,1)S(1)} %shard_map.65), channel_id=1, source_target_pairs={{0,6},{1,7},{2,4},{3,5},{4,2},{5,3},{6,0},{7,1},{8,14},{9,15},{10,... | collective-permute-start | bytes 165896 | tf_op jit(solution)/shard_map/ppermute | solution.py:389
  12.6 5.1 %collective-permute-start.4 = (bf16[1,2,24,576]{3,2,1,0:T(8,128)(2,1)S(1)}, bf16[1,2,24,576]{3,2,1,0:T(8,128)(2,1)S(1)}, u32[]{:S(2)}, u32[]{:S(2)}) collective-permute-start(bf16[1,2,24,576]{3,2,1,0:T(8,128)(2,1)S(1)} %shard_map.65), channel_id=1, source_target_pairs={{0,4},{1,5},{2,6},{3,7},{4,0},{5,1},{6,2},{7,3},{8,12},{9,13},{10,... | collective-permute-start | bytes 165896 | tf_op jit(solution)/shard_map/ppermute | solution.py:389
  12.6 5.1 %collective-permute-start.3 = (bf16[1,2,24,576]{3,2,1,0:T(8,128)(2,1)S(1)}, bf16[1,2,24,576]{3,2,1,0:T(8,128)(2,1)S(1)}, u32[]{:S(2)}, u32[]{:S(2)}) collective-permute-start(bf16[1,2,24,576]{3,2,1,0:T(8,128)(2,1)S(1)} %shard_map.65), channel_id=1, source_target_pairs={{0,2},{1,3},{2,0},{3,1},{4,6},{5,7},{6,4},{7,5},{8,10},{9,11},{10,... | collective-permute-start | bytes 165896 | tf_op jit(solution)/shard_map/ppermute | solution.py:389
  17.8 1.6 %collective-permute-start.6 = (bf16[4,2,24,576]{3,2,1,0:T(8,128)(2,1)S(1)}, bf16[4,2,24,576]{3,2,1,0:T(8,128)(2,1)S(1)}, u32[]{:S(2)}, u32[]{:S(2)}) collective-permute-start(bf16[4,2,24,576]{3,2,1,0:T(8,128)(2,1)S(1)} %pad_maximum_fusion.refs_0_), channel_id=1, source_target_pairs={{0,1},{1,0},{2,3},{3,2},{4,5},{5,4},{6,7},{7,6},{8,9},{9,8},{10,11... | collective-permute-start | bytes 663560 | tf_op jit(solution)/shard_map/ppermute | solution.py:389

commit v4 on v3

--- a/solution.py
+++ b/solution.py
@@ -212,18 +212,18 @@
     )(*[in_hbm(array) for array in given])
 
 
-def choose_body(shift_ref, *refs):
-    for by, ref in enumerate(refs[:-1]):
+def choose_body(shifts, shift_ref, *refs):
+    for by, ref in zip(shifts, refs[:-1]):
 
         @pl.when(shift_ref[0] == by)
         def _(ref=ref):
             refs[-1][...] = ref[...]
 
 
-def choose(shift, arrays):
+def choose(shift, shifts, arrays):
     whole = pl.BlockSpec(memory_space=pltpu.VMEM)
     return pl.pallas_call(
-        choose_body,
+        functools.partial(choose_body, shifts),
         out_shape=pltpu.VMEM(arrays[0].shape, arrays[0].dtype),
         in_specs=[pl.BlockSpec(memory_space=pltpu.SMEM), *[whole] * len(arrays)],
         out_specs=whole,
@@ -244,24 +244,29 @@
     return found
 
 
-def forward(refs, first, target_ref, plane_ref, kernel_ref, field_ref, held_ref, work_ref):
+def exchange_body(count, first, started, *refs):
+    orbital_refs, refs = refs[:count], refs[count:]
+    target_ref, plane_ref, kernel_ref, refs = refs[0], refs[1], refs[2], refs[3:]
+    out_ref, field_ref, held_ref, work_ref = refs[-4:]
     grid_size, plane = target_ref.shape[2:]
-    members = [(ref, row) for ref in refs for row in range(ref.shape[0])]
-    lanes = field_ref.shape[4] // LANES
-    count = BATCH * grid_size
+    width = plane // RADIX
+    lanes = padded(width) // LANES
+    size = BATCH * grid_size
+    members = [(ref, row) for ref in orbital_refs for row in range(ref.shape[0])]
     for start in range(0, len(members), BATCH):
         batch = (first + start) // BATCH
         for place, (ref, row) in enumerate(members[start : start + BATCH]):
             for part in range(2):
-                for block, values in enumerate(lane_blocks(ref[row, part], plane // RADIX)):
-                    held_ref[batch, place, part, block] = values.astype(F32)
+                for block, values in enumerate(lane_blocks(ref[row, part], width)):
+                    held_ref[place, part, block] = values.astype(F32)
+        starts = {}
         for tile in range(0, grid_size, SUBLANES):
             rows = slice(tile, tile + SUBLANES)
-            target = [lane_blocks(target_ref[0, part, rows], plane // RADIX) for part in range(2)]
+            target = [lane_blocks(target_ref[0, part, rows], width) for part in range(2)]
             for place in range(BATCH):
                 blocks = []
                 for block in range(RADIX):
-                    real, imag = (held_ref[batch, place, part, block, rows] for part in range(2))
+                    real, imag = (held_ref[place, part, block, rows] for part in range(2))
                     target_real, target_imag = target[0][block], target[1][block]
                     blocks.append(
                         (
@@ -272,18 +277,20 @@
                 at = place * grid_size + tile
                 for residue, value in enumerate(line_transform(blocks, 1.0)):
                     for part in range(2):
-                        work_ref[residue, part, at : at + SUBLANES] = value[part]
-        for fold in range(RADIX // FOLD):
+                        starts[residue, part, at] = value[part]
+        def over_plane(fold):
             for upper in range(FOLD):
                 residue = fold * FOLD + upper
-                parts = [work_ref[residue, part, :count] for part in range(2)]
+                parts = [jnp.concatenate([starts[residue, part, at] for at in range(0, size, SUBLANES)], axis=0) for part in range(2)]
                 parts = plane_transform(*parts, [plane_ref[0, residue, j] for j in range(2)])
                 for part in range(2):
-                    field_ref[batch, fold, part, upper * count : (upper + 1) * count] = parts[part]
+                    field_ref[fold, part, upper * size : (upper + 1) * size] = parts[part]
+
+        def over_line(fold):
             for lane in range(lanes):
                 at = slice(lane * LANES, (lane + 1) * LANES)
                 values = [
-                    tuple(field_ref[batch, fold, part, pl.ds(a, SUBLANES, stride=grid_size), at] for part in range(2))
+                    tuple(field_ref[fold, part, pl.ds(a, SUBLANES, stride=grid_size), at] for part in range(2))
                     for a in range(grid_size)
                 ]
                 scaled = []
@@ -292,82 +299,63 @@
                     scaled.append((real * kernel, imag * kernel))
                 for a, value in enumerate(line_transform(scaled, -1.0)):
                     for part in range(2):
-                        field_ref[batch, fold, part, pl.ds(a, SUBLANES, stride=grid_size), at] = value[part]
-
-
-def early_body(count, *refs):
-    forward(refs[:count], 0, *refs[count:])
-
-
-def late_body(count, first, *refs):
-    orbital_refs, refs = refs[:count], refs[count:]
-    target_ref, plane_ref, kernel_ref, _, _, out_ref, field_ref, held_ref, work_ref = refs
-    forward(orbital_refs, first, target_ref, plane_ref, kernel_ref, field_ref, held_ref, work_ref)
-    grid_size, plane = target_ref.shape[2:]
-    width = plane // RADIX
-    batches = field_ref.shape[0]
-    count = BATCH * grid_size
-    for start in range(0, batches, 2):
-        pair = range(start, min(start + 2, batches))
-        for residue in range(RADIX):
-            fold, upper = divmod(residue, FOLD)
-            rows = slice(upper * count, (upper + 1) * count)
-            parts = [
-                jnp.concatenate([field_ref[batch, fold, part, rows] for batch in pair], axis=0) for part in range(2)
-            ]
-            parts = plane_transform(*parts, [plane_ref[1, residue, j] for j in range(2)])
-            for part in range(2):
-                work_ref[residue, part, : len(pair) * count] = parts[part]
+                        field_ref[fold, part, pl.ds(a, SUBLANES, stride=grid_size), at] = value[part]
+
+        ends = {}
+
+        def back(fold):
+            for upper in range(FOLD):
+                residue = fold * FOLD + upper
+                parts = [field_ref[fold, part, upper * size : (upper + 1) * size] for part in range(2)]
+                parts = plane_transform(*parts, [plane_ref[1, residue, j] for j in range(2)])
+                ends[residue] = parts
+
+        folds = RADIX // FOLD
+        for turn_number in range(folds + 2):
+            if turn_number < folds:
+                over_plane(turn_number)
+            if 0 <= turn_number - 1 < folds:
+                over_line(turn_number - 1)
+            if 0 <= turn_number - 2 < folds:
+                back(turn_number - 2)
         for tile in range(0, grid_size, SUBLANES):
             rows = slice(tile, tile + SUBLANES)
             totals = [[0.0, 0.0] for _ in range(RADIX)]
-            for batch in pair:
-                for place in range(BATCH):
-                    at = (batch - start) * count + place * grid_size + tile
-                    at = slice(at, at + SUBLANES)
-                    blocks = line_transform(
-                        [tuple(work_ref[residue, part, at] for part in range(2)) for residue in range(RADIX)], -1.0
-                    )
-                    for block, (pot_real, pot_imag) in enumerate(blocks):
-                        real, imag = (held_ref[batch, place, part, block, rows] for part in range(2))
-                        totals[block][0] -= real * pot_real - imag * pot_imag
-                        totals[block][1] -= real * pot_imag + imag * pot_real
+            for place in range(BATCH):
+                at = slice(place * grid_size + tile, place * grid_size + tile + SUBLANES)
+                blocks = line_transform(
+                    [tuple(ends[residue][part][at] for part in range(2)) for residue in range(RADIX)], -1.0
+                )
+                for block, (pot_real, pot_imag) in enumerate(blocks):
+                    real, imag = (held_ref[place, part, block, rows] for part in range(2))
+                    totals[block][0] -= real * pot_real - imag * pot_imag
+                    totals[block][1] -= real * pot_imag + imag * pot_real
             for part in range(2):
                 found = jnp.concatenate([totals[block][part][:, :width] for block in range(RADIX)], axis=1)
-                out_ref[0, part, rows] = found if start == 0 else out_ref[0, part, rows] + found
-
-
-def exchange(early, late, target, kernels, tables):
+                if start:
+                    found = out_ref[0, part, rows] + found
+                elif started:
+                    found = refs[0][0, part, rows] + found
+                out_ref[0, part, rows] = found
+
+
+def exchange(orbitals, first, target, tables, kernels, total=None):
     grid_size, plane = target.shape[2:]
     room = padded(plane // RADIX)
-    batches = kernels.shape[0]
-    known = sum(array.shape[0] for array in early)
-    carried = [
-        pltpu.VMEM((batches, RADIX // FOLD, 2, SUBLANES * grid_size, room), F32),
-        pltpu.VMEM((batches, BATCH, 2, RADIX, grid_size, room), F32),
-    ]
-    work = pltpu.VMEM((RADIX, 2, 2 * BATCH * grid_size, room), F32)
+    given = [*orbitals, target, tables, kernels] + ([] if total is None else [total])
     whole = pl.BlockSpec(memory_space=pltpu.VMEM)
-    params = pltpu.CompilerParams(vmem_limit_bytes=SCOPED_BYTES)
-    given = [*early, target, tables, kernels]
-    field, held = pl.pallas_call(
-        functools.partial(early_body, len(early)),
-        out_shape=carried,
+    return pl.pallas_call(
+        functools.partial(exchange_body, len(orbitals), first, total is not None),
+        out_shape=jax.ShapeDtypeStruct(target.shape, F32) if total is not None else pltpu.VMEM(target.shape, F32),
         in_specs=[whole] * len(given),
-        out_specs=[whole] * 2,
-        scratch_shapes=[work],
-        compiler_params=params,
+        out_specs=whole,
+        scratch_shapes=[
+            pltpu.VMEM((RADIX // FOLD, 2, SUBLANES * grid_size, room), F32),
+            pltpu.VMEM((BATCH, 2, RADIX, grid_size, room), F32),
+            pltpu.VMEM((RADIX, 2, BATCH * grid_size, room), F32),
+        ],
+        compiler_params=pltpu.CompilerParams(vmem_limit_bytes=SCOPED_BYTES),
     )(*given)
-    given = [*late, target, tables, kernels, field, held]
-    return pl.pallas_call(
-        functools.partial(late_body, len(late), known),
-        out_shape=[jax.ShapeDtypeStruct(target.shape, F32), *carried],
-        in_specs=[whole] * len(given),
-        out_specs=[whole] * 3,
-        scratch_shapes=[work],
-        input_output_aliases={len(given) - 2: 1, len(given) - 1: 2},
-        compiler_params=params,
-    )(*given)[0]
 
 
 def shards(targets, occupied, kernels, partner, kernel_index):
@@ -380,17 +368,17 @@
     kernel_blocks, shift, own, target, tables = prepare(
         steps, partner, kernel_index, kernels, occupied, targets, tables
     )
-    came = [
-        lax.ppermute(occupied, "ka", [(i ^ by, i) for i in range(groups)]) for by in range(1, groups)
-    ]
-    visitor = choose(shift, [own, *came])
+    shifts = list(range(groups - 1, 0, -1))
+    came = [lax.ppermute(occupied, "ka", [(i ^ by, i) for i in range(groups)]) for by in shifts]
+    visitor = choose(shift, [0, *shifts], [own, *came])
 
     def along(array, by):
         return lax.ppermute(array, "band", [(i, i ^ by) for i in range(band_count)])
 
     mine = jnp.concatenate([visitor, *[along(visitor, 2 * step) for step in steps[1:chips]]], axis=0)
     others = along(mine, 1)
-    return exchange([mine], [others], target, kernel_blocks, tables)
+    total = exchange([mine], 0, target, tables, kernel_blocks)
+    return exchange([others], chips, target, tables, kernel_blocks, total)
 
 
 def solution(mesh):

time: 22 us -> 21.5 us (0.977)
  waiting for transfers between devices: 7.07 us -> 6.43 us
    ppermute x4, waiting for transfers between devices: 4.87 us -> 4.38 us  [along(): return lax.ppermute(array, 'band', [(i, i ^ by) for i in range(band_count)])]
  transfers between devices with their start and end apart: 7 -> 7, of which waited for: 5 -> 4; matrix products, arithmetic and copies ran while one was open for 0% -> 0% of each run, Pallas kernels for 15% -> 18%
where the time goes in v4:
time: 21.5 us; the launch traced here: 21.3 us
  starting transfers between devices  8.92 us (41%)
  waiting for transfers between devices  6.43 us (30%)
  Pallas kernels  5.86 us (27%)
    ppermute x3, starting transfers between devices, shards(): lax.ppermute(occupied, 'ka', [(i ^ by, i) for i in range(groups)])  4.46 us
    ppermute x4, starting transfers between devices, along(): return lax.ppermute(array, 'band', [(i, i ^ by) for i in range(band_count)])  4.46 us
    ppermute x4, waiting for transfers between devices, along(): return lax.ppermute(array, 'band', [(i, i ^ by) for i in range(band_count)])  4.38 us
    pallas_call x2, Pallas kernels, exchange(): pl.pallas_call(functools.partial(exchange_body, len(orbitals), first, tot...  3.55 us
    pallas_call x1, Pallas kernels, prepare(): pl.pallas_call(functools.partial(prepare_body, steps), out_shape=[pltpu.V...  2.3 us
    ppermute x3, waiting for transfers between devices, shards(): lax.ppermute(occupied, 'ka', [(i ^ by, i) for i in range(groups)])  2.05 us
  transfers between devices with their start and end apart: 7, of which 4 were waited for; matrix products, arithmetic and copies ran while one was open for 0% of the time, Pallas kernels for 18%

profile of v4, /device:TPU:0, one launch (start us, length us, event | category | flops | bytes accessed | tf_op | source)
XLA Modules:
  0.0 21.3 jit_solution(3214479541870658991)
XLA Ops:
  0.0 3.9 %collective-permute-start = (bf16[1,2,24,576]{3,2,1,0:T(8,128)(2,1)}, bf16[1,2,24,576]{3,2,1,0:T(8,128)(2,1)S(1)}, u32[]{:S(2)}, u32[]{:S(2)}) collective-permute-start(bf16[1,2,24,576]{3,2,1,0:T(8,128)(2,1)} %refs_0_.1), channel_id=1, source_target_pairs={{24,0},{16,8},{8,16},{0,24},{25,1},{17,9},{9,17},{1,25},{26,2},{18... | collective-permute-start | bytes 165896 | tf_op jit(solution)/shard_map/ppermute | solution.py:372
  3.9 0.5 %collective-permute-start.1 = (bf16[1,2,24,576]{3,2,1,0:T(8,128)(2,1)}, bf16[1,2,24,576]{3,2,1,0:T(8,128)(2,1)S(1)}, u32[]{:S(2)}, u32[]{:S(2)}) collective-permute-start(bf16[1,2,24,576]{3,2,1,0:T(8,128)(2,1)} %refs_0_.1), channel_id=1, source_target_pairs={{16,0},{24,8},{0,16},{8,24},{17,1},{25,9},{1,17},{9,25},{18,2},{26... | collective-permute-start | bytes 165896 | tf_op jit(solution)/shard_map/ppermute | solution.py:372
  4.4 0.1 collective-permute-start.2
  4.5 2.3 %shard_map.64 = (f32[2,3,1,24,8,128]{5,4,3,2,1,0:T(8,128)S(1)}, s32[1]{0:T(128)S(4)}, bf16[1,2,24,576]{3,2,1,0:T(8,128)(2,1)S(1)}, f32[1,2,24,576]{3,2,1,0:T(8,128)S(1)}, bf16[2,6,2,256,256]{4,3,2,1,0:T(8,128)(2,1)S(1)}) custom-call(s32[4]{0:T(128)} %partner_ref.1, s32[8,8]{1,0:T(8,128)} %index_ref.1, f32[16,24,576]{2,1,0:T(8,128)} %kernels_ref.1, ...), custom_call_target="tpu_custom_call" | custom-call | tf_op jit(solution)/shard_map/pallas_call | solution.py:192
  6.8 0.0 collective-permute-done.refs_1_
  6.8 1.5 %collective-permute-done.1.refs_2_ = bf16[1,2,24,576]{3,2,1,0:T(8,128)(2,1)S(1)} collective-permute-done((bf16[1,2,24,576]{3,2,1,0:T(8,128)(2,1)}, bf16[1,2,24,576]{3,2,1,0:T(8,128)(2,1)S(1)}, u32[]{:S(2)}, u32[]{:S(2)}) %collective-permute-start.1) | collective-permute-done | bytes 55328 | tf_op jit(solution)/shard_map/ppermute | solution.py:372
  8.3 0.5 %collective-permute-done.2.refs_3_ = bf16[1,2,24,576]{3,2,1,0:T(8,128)(2,1)S(1)} collective-permute-done((bf16[1,2,24,576]{3,2,1,0:T(8,128)(2,1)}, bf16[1,2,24,576]{3,2,1,0:T(8,128)(2,1)S(1)}, u32[]{:S(2)}, u32[]{:S(2)}) %collective-permute-start.2) | collective-permute-done | bytes 55328 | tf_op jit(solution)/shard_map/ppermute | solution.py:372
  8.8 3.6 %collective-permute-start.5 = (bf16[1,2,24,576]{3,2,1,0:T(8,128)(2,1)S(1)}, bf16[1,2,24,576]{3,2,1,0:T(8,128)(2,1)S(1)}, u32[]{:S(2)}, u32[]{:S(2)}) collective-permute-start(bf16[1,2,24,576]{3,2,1,0:T(8,128)(2,1)S(1)} %shard_map.65), channel_id=1, source_target_pairs={{0,6},{1,7},{2,4},{3,5},{4,2},{5,3},{6,0},{7,1},{8,14},{9,15},{10,... | collective-permute-start | bytes 165896 | tf_op jit(solution)/shard_map/ppermute | solution.py:376
  12.4 0.0 collective-permute-start.4
  12.4 0.8 %collective-permute-start.3 = (bf16[1,2,24,576]{3,2,1,0:T(8,128)(2,1)S(1)}, bf16[1,2,24,576]{3,2,1,0:T(8,128)(2,1)S(1)}, u32[]{:S(2)}, u32[]{:S(2)}) collective-permute-start(bf16[1,2,24,576]{3,2,1,0:T(8,128)(2,1)S(1)} %shard_map.65), channel_id=1, source_target_pairs={{0,2},{1,3},{2,0},{3,1},{4,6},{5,7},{6,4},{7,5},{8,10},{9,11},{10,... | collective-permute-start | bytes 165896 | tf_op jit(solution)/shard_map/ppermute | solution.py:376
  13.2 1.6 %collective-permute-done.5 = bf16[1,2,24,576]{3,2,1,0:T(8,128)(2,1)S(1)} collective-permute-done((bf16[1,2,24,576]{3,2,1,0:T(8,128)(2,1)S(1)}, bf16[1,2,24,576]{3,2,1,0:T(8,128)(2,1)S(1)}, u32[]{:S(2)}, u32[]{:S(2)}) %collective-permute-start.5) | collective-permute-done | bytes 55328 | tf_op jit(solution)/shard_map/ppermute | solution.py:376
  14.9 2.7 %collective-permute-done.4 = bf16[1,2,24,576]{3,2,1,0:T(8,128)(2,1)S(1)} collective-permute-done((bf16[1,2,24,576]{3,2,1,0:T(8,128)(2,1)S(1)}, bf16[1,2,24,576]{3,2,1,0:T(8,128)(2,1)S(1)}, u32[]{:S(2)}, u32[]{:S(2)}) %collective-permute-start.4) | collective-permute-done | bytes 55328 | tf_op jit(solution)/shard_map/ppermute | solution.py:376
  17.6 0.0 collective-permute-done.3
  17.6 0.1 pad_maximum_fusion.refs_0_
  17.6 0.1 collective-permute-start.6
  17.7 1.4 %shard_map.66.refs_4_ = f32[1,2,24,576]{3,2,1,0:T(8,128)S(1)} custom-call(bf16[4,2,24,576]{3,2,1,0:T(8,128)(2,1)S(1)} %pad_maximum_fusion.refs_0_, f32[1,2,24,576]{3,2,1,0:T(8,128)S(1)} %get-tuple-element.12.refs_1_, bf16[2,6,2,256,256]{4,3,2,1,0:T(8,128)(2,1)S(1)} %get-tuple-element.13.refs_2_, f32[2,3,1,24,8,128]{5,4,3,2,1,0:T(8,128)S(1)} %get-tuple-element.14.refs_3_), custom_call_target="tpu_custom_call" | custom-call | tf_op jit(solution)/shard_map/pallas_call | solution.py:347
  19.2 0.0 collective-permute-done.6.refs_0_
  19.2 2.1 %shard_map.67 = f32[1,2,24,576]{3,2,1,0:T(8,128)} custom-call(bf16[4,2,24,576]{3,2,1,0:T(8,128)(2,1)S(1)} %collective-permute-done.6.refs_0_, f32[1,2,24,576]{3,2,1,0:T(8,128)S(1)} %get-tuple-element.12.refs_1_, bf16[2,6,2,256,256]{4,3,2,1,0:T(8,128)(2,1)S(1)} %get-tuple-element.13.refs_2_, f32[2,3,1,24,8,128]{5,4,3,2,1,0:T(8,128)S(1)} %get-tuple-element.14.refs_3_, ...), custom_call_target="tpu_custom_call" | custom-call | tf_op jit(solution)/shard_map/pallas_call | solution.py:347
  (1 shorter events, 0.0 us)
Async XLA Ops:
  0.0 6.8 %collective-permute-start = (bf16[1,2,24,576]{3,2,1,0:T(8,128)(2,1)}, bf16[1,2,24,576]{3,2,1,0:T(8,128)(2,1)S(1)}, u32[]{:S(2)}, u32[]{:S(2)}) collective-permute-start(bf16[1,2,24,576]{3,2,1,0:T(8,128)(2,1)} %refs_0_.1), channel_id=1, source_target_pairs={{24,0},{16,8},{8,16},{0,24},{25,1},{17,9},{9,17},{1,25},{26,2},{18... | collective-permute-start | bytes 165896 | tf_op jit(solution)/shard_map/ppermute | solution.py:372
  3.9 4.4 %collective-permute-start.1 = (bf16[1,2,24,576]{3,2,1,0:T(8,128)(2,1)}, bf16[1,2,24,576]{3,2,1,0:T(8,128)(2,1)S(1)}, u32[]{:S(2)}, u32[]{:S(2)}) collective-permute-start(bf16[1,2,24,576]{3,2,1,0:T(8,128)(2,1)} %refs_0_.1), channel_id=1, source_target_pairs={{16,0},{24,8},{0,16},{8,24},{17,1},{25,9},{1,17},{9,25},{18,2},{26... | collective-permute-start | bytes 165896 | tf_op jit(solution)/shard_map/ppermute | solution.py:372
  4.4 4.4 %collective-permute-start.2 = (bf16[1,2,24,576]{3,2,1,0:T(8,128)(2,1)}, bf16[1,2,24,576]{3,2,1,0:T(8,128)(2,1)S(1)}, u32[]{:S(2)}, u32[]{:S(2)}) collective-permute-start(bf16[1,2,24,576]{3,2,1,0:T(8,128)(2,1)} %refs_0_.1), channel_id=1, source_target_pairs={{8,0},{0,8},{24,16},{16,24},{9,1},{1,9},{25,17},{17,25},{10,2},{2,... | collective-permute-start | bytes 165896 | tf_op jit(solution)/shard_map/ppermute | solution.py:372
  8.8 6.0 %collective-permute-start.5 = (bf16[1,2,24,576]{3,2,1,0:T(8,128)(2,1)S(1)}, bf16[1,2,24,576]{3,2,1,0:T(8,128)(2,1)S(1)}, u32[]{:S(2)}, u32[]{:S(2)}) collective-permute-start(bf16[1,2,24,576]{3,2,1,0:T(8,128)(2,1)S(1)} %shard_map.65), channel_id=1, source_target_pairs={{0,6},{1,7},{2,4},{3,5},{4,2},{5,3},{6,0},{7,1},{8,14},{9,15},{10,... | collective-permute-start | bytes 165896 | tf_op jit(solution)/shard_map/ppermute | solution.py:376
  12.4 5.1 %collective-permute-start.4 = (bf16[1,2,24,576]{3,2,1,0:T(8,128)(2,1)S(1)}, bf16[1,2,24,576]{3,2,1,0:T(8,128)(2,1)S(1)}, u32[]{:S(2)}, u32[]{:S(2)}) collective-permute-start(bf16[1,2,24,576]{3,2,1,0:T(8,128)(2,1)S(1)} %shard_map.65), channel_id=1, source_target_pairs={{0,4},{1,5},{2,6},{3,7},{4,0},{5,1},{6,2},{7,3},{8,12},{9,13},{10,... | collective-permute-start | bytes 165896 | tf_op jit(solution)/shard_map/ppermute | solution.py:376
  12.4 5.1 %collective-permute-start.3 = (bf16[1,2,24,576]{3,2,1,0:T(8,128)(2,1)S(1)}, bf16[1,2,24,576]{3,2,1,0:T(8,128)(2,1)S(1)}, u32[]{:S(2)}, u32[]{:S(2)}) collective-permute-start(bf16[1,2,24,576]{3,2,1,0:T(8,128)(2,1)S(1)} %shard_map.65), channel_id=1, source_target_pairs={{0,2},{1,3},{2,0},{3,1},{4,6},{5,7},{6,4},{7,5},{8,10},{9,11},{10,... | collective-permute-start | bytes 165896 | tf_op jit(solution)/shard_map/ppermute | solution.py:376
  17.6 1.6 %collective-permute-start.6 = (bf16[4,2,24,576]{3,2,1,0:T(8,128)(2,1)S(1)}, bf16[4,2,24,576]{3,2,1,0:T(8,128)(2,1)S(1)}, u32[]{:S(2)}, u32[]{:S(2)}) collective-permute-start(bf16[4,2,24,576]{3,2,1,0:T(8,128)(2,1)S(1)} %pad_maximum_fusion.refs_0_), channel_id=1, source_target_pairs={{0,1},{1,0},{2,3},{3,2},{4,5},{5,4},{6,7},{7,6},{8,9},{9,8},{10,11... | collective-permute-start | bytes 663560 | tf_op jit(solution)/shard_map/ppermute | solution.py:376

commit v5 on v4

--- a/solution.py
+++ b/solution.py
@@ -244,30 +244,33 @@
     return found
 
 
-def exchange_body(count, first, started, *refs):
-    orbital_refs, refs = refs[:count], refs[count:]
-    target_ref, plane_ref, kernel_ref, refs = refs[0], refs[1], refs[2], refs[3:]
-    out_ref, field_ref, held_ref, work_ref = refs[-4:]
-    grid_size, plane = target_ref.shape[2:]
+def exchange_body(given, aims, first, started, *refs):
+    orbital_refs, target_refs, refs = refs[:given], refs[given : given + aims], refs[given + aims :]
+    plane_ref, kernel_ref, refs = refs[0], refs[1], refs[2:]
+    total_refs, refs = refs[: aims * started], refs[aims * started :]
+    out_refs, (field_ref, held_ref, work_ref) = refs[:aims], refs[aims:]
+    grid_size, plane = target_refs[0].shape[2:]
     width = plane // RADIX
     lanes = padded(width) // LANES
-    size = BATCH * grid_size
-    members = [(ref, row) for ref in orbital_refs for row in range(ref.shape[0])]
+    members = [(aim, ref, row) for aim in range(aims) for ref in orbital_refs for row in range(ref.shape[0])]
+    written = set()
     for start in range(0, len(members), BATCH):
-        batch = (first + start) // BATCH
-        for place, (ref, row) in enumerate(members[start : start + BATCH]):
+        batch = first + start // BATCH
+        count = min(BATCH, len(members) - start)
+        size = count * grid_size
+        for place, (_, ref, row) in enumerate(members[start : start + count]):
             for part in range(2):
                 for block, values in enumerate(lane_blocks(ref[row, part], width)):
                     held_ref[place, part, block] = values.astype(F32)
         starts = {}
         for tile in range(0, grid_size, SUBLANES):
             rows = slice(tile, tile + SUBLANES)
-            target = [lane_blocks(target_ref[0, part, rows], width) for part in range(2)]
-            for place in range(BATCH):
+            targets = [[lane_blocks(ref[0, part, rows], width) for part in range(2)] for ref in target_refs]
+            for place in range(count):
                 blocks = []
                 for block in range(RADIX):
                     real, imag = (held_ref[place, part, block, rows] for part in range(2))
-                    target_real, target_imag = target[0][block], target[1][block]
+                    target_real, target_imag = (targets[members[start + place][0]][part][block] for part in range(2))
                     blocks.append(
                         (
                             real * target_real + imag * target_imag,
@@ -284,7 +287,7 @@
                 parts = [jnp.concatenate([starts[residue, part, at] for at in range(0, size, SUBLANES)], axis=0) for part in range(2)]
                 parts = plane_transform(*parts, [plane_ref[0, residue, j] for j in range(2)])
                 for part in range(2):
-                    field_ref[fold, part, upper * size : (upper + 1) * size] = parts[part]
+                    field_ref[fold, part, upper * BATCH * grid_size : upper * BATCH * grid_size + size] = parts[part]
 
         def over_line(fold):
             for lane in range(lanes):
@@ -306,7 +309,7 @@
         def back(fold):
             for upper in range(FOLD):
                 residue = fold * FOLD + upper
-                parts = [field_ref[fold, part, upper * size : (upper + 1) * size] for part in range(2)]
+                parts = [field_ref[fold, part, upper * BATCH * grid_size : upper * BATCH * grid_size + size] for part in range(2)]
                 parts = plane_transform(*parts, [plane_ref[1, residue, j] for j in range(2)])
                 ends[residue] = parts
 
@@ -320,41 +323,46 @@
                 back(turn_number - 2)
         for tile in range(0, grid_size, SUBLANES):
             rows = slice(tile, tile + SUBLANES)
-            totals = [[0.0, 0.0] for _ in range(RADIX)]
-            for place in range(BATCH):
+            totals = [[[0.0, 0.0] for _ in range(RADIX)] for _ in range(aims)]
+            for place in range(count):
+                aim = members[start + place][0]
                 at = slice(place * grid_size + tile, place * grid_size + tile + SUBLANES)
                 blocks = line_transform(
                     [tuple(ends[residue][part][at] for part in range(2)) for residue in range(RADIX)], -1.0
                 )
                 for block, (pot_real, pot_imag) in enumerate(blocks):
                     real, imag = (held_ref[place, part, block, rows] for part in range(2))
-                    totals[block][0] -= real * pot_real - imag * pot_imag
-                    totals[block][1] -= real * pot_imag + imag * pot_real
-            for part in range(2):
-                found = jnp.concatenate([totals[block][part][:, :width] for block in range(RADIX)], axis=1)
-                if start:
-                    found = out_ref[0, part, rows] + found
-                elif started:
-                    found = refs[0][0, part, rows] + found
-                out_ref[0, part, rows] = found
-
-
-def exchange(orbitals, first, target, tables, kernels, total=None):
-    grid_size, plane = target.shape[2:]
+                    totals[aim][block][0] -= real * pot_real - imag * pot_imag
+                    totals[aim][block][1] -= real * pot_imag + imag * pot_real
+            for aim in sorted({members[start + place][0] for place in range(count)}):
+                for part in range(2):
+                    found = [totals[aim][block][part][:, :width] for block in range(RADIX)]
+                    found = jnp.concatenate(found, axis=1)
+                    if (aim, tile) in written:
+                        found = out_refs[aim][0, part, rows] + found
+                    elif started:
+                        found = total_refs[aim][0, part, rows] + found
+                    out_refs[aim][0, part, rows] = found
+                written.add((aim, tile))
+
+
+def exchange(orbitals, targets, first, tables, kernels, totals=(), **options):
+    grid_size, plane = targets[0].shape[2:]
     room = padded(plane // RADIX)
-    given = [*orbitals, target, tables, kernels] + ([] if total is None else [total])
+    given = [*orbitals, *targets, tables, kernels, *totals]
     whole = pl.BlockSpec(memory_space=pltpu.VMEM)
     return pl.pallas_call(
-        functools.partial(exchange_body, len(orbitals), first, total is not None),
-        out_shape=jax.ShapeDtypeStruct(target.shape, F32) if total is not None else pltpu.VMEM(target.shape, F32),
+        functools.partial(exchange_body, len(orbitals), len(targets), first, len(totals) > 0),
+        out_shape=[pltpu.VMEM(array.shape, F32) for array in targets],
         in_specs=[whole] * len(given),
-        out_specs=whole,
+        out_specs=[whole] * len(targets),
         scratch_shapes=[
             pltpu.VMEM((RADIX // FOLD, 2, SUBLANES * grid_size, room), F32),
             pltpu.VMEM((BATCH, 2, RADIX, grid_size, room), F32),
             pltpu.VMEM((RADIX, 2, BATCH * grid_size, room), F32),
         ],
         compiler_params=pltpu.CompilerParams(vmem_limit_bytes=SCOPED_BYTES),
+        **options,
     )(*given)
 
 
@@ -363,7 +371,12 @@
     band_count = lax.axis_size("band")
     chips = band_count // 2
 
-    steps = list(range(chips)) * 2
+    def along(array, by):
+        return lax.ppermute(array, "band", [(i, i ^ by) for i in range(band_count)])
+
+    near_steps = list(range(chips - 2, 0, -1))
+    steps = [0, chips - 1] * (BATCH // 2) + near_steps
+    steps += [0] * (-len(steps) % BATCH)
     tables = jnp.asarray(plane_tables(targets.shape[2]))
     kernel_blocks, shift, own, target, tables = prepare(
         steps, partner, kernel_index, kernels, occupied, targets, tables
@@ -372,13 +385,15 @@
     came = [lax.ppermute(occupied, "ka", [(i ^ by, i) for i in range(groups)]) for by in shifts]
     visitor = choose(shift, [0, *shifts], [own, *came])
 
-    def along(array, by):
-        return lax.ppermute(array, "band", [(i, i ^ by) for i in range(band_count)])
-
-    mine = jnp.concatenate([visitor, *[along(visitor, 2 * step) for step in steps[1:chips]]], axis=0)
-    others = along(mine, 1)
-    total = exchange([mine], 0, target, tables, kernel_blocks)
-    return exchange([others], chips, target, tables, kernel_blocks, total)
+    sibling = along(target, 1)
+    early = [visitor, along(visitor, 2 * (chips - 1))]
+    late = [along(visitor, 2 * step) for step in near_steps]
+    free = pl.CostEstimate(flops=0, bytes_accessed=0, transcendentals=0)
+    mine, other = exchange(early, [target, sibling], 0, tables, kernel_blocks, cost_estimate=free)
+    (other,) = exchange(late, [sibling], 1, tables, kernel_blocks, [other])
+    came = along(other, 1)
+    (mine,) = exchange(late, [target], 1, tables, kernel_blocks, [mine])
+    return mine + came
 
 
 def solution(mesh):

time: 21.5 us -> 21 us (0.977)
  waiting for transfers between devices: 6.43 us -> 4.85 us
  other arithmetic: 0.05 us -> 0.66 us
  Pallas kernels: 5.86 us -> 6.33 us
    ppermute x4 -> x5, waiting for transfers between devices: 4.38 us -> 2.85 us  [along(): return lax.ppermute(array, 'band', [(i, i ^ by) for i in range(band_count)])]
    add x0 -> x1, other arithmetic: none -> 0.66 us  [shards(): return mine + came]
    pallas_call x2 -> x3, Pallas kernels: 3.55 us -> 4.02 us  [exchange(): pl.pallas_call(functools.partial(exchange_body, len(orbitals), len(target...]
    ppermute x4 -> x5, starting transfers between devices: 4.46 us -> 4.53 us  [along(): return lax.ppermute(array, 'band', [(i, i ^ by) for i in range(band_count)])]
  transfers between devices with their start and end apart: 7 -> 8, of which waited for: 4 -> 6; matrix products, arithmetic and copies ran while one was open for 0% -> 0% of each run, Pallas kernels for 18% -> 24%
where the time goes in v5:
time: 21 us; the launch traced here: 20.9 us
  starting transfers between devices  8.99 us (43%)
  Pallas kernels  6.33 us (30%)
  waiting for transfers between devices  4.85 us (23%)
  other arithmetic  0.66 us (3%)
    ppermute x5, starting transfers between devices, along(): return lax.ppermute(array, 'band', [(i, i ^ by) for i in range(band_count)])  4.53 us
    ppermute x3, starting transfers between devices, shards(): lax.ppermute(occupied, 'ka', [(i ^ by, i) for i in range(groups)])  4.46 us
    pallas_call x3, Pallas kernels, exchange(): pl.pallas_call(functools.partial(exchange_body, len(orbitals), len(target...  4.02 us
    ppermute x5, waiting for transfers between devices, along(): return lax.ppermute(array, 'band', [(i, i ^ by) for i in range(band_count)])  2.85 us
    pallas_call x1, Pallas kernels, prepare(): pl.pallas_call(functools.partial(prepare_body, steps), out_shape=[pltpu.V...  2.3 us
    ppermute x3, waiting for transfers between devices, shards(): lax.ppermute(occupied, 'ka', [(i ^ by, i) for i in range(groups)])  2 us
    add x1, other arithmetic, shards(): return mine + came  0.66 us
  transfers between devices with their start and end apart: 8, of which 6 were waited for; matrix products, arithmetic and copies ran while one was open for 0% of the time, Pallas kernels for 24%

profile of v5, /device:TPU:0, one launch (start us, length us, event | category | flops | bytes accessed | tf_op | source)
XLA Modules:
  0.0 20.9 jit_solution(5139537109048357329)
XLA Ops:
  0.0 3.9 %collective-permute-start = (bf16[1,2,24,576]{3,2,1,0:T(8,128)(2,1)}, bf16[1,2,24,576]{3,2,1,0:T(8,128)(2,1)S(1)}, u32[]{:S(2)}, u32[]{:S(2)}) collective-permute-start(bf16[1,2,24,576]{3,2,1,0:T(8,128)(2,1)} %refs_0_.1), channel_id=1, source_target_pairs={{24,0},{16,8},{8,16},{0,24},{25,1},{17,9},{9,17},{1,25},{26,2},{18... | collective-permute-start | bytes 165896 | tf_op jit(solution)/shard_map/ppermute | solution.py:385
  3.9 0.5 %collective-permute-start.2 = (bf16[1,2,24,576]{3,2,1,0:T(8,128)(2,1)}, bf16[1,2,24,576]{3,2,1,0:T(8,128)(2,1)S(1)}, u32[]{:S(2)}, u32[]{:S(2)}) collective-permute-start(bf16[1,2,24,576]{3,2,1,0:T(8,128)(2,1)} %refs_0_.1), channel_id=1, source_target_pairs={{8,0},{0,8},{24,16},{16,24},{9,1},{1,9},{25,17},{17,25},{10,2},{2,... | collective-permute-start | bytes 165896 | tf_op jit(solution)/shard_map/ppermute | solution.py:385
  4.4 0.0 collective-permute-start.1
  4.5 2.3 %shard_map.64 = (f32[2,3,1,24,8,128]{5,4,3,2,1,0:T(8,128)S(1)}, s32[1]{0:T(128)S(4)}, bf16[1,2,24,576]{3,2,1,0:T(8,128)(2,1)S(1)}, f32[1,2,24,576]{3,2,1,0:T(8,128)S(1)}, bf16[2,6,2,256,256]{4,3,2,1,0:T(8,128)(2,1)S(1)}) custom-call(s32[4]{0:T(128)} %partner_ref.1, s32[8,8]{1,0:T(8,128)} %index_ref.1, f32[16,24,576]{2,1,0:T(8,128)} %kernels_ref.1, ...), custom_call_target="tpu_custom_call" | custom-call | tf_op jit(solution)/shard_map/pallas_call | solution.py:192
  6.8 0.1 collective-permute-start.6
  6.9 0.0 collective-permute-done.refs_1_
  6.9 1.5 %collective-permute-done.2.refs_3_ = bf16[1,2,24,576]{3,2,1,0:T(8,128)(2,1)S(1)} collective-permute-done((bf16[1,2,24,576]{3,2,1,0:T(8,128)(2,1)}, bf16[1,2,24,576]{3,2,1,0:T(8,128)(2,1)S(1)}, u32[]{:S(2)}, u32[]{:S(2)}) %collective-permute-start.2) | collective-permute-done | bytes 55328 | tf_op jit(solution)/shard_map/ppermute | solution.py:385
  8.3 0.5 %collective-permute-done.1.refs_2_ = bf16[1,2,24,576]{3,2,1,0:T(8,128)(2,1)S(1)} collective-permute-done((bf16[1,2,24,576]{3,2,1,0:T(8,128)(2,1)}, bf16[1,2,24,576]{3,2,1,0:T(8,128)(2,1)S(1)}, u32[]{:S(2)}, u32[]{:S(2)}) %collective-permute-start.1) | collective-permute-done | bytes 55328 | tf_op jit(solution)/shard_map/ppermute | solution.py:385
  8.9 3.6 %collective-permute-start.5 = (bf16[1,2,24,576]{3,2,1,0:T(8,128)(2,1)S(1)}, bf16[1,2,24,576]{3,2,1,0:T(8,128)(2,1)S(1)}, u32[]{:S(2)}, u32[]{:S(2)}) collective-permute-start(bf16[1,2,24,576]{3,2,1,0:T(8,128)(2,1)S(1)} %shard_map.65.refs_0_), channel_id=1, source_target_pairs={{0,6},{1,7},{2,4},{3,5},{4,2},{5,3},{6,0},{7,1},{8,14},{9,15},{10,... | collective-permute-start | bytes 165896 | tf_op jit(solution)/shard_map/ppermute | solution.py:375
  12.5 0.0 collective-permute-start.4
  12.5 0.8 %collective-permute-start.3 = (bf16[1,2,24,576]{3,2,1,0:T(8,128)(2,1)S(1)}, bf16[1,2,24,576]{3,2,1,0:T(8,128)(2,1)S(1)}, u32[]{:S(2)}, u32[]{:S(2)}) collective-permute-start(bf16[1,2,24,576]{3,2,1,0:T(8,128)(2,1)S(1)} %shard_map.65.refs_0_), channel_id=1, source_target_pairs={{0,4},{1,5},{2,6},{3,7},{4,0},{5,1},{6,2},{7,3},{8,12},{9,13},{10,... | collective-permute-start | bytes 165896 | tf_op jit(solution)/shard_map/ppermute | solution.py:375
  13.3 1.7 %collective-permute-done.5.refs_1_ = bf16[1,2,24,576]{3,2,1,0:T(8,128)(2,1)S(1)} collective-permute-done((bf16[1,2,24,576]{3,2,1,0:T(8,128)(2,1)S(1)}, bf16[1,2,24,576]{3,2,1,0:T(8,128)(2,1)S(1)}, u32[]{:S(2)}, u32[]{:S(2)}) %collective-permute-start.5) | collective-permute-done | bytes 55328 | tf_op jit(solution)/shard_map/ppermute | solution.py:375
  15.0 0.0 collective-permute-done.6.refs_3_.refs_2_
  15.0 1.6 %shard_map.66 = (f32[1,2,24,576]{3,2,1,0:T(8,128)S(1)}, f32[1,2,24,576]{3,2,1,0:T(8,128)S(1)}) custom-call(bf16[1,2,24,576]{3,2,1,0:T(8,128)(2,1)S(1)} %shard_map.65.refs_0_, bf16[1,2,24,576]{3,2,1,0:T(8,128)(2,1)S(1)} %collective-permute-done.5.refs_1_, f32[1,2,24,576]{3,2,1,0:T(8,128)S(1)} %get-tuple-element.14.refs_2_, ...), custom_call_target="tpu_custom_call" | custom-call | tf_op jit(solution)/shard_map/pallas_call | solution.py:354
  16.6 0.1 collective-permute-done.4.refs_1_
  16.7 0.9 %collective-permute-done.3.refs_0_ = bf16[1,2,24,576]{3,2,1,0:T(8,128)(2,1)S(1)} collective-permute-done((bf16[1,2,24,576]{3,2,1,0:T(8,128)(2,1)S(1)}, bf16[1,2,24,576]{3,2,1,0:T(8,128)(2,1)S(1)}, u32[]{:S(2)}, u32[]{:S(2)}) %collective-permute-start.3) | collective-permute-done | bytes 55328 | tf_op jit(solution)/shard_map/ppermute | solution.py:375
  17.6 1.2 %shard_map.68 = f32[1,2,24,576]{3,2,1,0:T(8,128)S(1)} custom-call(bf16[1,2,24,576]{3,2,1,0:T(8,128)(2,1)S(1)} %collective-permute-done.3.refs_0_, bf16[1,2,24,576]{3,2,1,0:T(8,128)(2,1)S(1)} %collective-permute-done.4.refs_1_, f32[1,2,24,576]{3,2,1,0:T(8,128)S(1)} %collective-permute-done.6.refs_3_.refs_2_, ...), custom_call_target="tpu_custom_call" | custom-call | tf_op jit(solution)/shard_map/pallas_call | solution.py:354
  18.8 0.1 collective-permute-start.7
  18.9 1.2 %shard_map.67 = f32[1,2,24,576]{3,2,1,0:T(8,128)S(1)} custom-call(bf16[1,2,24,576]{3,2,1,0:T(8,128)(2,1)S(1)} %collective-permute-done.3.refs_0_, bf16[1,2,24,576]{3,2,1,0:T(8,128)(2,1)S(1)} %collective-permute-done.4.refs_1_, f32[1,2,24,576]{3,2,1,0:T(8,128)S(1)} %get-tuple-element.14.refs_2_, ...), custom_call_target="tpu_custom_call" | custom-call | tf_op jit(solution)/shard_map/pallas_call | solution.py:354
  20.1 0.1 collective-permute-done.7
  20.2 0.7 %add.3 = f32[1,2,24,576]{3,2,1,0:T(8,128)} add(f32[1,2,24,576]{3,2,1,0:T(8,128)S(1)} %shard_map.67, f32[1,2,24,576]{3,2,1,0:T(8,128)S(1)} %collective-permute-done.7) | non-fusion elementwise | flops 27648 | bytes 331776 | tf_op jit(solution)/shard_map/add | solution.py:396
  (1 shorter events, 0.0 us)
Async XLA Ops:
  0.0 6.9 %collective-permute-start = (bf16[1,2,24,576]{3,2,1,0:T(8,128)(2,1)}, bf16[1,2,24,576]{3,2,1,0:T(8,128)(2,1)S(1)}, u32[]{:S(2)}, u32[]{:S(2)}) collective-permute-start(bf16[1,2,24,576]{3,2,1,0:T(8,128)(2,1)} %refs_0_.1), channel_id=1, source_target_pairs={{24,0},{16,8},{8,16},{0,24},{25,1},{17,9},{9,17},{1,25},{26,2},{18... | collective-permute-start | bytes 165896 | tf_op jit(solution)/shard_map/ppermute | solution.py:385
  3.9 4.4 %collective-permute-start.2 = (bf16[1,2,24,576]{3,2,1,0:T(8,128)(2,1)}, bf16[1,2,24,576]{3,2,1,0:T(8,128)(2,1)S(1)}, u32[]{:S(2)}, u32[]{:S(2)}) collective-permute-start(bf16[1,2,24,576]{3,2,1,0:T(8,128)(2,1)} %refs_0_.1), channel_id=1, source_target_pairs={{8,0},{0,8},{24,16},{16,24},{9,1},{1,9},{25,17},{17,25},{10,2},{2,... | collective-permute-start | bytes 165896 | tf_op jit(solution)/shard_map/ppermute | solution.py:385
  4.4 4.4 %collective-permute-start.1 = (bf16[1,2,24,576]{3,2,1,0:T(8,128)(2,1)}, bf16[1,2,24,576]{3,2,1,0:T(8,128)(2,1)S(1)}, u32[]{:S(2)}, u32[]{:S(2)}) collective-permute-start(bf16[1,2,24,576]{3,2,1,0:T(8,128)(2,1)} %refs_0_.1), channel_id=1, source_target_pairs={{16,0},{24,8},{0,16},{8,24},{17,1},{25,9},{1,17},{9,25},{18,2},{26... | collective-permute-start | bytes 165896 | tf_op jit(solution)/shard_map/ppermute | solution.py:385
  6.8 8.2 %collective-permute-start.6 = (f32[1,2,24,576]{3,2,1,0:T(8,128)S(1)}, f32[1,2,24,576]{3,2,1,0:T(8,128)S(1)}, u32[]{:S(2)}, u32[]{:S(2)}) collective-permute-start(f32[1,2,24,576]{3,2,1,0:T(8,128)S(1)} %get-tuple-element.14.refs_2_), channel_id=1, source_target_pairs={{0,1},{1,0},{2,3},{3,2},{4,5},{5,4},{6,7},{7,6},{8,9},{9,8},{10,11... | collective-permute-start | bytes 331784 | tf_op jit(solution)/shard_map/ppermute | solution.py:375
  8.9 6.1 %collective-permute-start.5 = (bf16[1,2,24,576]{3,2,1,0:T(8,128)(2,1)S(1)}, bf16[1,2,24,576]{3,2,1,0:T(8,128)(2,1)S(1)}, u32[]{:S(2)}, u32[]{:S(2)}) collective-permute-start(bf16[1,2,24,576]{3,2,1,0:T(8,128)(2,1)S(1)} %shard_map.65.refs_0_), channel_id=1, source_target_pairs={{0,6},{1,7},{2,4},{3,5},{4,2},{5,3},{6,0},{7,1},{8,14},{9,15},{10,... | collective-permute-start | bytes 165896 | tf_op jit(solution)/shard_map/ppermute | solution.py:375
  12.5 4.2 %collective-permute-start.4 = (bf16[1,2,24,576]{3,2,1,0:T(8,128)(2,1)S(1)}, bf16[1,2,24,576]{3,2,1,0:T(8,128)(2,1)S(1)}, u32[]{:S(2)}, u32[]{:S(2)}) collective-permute-start(bf16[1,2,24,576]{3,2,1,0:T(8,128)(2,1)S(1)} %shard_map.65.refs_0_), channel_id=1, source_target_pairs={{0,2},{1,3},{2,0},{3,1},{4,6},{5,7},{6,4},{7,5},{8,10},{9,11},{10,... | collective-permute-start | bytes 165896 | tf_op jit(solution)/shard_map/ppermute | solution.py:375
  12.5 5.1 %collective-permute-start.3 = (bf16[1,2,24,576]{3,2,1,0:T(8,128)(2,1)S(1)}, bf16[1,2,24,576]{3,2,1,0:T(8,128)(2,1)S(1)}, u32[]{:S(2)}, u32[]{:S(2)}) collective-permute-start(bf16[1,2,24,576]{3,2,1,0:T(8,128)(2,1)S(1)} %shard_map.65.refs_0_), channel_id=1, source_target_pairs={{0,4},{1,5},{2,6},{3,7},{4,0},{5,1},{6,2},{7,3},{8,12},{9,13},{10,... | collective-permute-start | bytes 165896 | tf_op jit(solution)/shard_map/ppermute | solution.py:375
  18.8 1.4 %collective-permute-start.7 = (f32[1,2,24,576]{3,2,1,0:T(8,128)S(1)}, f32[1,2,24,576]{3,2,1,0:T(8,128)S(1)}, u32[]{:S(2)}, u32[]{:S(2)}) collective-permute-start(f32[1,2,24,576]{3,2,1,0:T(8,128)S(1)} %shard_map.68), channel_id=1, source_target_pairs={{0,1},{1,0},{2,3},{3,2},{4,5},{5,4},{6,7},{7,6},{8,9},{9,8},{10,11... | collective-permute-start | bytes 331784 | tf_op jit(solution)/shard_map/ppermute | solution.py:375

commit v6 on v5

--- a/solution.py
+++ b/solution.py
@@ -16,7 +16,7 @@
 LANES = 128
 SUBLANES = 8
 FOLD = SUBLANES // BATCH
-CARRIED = 3
+CARRIED = 4
 SCOPED_BYTES = 16 * 1024 * 1024
 BF16 = jnp.bfloat16
 F32 = jnp.float32
@@ -37,18 +37,20 @@
     width = inner * grid_size
     room = padded(width) - width
     b, c = np.divmod(np.arange(width), grid_size)
-    found = []
-    for sign in (1.0, -1.0):
-        for residue in range(RADIX):
-            turns = b[:, None] * (RADIX * b[None, :] + residue) + c[:, None] * c[None, :]
-            angles = (turns % grid_size) * (2.0 * np.pi / grid_size)
-            if sign < 0:
-                angles = angles.T
-            cosine = np.pad(np.cos(angles), [(0, room)] * 2)
-            sine = np.pad(sign * np.sin(angles), [(0, room)] * 2)
-            found.append(split_table(np.block([[cosine, -sine], [sine, cosine]])))
-    found = np.array(found)
-    return found.reshape((2, RADIX) + found.shape[1:])
+    turns = RADIX * b[:, None] * b[None, :] + c[:, None] * c[None, :]
+    angles = (turns % grid_size) * (2.0 * np.pi / grid_size)
+    cosine = np.pad(np.cos(angles), [(0, room)] * 2)
+    sine = np.pad(np.sin(angles), [(0, room)] * 2)
+    found = [split_table(np.block([[cosine, -sign * sine], [sign * sine, cosine]])) for sign in (1.0, -1.0)]
+    return np.array(found)
+
+
+def twist_tables(grid_size):
+    width = grid_size // RADIX * grid_size
+    b = np.pad(np.arange(width) // grid_size, (0, padded(width) - width))
+    angles = np.arange(RADIX)[:, None] * b[None, :] * (2.0 * np.pi / grid_size)
+    found = np.stack([np.cos(angles), np.sin(angles)], axis=1)
+    return np.repeat(found[:, :, None], SUBLANES, axis=2).astype(np.float32)
 
 
 def halves(values):
@@ -246,9 +248,9 @@
 
 def exchange_body(given, aims, first, started, *refs):
     orbital_refs, target_refs, refs = refs[:given], refs[given : given + aims], refs[given + aims :]
-    plane_ref, kernel_ref, refs = refs[0], refs[1], refs[2:]
+    plane_ref, twist_ref, kernel_ref, refs = refs[0], refs[1], refs[2], refs[3:]
     total_refs, refs = refs[: aims * started], refs[aims * started :]
-    out_refs, (field_ref, held_ref, work_ref) = refs[:aims], refs[aims:]
+    out_refs, (field_ref, held_ref) = refs[:aims], refs[aims:]
     grid_size, plane = target_refs[0].shape[2:]
     width = plane // RADIX
     lanes = padded(width) // LANES
@@ -278,16 +280,21 @@
                         )
                     )
                 at = place * grid_size + tile
-                for residue, value in enumerate(line_transform(blocks, 1.0)):
-                    for part in range(2):
-                        starts[residue, part, at] = value[part]
+                for residue, (real, imag) in enumerate(line_transform(blocks, 1.0)):
+                    if residue:
+                        cosine, sine = twist_ref[residue, 0], twist_ref[residue, 1]
+                        real, imag = real * cosine + imag * sine, imag * cosine - real * sine
+                    starts[residue, 0, at], starts[residue, 1, at] = real, imag
+
         def over_plane(fold):
-            for upper in range(FOLD):
-                residue = fold * FOLD + upper
-                parts = [jnp.concatenate([starts[residue, part, at] for at in range(0, size, SUBLANES)], axis=0) for part in range(2)]
-                parts = plane_transform(*parts, [plane_ref[0, residue, j] for j in range(2)])
-                for part in range(2):
-                    field_ref[fold, part, upper * BATCH * grid_size : upper * BATCH * grid_size + size] = parts[part]
+            residues = range(fold * FOLD, (fold + 1) * FOLD)
+            places = [(residue, at) for residue in residues for at in range(0, size, SUBLANES)]
+            parts = [jnp.concatenate([starts[residue, part, at] for residue, at in places], axis=0) for part in range(2)]
+            parts = plane_transform(*parts, [plane_ref[0, j] for j in range(2)])
+            for part in range(2):
+                for upper in range(FOLD):
+                    at = upper * BATCH * grid_size
+                    field_ref[fold, part, at : at + size] = parts[part][upper * size : (upper + 1) * size]
 
         def over_line(fold):
             for lane in range(lanes):
@@ -307,11 +314,13 @@
         ends = {}
 
         def back(fold):
+            parts = []
+            for part in range(2):
+                at = [upper * BATCH * grid_size for upper in range(FOLD)]
+                parts.append(jnp.concatenate([field_ref[fold, part, start : start + size] for start in at], axis=0))
+            parts = plane_transform(*parts, [plane_ref[1, j] for j in range(2)])
             for upper in range(FOLD):
-                residue = fold * FOLD + upper
-                parts = [field_ref[fold, part, upper * BATCH * grid_size : upper * BATCH * grid_size + size] for part in range(2)]
-                parts = plane_transform(*parts, [plane_ref[1, residue, j] for j in range(2)])
-                ends[residue] = parts
+                ends[fold * FOLD + upper] = [values[upper * size : (upper + 1) * size] for values in parts]
 
         folds = RADIX // FOLD
         for turn_number in range(folds + 2):
@@ -327,9 +336,14 @@
             for place in range(count):
                 aim = members[start + place][0]
                 at = slice(place * grid_size + tile, place * grid_size + tile + SUBLANES)
-                blocks = line_transform(
-                    [tuple(ends[residue][part][at] for part in range(2)) for residue in range(RADIX)], -1.0
-                )
+                blocks = []
+                for residue in range(RADIX):
+                    real, imag = (ends[residue][part][at] for part in range(2))
+                    if residue:
+                        cosine, sine = twist_ref[residue, 0], twist_ref[residue, 1]
+                        real, imag = real * cosine - imag * sine, imag * cosine + real * sine
+                    blocks.append((real, imag))
+                blocks = line_transform(blocks, -1.0)
                 for block, (pot_real, pot_imag) in enumerate(blocks):
                     real, imag = (held_ref[place, part, block, rows] for part in range(2))
                     totals[aim][block][0] -= real * pot_real - imag * pot_imag
@@ -349,7 +363,7 @@
 def exchange(orbitals, targets, first, tables, kernels, totals=(), **options):
     grid_size, plane = targets[0].shape[2:]
     room = padded(plane // RADIX)
-    given = [*orbitals, *targets, tables, kernels, *totals]
+    given = [*orbitals, *targets, *tables, kernels, *totals]
     whole = pl.BlockSpec(memory_space=pltpu.VMEM)
     return pl.pallas_call(
         functools.partial(exchange_body, len(orbitals), len(targets), first, len(totals) > 0),
@@ -359,7 +373,6 @@
         scratch_shapes=[
             pltpu.VMEM((RADIX // FOLD, 2, SUBLANES * grid_size, room), F32),
             pltpu.VMEM((BATCH, 2, RADIX, grid_size, room), F32),
-            pltpu.VMEM((RADIX, 2, BATCH * grid_size, room), F32),
         ],
         compiler_params=pltpu.CompilerParams(vmem_limit_bytes=SCOPED_BYTES),
         **options,
@@ -377,9 +390,9 @@
     near_steps = list(range(chips - 2, 0, -1))
     steps = [0, chips - 1] * (BATCH // 2) + near_steps
     steps += [0] * (-len(steps) % BATCH)
-    tables = jnp.asarray(plane_tables(targets.shape[2]))
-    kernel_blocks, shift, own, target, tables = prepare(
-        steps, partner, kernel_index, kernels, occupied, targets, tables
+    tables = [jnp.asarray(table(targets.shape[2])) for table in (plane_tables, twist_tables)]
+    kernel_blocks, shift, own, target, *tables = prepare(
+        steps, partner, kernel_index, kernels, occupied, targets, *tables
     )
     shifts = list(range(groups - 1, 0, -1))
     came = [lax.ppermute(occupied, "ka", [(i ^ by, i) for i in range(groups)]) for by in shifts]

time: 21 us -> 21 us (level)
  Pallas kernels: 6.33 us -> 5.45 us
  waiting for transfers between devices: 4.85 us -> 5.68 us
    ppermute x3, waiting for transfers between devices: 2 us -> 2.78 us  [shards(): lax.ppermute(occupied, 'ka', [(i ^ by, i) for i in range(groups)])]
    pallas_call x1, Pallas kernels: 2.3 us -> 1.53 us  [prepare(): pl.pallas_call(functools.partial(prepare_body, steps), out_shape=[pltpu.V...]
  transfers between devices with their start and end apart: 8 -> 8, of which waited for: 6 -> 7; matrix products, arithmetic and copies ran while one was open for 0% -> 0% of each run, Pallas kernels for 24% -> 21%
where the time goes in v6:
time: 21 us; the launch traced here: 20.8 us
  starting transfers between devices  8.99 us (43%)
  waiting for transfers between devices  5.68 us (27%)
  Pallas kernels  5.45 us (26%)
  other arithmetic  0.66 us (3%)
    ppermute x5, starting transfers between devices, along(): return lax.ppermute(array, 'band', [(i, i ^ by) for i in range(band_count)])  4.53 us
    ppermute x3, starting transfers between devices, shards(): lax.ppermute(occupied, 'ka', [(i ^ by, i) for i in range(groups)])  4.46 us
    pallas_call x3, Pallas kernels, exchange(): pl.pallas_call(functools.partial(exchange_body, len(orbitals), len(target...  3.92 us
    ppermute x5, waiting for transfers between devices, along(): return lax.ppermute(array, 'band', [(i, i ^ by) for i in range(band_count)])  2.9 us
    ppermute x3, waiting for transfers between devices, shards(): lax.ppermute(occupied, 'ka', [(i ^ by, i) for i in range(groups)])  2.78 us
    pallas_call x1, Pallas kernels, prepare(): pl.pallas_call(functools.partial(prepare_body, steps), out_shape=[pltpu.V...  1.53 us
    add x1, other arithmetic, shards(): return mine + came  0.66 us
  transfers between devices with their start and end apart: 8, of which 7 were waited for; matrix products, arithmetic and copies ran while one was open for 0% of the time, Pallas kernels for 21%

profile of v6, /device:TPU:0, one launch (start us, length us, event | category | flops | bytes accessed | tf_op | source)
XLA Modules:
  0.0 20.8 jit_solution(7519093508500911472)
XLA Ops:
  0.0 3.9 %collective-permute-start = (bf16[1,2,24,576]{3,2,1,0:T(8,128)(2,1)}, bf16[1,2,24,576]{3,2,1,0:T(8,128)(2,1)S(1)}, u32[]{:S(2)}, u32[]{:S(2)}) collective-permute-start(bf16[1,2,24,576]{3,2,1,0:T(8,128)(2,1)} %refs_0_.1), channel_id=1, source_target_pairs={{24,0},{16,8},{8,16},{0,24},{25,1},{17,9},{9,17},{1,25},{26,2},{18... | collective-permute-start | bytes 165896 | tf_op jit(solution)/shard_map/ppermute | solution.py:398
  3.9 0.5 %collective-permute-start.2 = (bf16[1,2,24,576]{3,2,1,0:T(8,128)(2,1)}, bf16[1,2,24,576]{3,2,1,0:T(8,128)(2,1)S(1)}, u32[]{:S(2)}, u32[]{:S(2)}) collective-permute-start(bf16[1,2,24,576]{3,2,1,0:T(8,128)(2,1)} %refs_0_.1), channel_id=1, source_target_pairs={{8,0},{0,8},{24,16},{16,24},{9,1},{1,9},{25,17},{17,25},{10,2},{2,... | collective-permute-start | bytes 165896 | tf_op jit(solution)/shard_map/ppermute | solution.py:398
  4.4 0.0 collective-permute-start.1
  4.5 1.5 %shard_map.73 = (f32[2,3,1,24,8,128]{5,4,3,2,1,0:T(8,128)S(1)}, s32[1]{0:T(128)S(4)}, bf16[1,2,24,576]{3,2,1,0:T(8,128)(2,1)S(1)}, f32[1,2,24,576]{3,2,1,0:T(8,1...) custom-call(s32[4]{0:T(128)} %partner_ref.1, s32[8,8]{1,0:T(8,128)} %index_ref.1, ...), custom_call_target="tpu_custom_call" | custom-call | tf_op jit(solution)/shard_map/pallas_call | solution.py:194
  6.0 0.1 collective-permute-start.6
  6.1 0.4 %collective-permute-done.refs_1_ = bf16[1,2,24,576]{3,2,1,0:T(8,128)(2,1)S(1)} collective-permute-done((bf16[1,2,24,576]{3,2,1,0:T(8,128)(2,1)}, bf16[1,2,24,576]{3,2,1,0:T(8,128)(2,1)S(1)}, u32[]{:S(2)}, u32[]{:S(2)}) %collective-permute-start) | collective-permute-done | bytes 55328 | tf_op jit(solution)/shard_map/ppermute | solution.py:398
  6.5 1.9 %collective-permute-done.2.refs_3_ = bf16[1,2,24,576]{3,2,1,0:T(8,128)(2,1)S(1)} collective-permute-done((bf16[1,2,24,576]{3,2,1,0:T(8,128)(2,1)}, bf16[1,2,24,576]{3,2,1,0:T(8,128)(2,1)S(1)}, u32[]{:S(2)}, u32[]{:S(2)}) %collective-permute-start.2) | collective-permute-done | bytes 55328 | tf_op jit(solution)/shard_map/ppermute | solution.py:398
  8.3 0.5 %collective-permute-done.1.refs_2_ = bf16[1,2,24,576]{3,2,1,0:T(8,128)(2,1)S(1)} collective-permute-done((bf16[1,2,24,576]{3,2,1,0:T(8,128)(2,1)}, bf16[1,2,24,576]{3,2,1,0:T(8,128)(2,1)S(1)}, u32[]{:S(2)}, u32[]{:S(2)}) %collective-permute-start.1) | collective-permute-done | bytes 55328 | tf_op jit(solution)/shard_map/ppermute | solution.py:398
  8.9 3.6 %collective-permute-start.5 = (bf16[1,2,24,576]{3,2,1,0:T(8,128)(2,1)S(1)}, bf16[1,2,24,576]{3,2,1,0:T(8,128)(2,1)S(1)}, u32[]{:S(2)}, u32[]{:S(2)}) collective-permute-start(bf16[1,2,24,576]{3,2,1,0:T(8,128)(2,1)S(1)} %shard_map.74.refs_0_), channel_id=1, source_target_pairs={{0,6},{1,7},{2,4},{3,5},{4,2},{5,3},{6,0},{7,1},{8,14},{9,15},{10,... | collective-permute-start | bytes 165896 | tf_op jit(solution)/shard_map/ppermute | solution.py:388
  12.5 0.0 collective-permute-start.4
  12.5 0.8 %collective-permute-start.3 = (bf16[1,2,24,576]{3,2,1,0:T(8,128)(2,1)S(1)}, bf16[1,2,24,576]{3,2,1,0:T(8,128)(2,1)S(1)}, u32[]{:S(2)}, u32[]{:S(2)}) collective-permute-start(bf16[1,2,24,576]{3,2,1,0:T(8,128)(2,1)S(1)} %shard_map.74.refs_0_), channel_id=1, source_target_pairs={{0,4},{1,5},{2,6},{3,7},{4,0},{5,1},{6,2},{7,3},{8,12},{9,13},{10,... | collective-permute-start | bytes 165896 | tf_op jit(solution)/shard_map/ppermute | solution.py:388
  13.3 1.7 %collective-permute-done.5.refs_1_ = bf16[1,2,24,576]{3,2,1,0:T(8,128)(2,1)S(1)} collective-permute-done((bf16[1,2,24,576]{3,2,1,0:T(8,128)(2,1)S(1)}, bf16[1,2,24,576]{3,2,1,0:T(8,128)(2,1)S(1)}, u32[]{:S(2)}, u32[]{:S(2)}) %collective-permute-start.5) | collective-permute-done | bytes 55328 | tf_op jit(solution)/shard_map/ppermute | solution.py:388
  14.9 0.0 collective-permute-done.6.refs_3_.refs_2_
  14.9 1.6 %shard_map.75 = (f32[1,2,24,576]{3,2,1,0:T(8,128)S(1)}, f32[1,2,24,576]{3,2,1,0:T(8,128)S(1)}) custom-call(bf16[1,2,24,576]{3,2,1,0:T(8,128)(2,1)S(1)} %shard_map.74.refs_0_, bf16[1,2,24,576]{3,2,1,0:T(8,128)(2,1)S(1)} %collective-permute-done.5.refs_1_, f32[1,2,24,576]{3,2,1,0:T(8,128)S(1)} %get-tuple-element.15.refs_2_, ...), custom_call_target="tpu_custom_call" | custom-call | tf_op jit(solution)/shard_map/pallas_call | solution.py:368
  16.5 0.2 collective-permute-done.4.refs_1_
  16.7 0.9 %collective-permute-done.3.refs_0_ = bf16[1,2,24,576]{3,2,1,0:T(8,128)(2,1)S(1)} collective-permute-done((bf16[1,2,24,576]{3,2,1,0:T(8,128)(2,1)S(1)}, bf16[1,2,24,576]{3,2,1,0:T(8,128)(2,1)S(1)}, u32[]{:S(2)}, u32[]{:S(2)}) %collective-permute-start.3) | collective-permute-done | bytes 55328 | tf_op jit(solution)/shard_map/ppermute | solution.py:388
  17.6 1.2 %shard_map.77 = f32[1,2,24,576]{3,2,1,0:T(8,128)S(1)} custom-call(bf16[1,2,24,576]{3,2,1,0:T(8,128)(2,1)S(1)} %collective-permute-done.3.refs_0_, bf16[1,2,24,576]{3,2,1,0:T(8,128)(2,1)S(1)} %collective-permute-done.4.refs_1_, f32[1,2,24,576]{3,2,1,0:T(8,128)S(1)} %collective-permute-done.6.refs_3_.refs_2_, ...), custom_call_target="tpu_custom_call" | custom-call | tf_op jit(solution)/shard_map/pallas_call | solution.py:368
  18.8 0.1 collective-permute-start.7
  18.9 1.2 %shard_map.76 = f32[1,2,24,576]{3,2,1,0:T(8,128)S(1)} custom-call(bf16[1,2,24,576]{3,2,1,0:T(8,128)(2,1)S(1)} %collective-permute-done.3.refs_0_, bf16[1,2,24,576]{3,2,1,0:T(8,128)(2,1)S(1)} %collective-permute-done.4.refs_1_, f32[1,2,24,576]{3,2,1,0:T(8,128)S(1)} %get-tuple-element.15.refs_2_, ...), custom_call_target="tpu_custom_call" | custom-call | tf_op jit(solution)/shard_map/pallas_call | solution.py:368
  20.0 0.1 collective-permute-done.7
  20.2 0.7 %add.3 = f32[1,2,24,576]{3,2,1,0:T(8,128)} add(f32[1,2,24,576]{3,2,1,0:T(8,128)S(1)} %shard_map.76, f32[1,2,24,576]{3,2,1,0:T(8,128)S(1)} %collective-permute-done.7) | non-fusion elementwise | flops 27648 | bytes 331776 | tf_op jit(solution)/shard_map/add | solution.py:409
  (1 shorter events, 0.0 us)
Async XLA Ops:
  0.0 6.5 %collective-permute-start = (bf16[1,2,24,576]{3,2,1,0:T(8,128)(2,1)}, bf16[1,2,24,576]{3,2,1,0:T(8,128)(2,1)S(1)}, u32[]{:S(2)}, u32[]{:S(2)}) collective-permute-start(bf16[1,2,24,576]{3,2,1,0:T(8,128)(2,1)} %refs_0_.1), channel_id=1, source_target_pairs={{24,0},{16,8},{8,16},{0,24},{25,1},{17,9},{9,17},{1,25},{26,2},{18... | collective-permute-start | bytes 165896 | tf_op jit(solution)/shard_map/ppermute | solution.py:398
  3.9 4.4 %collective-permute-start.2 = (bf16[1,2,24,576]{3,2,1,0:T(8,128)(2,1)}, bf16[1,2,24,576]{3,2,1,0:T(8,128)(2,1)S(1)}, u32[]{:S(2)}, u32[]{:S(2)}) collective-permute-start(bf16[1,2,24,576]{3,2,1,0:T(8,128)(2,1)} %refs_0_.1), channel_id=1, source_target_pairs={{8,0},{0,8},{24,16},{16,24},{9,1},{1,9},{25,17},{17,25},{10,2},{2,... | collective-permute-start | bytes 165896 | tf_op jit(solution)/shard_map/ppermute | solution.py:398
  4.4 4.4 %collective-permute-start.1 = (bf16[1,2,24,576]{3,2,1,0:T(8,128)(2,1)}, bf16[1,2,24,576]{3,2,1,0:T(8,128)(2,1)S(1)}, u32[]{:S(2)}, u32[]{:S(2)}) collective-permute-start(bf16[1,2,24,576]{3,2,1,0:T(8,128)(2,1)} %refs_0_.1), channel_id=1, source_target_pairs={{16,0},{24,8},{0,16},{8,24},{17,1},{25,9},{1,17},{9,25},{18,2},{26... | collective-permute-start | bytes 165896 | tf_op jit(solution)/shard_map/ppermute | solution.py:398
  6.0 8.9 %collective-permute-start.6 = (f32[1,2,24,576]{3,2,1,0:T(8,128)S(1)}, f32[1,2,24,576]{3,2,1,0:T(8,128)S(1)}, u32[]{:S(2)}, u32[]{:S(2)}) collective-permute-start(f32[1,2,24,576]{3,2,1,0:T(8,128)S(1)} %get-tuple-element.15.refs_2_), channel_id=1, source_target_pairs={{0,1},{1,0},{2,3},{3,2},{4,5},{5,4},{6,7},{7,6},{8,9},{9,8},{10,11... | collective-permute-start | bytes 331784 | tf_op jit(solution)/shard_map/ppermute | solution.py:388
  8.9 6.1 %collective-permute-start.5 = (bf16[1,2,24,576]{3,2,1,0:T(8,128)(2,1)S(1)}, bf16[1,2,24,576]{3,2,1,0:T(8,128)(2,1)S(1)}, u32[]{:S(2)}, u32[]{:S(2)}) collective-permute-start(bf16[1,2,24,576]{3,2,1,0:T(8,128)(2,1)S(1)} %shard_map.74.refs_0_), channel_id=1, source_target_pairs={{0,6},{1,7},{2,4},{3,5},{4,2},{5,3},{6,0},{7,1},{8,14},{9,15},{10,... | collective-permute-start | bytes 165896 | tf_op jit(solution)/shard_map/ppermute | solution.py:388
  12.5 4.2 %collective-permute-start.4 = (bf16[1,2,24,576]{3,2,1,0:T(8,128)(2,1)S(1)}, bf16[1,2,24,576]{3,2,1,0:T(8,128)(2,1)S(1)}, u32[]{:S(2)}, u32[]{:S(2)}) collective-permute-start(bf16[1,2,24,576]{3,2,1,0:T(8,128)(2,1)S(1)} %shard_map.74.refs_0_), channel_id=1, source_target_pairs={{0,2},{1,3},{2,0},{3,1},{4,6},{5,7},{6,4},{7,5},{8,10},{9,11},{10,... | collective-permute-start | bytes 165896 | tf_op jit(solution)/shard_map/ppermute | solution.py:388
  12.5 5.1 %collective-permute-start.3 = (bf16[1,2,24,576]{3,2,1,0:T(8,128)(2,1)S(1)}, bf16[1,2,24,576]{3,2,1,0:T(8,128)(2,1)S(1)}, u32[]{:S(2)}, u32[]{:S(2)}) collective-permute-start(bf16[1,2,24,576]{3,2,1,0:T(8,128)(2,1)S(1)} %shard_map.74.refs_0_), channel_id=1, source_target_pairs={{0,4},{1,5},{2,6},{3,7},{4,0},{5,1},{6,2},{7,3},{8,12},{9,13},{10,... | collective-permute-start | bytes 165896 | tf_op jit(solution)/shard_map/ppermute | solution.py:388
  18.8 1.4 %collective-permute-start.7 = (f32[1,2,24,576]{3,2,1,0:T(8,128)S(1)}, f32[1,2,24,576]{3,2,1,0:T(8,128)S(1)}, u32[]{:S(2)}, u32[]{:S(2)}) collective-permute-start(f32[1,2,24,576]{3,2,1,0:T(8,128)S(1)} %shard_map.77), channel_id=1, source_target_pairs={{0,1},{1,0},{2,3},{3,2},{4,5},{5,4},{6,7},{7,6},{8,9},{9,8},{10,11... | collective-permute-start | bytes 331784 | tf_op jit(solution)/shard_map/ppermute | solution.py:388

commit v7 on v6

--- a/solution.py
+++ b/solution.py
@@ -398,7 +398,7 @@
     came = [lax.ppermute(occupied, "ka", [(i ^ by, i) for i in range(groups)]) for by in shifts]
     visitor = choose(shift, [0, *shifts], [own, *came])
 
-    sibling = along(target, 1)
+    sibling = along(targets, 1)
     early = [visitor, along(visitor, 2 * (chips - 1))]
     late = [along(visitor, 2 * step) for step in near_steps]
     free = pl.CostEstimate(flops=0, bytes_accessed=0, transcendentals=0)

time: 21 us -> 21 us (level)
  no operation moved by 1% of the time
where the time goes in v7:
time: 21 us; the launch traced here: 20.8 us
  starting transfers between devices  8.92 us (42%)
  waiting for transfers between devices  5.77 us (27%)
  Pallas kernels  5.44 us (26%)
  other arithmetic  0.66 us (3%)
    ppermute x5, starting transfers between devices, along(): return lax.ppermute(array, 'band', [(i, i ^ by) for i in range(band_count)])  4.46 us
    ppermute x3, starting transfers between devices, shards(): lax.ppermute(occupied, 'ka', [(i ^ by, i) for i in range(groups)])  4.46 us
    pallas_call x3, Pallas kernels, exchange(): pl.pallas_call(functools.partial(exchange_body, len(orbitals), len(target...  3.91 us
    ppermute x5, waiting for transfers between devices, along(): return lax.ppermute(array, 'band', [(i, i ^ by) for i in range(band_count)])  2.91 us
    ppermute x3, waiting for transfers between devices, shards(): lax.ppermute(occupied, 'ka', [(i ^ by, i) for i in range(groups)])  2.86 us
    pallas_call x1, Pallas kernels, prepare(): pl.pallas_call(functools.partial(prepare_body, steps), out_shape=[pltpu.V...  1.53 us
    add x1, other arithmetic, shards(): return mine + came  0.66 us
  transfers between devices with their start and end apart: 8, of which 7 were waited for; matrix products, arithmetic and copies ran while one was open for 0% of the time, Pallas kernels for 21%

profile of v7, /device:TPU:0, one launch (start us, length us, event | category | flops | bytes accessed | tf_op | source)
XLA Modules:
  0.0 20.8 jit_solution(8582881799699405666)
XLA Ops:
  0.0 3.9 %collective-permute-start = (bf16[1,2,24,576]{3,2,1,0:T(8,128)(2,1)}, bf16[1,2,24,576]{3,2,1,0:T(8,128)(2,1)S(1)}, u32[]{:S(2)}, u32[]{:S(2)}) collective-permute-start(bf16[1,2,24,576]{3,2,1,0:T(8,128)(2,1)} %refs_0_.1), channel_id=1, source_target_pairs={{24,0},{16,8},{8,16},{0,24},{25,1},{17,9},{9,17},{1,25},{26,2},{18... | collective-permute-start | bytes 165896 | tf_op jit(solution)/shard_map/ppermute | solution.py:398
  3.9 0.5 %collective-permute-start.2 = (bf16[1,2,24,576]{3,2,1,0:T(8,128)(2,1)}, bf16[1,2,24,576]{3,2,1,0:T(8,128)(2,1)S(1)}, u32[]{:S(2)}, u32[]{:S(2)}) collective-permute-start(bf16[1,2,24,576]{3,2,1,0:T(8,128)(2,1)} %refs_0_.1), channel_id=1, source_target_pairs={{8,0},{0,8},{24,16},{16,24},{9,1},{1,9},{25,17},{17,25},{10,2},{2,... | collective-permute-start | bytes 165896 | tf_op jit(solution)/shard_map/ppermute | solution.py:398
  4.4 0.0 collective-permute-start.1
  4.5 0.0 collective-permute-start.6
  4.5 1.5 %shard_map.73 = (f32[2,3,1,24,8,128]{5,4,3,2,1,0:T(8,128)S(1)}, s32[1]{0:T(128)S(4)}, bf16[1,2,24,576]{3,2,1,0:T(8,128)(2,1)S(1)}, f32[1,2,24,576]{3,2,1,0:T(8,1...) custom-call(s32[4]{0:T(128)} %partner_ref.1, s32[8,8]{1,0:T(8,128)} %index_ref.1, ...), custom_call_target="tpu_custom_call" | custom-call | tf_op jit(solution)/shard_map/pallas_call | solution.py:194
  6.0 0.5 %collective-permute-done.refs_1_ = bf16[1,2,24,576]{3,2,1,0:T(8,128)(2,1)S(1)} collective-permute-done((bf16[1,2,24,576]{3,2,1,0:T(8,128)(2,1)}, bf16[1,2,24,576]{3,2,1,0:T(8,128)(2,1)S(1)}, u32[]{:S(2)}, u32[]{:S(2)}) %collective-permute-start) | collective-permute-done | bytes 55328 | tf_op jit(solution)/shard_map/ppermute | solution.py:398
  6.5 1.9 %collective-permute-done.2.refs_3_ = bf16[1,2,24,576]{3,2,1,0:T(8,128)(2,1)S(1)} collective-permute-done((bf16[1,2,24,576]{3,2,1,0:T(8,128)(2,1)}, bf16[1,2,24,576]{3,2,1,0:T(8,128)(2,1)S(1)}, u32[]{:S(2)}, u32[]{:S(2)}) %collective-permute-start.2) | collective-permute-done | bytes 55328 | tf_op jit(solution)/shard_map/ppermute | solution.py:398
  8.3 0.5 %collective-permute-done.1.refs_2_ = bf16[1,2,24,576]{3,2,1,0:T(8,128)(2,1)S(1)} collective-permute-done((bf16[1,2,24,576]{3,2,1,0:T(8,128)(2,1)}, bf16[1,2,24,576]{3,2,1,0:T(8,128)(2,1)S(1)}, u32[]{:S(2)}, u32[]{:S(2)}) %collective-permute-start.1) | collective-permute-done | bytes 55328 | tf_op jit(solution)/shard_map/ppermute | solution.py:398
  8.9 3.6 %collective-permute-start.5 = (bf16[1,2,24,576]{3,2,1,0:T(8,128)(2,1)S(1)}, bf16[1,2,24,576]{3,2,1,0:T(8,128)(2,1)S(1)}, u32[]{:S(2)}, u32[]{:S(2)}) collective-permute-start(bf16[1,2,24,576]{3,2,1,0:T(8,128)(2,1)S(1)} %shard_map.74.refs_0_), channel_id=1, source_target_pairs={{0,6},{1,7},{2,4},{3,5},{4,2},{5,3},{6,0},{7,1},{8,14},{9,15},{10,... | collective-permute-start | bytes 165896 | tf_op jit(solution)/shard_map/ppermute | solution.py:388
  12.5 0.0 collective-permute-start.4
  12.5 0.8 %collective-permute-start.3 = (bf16[1,2,24,576]{3,2,1,0:T(8,128)(2,1)S(1)}, bf16[1,2,24,576]{3,2,1,0:T(8,128)(2,1)S(1)}, u32[]{:S(2)}, u32[]{:S(2)}) collective-permute-start(bf16[1,2,24,576]{3,2,1,0:T(8,128)(2,1)S(1)} %shard_map.74.refs_0_), channel_id=1, source_target_pairs={{0,4},{1,5},{2,6},{3,7},{4,0},{5,1},{6,2},{7,3},{8,12},{9,13},{10,... | collective-permute-start | bytes 165896 | tf_op jit(solution)/shard_map/ppermute | solution.py:388
  13.3 0.0 collective-permute-done.6.refs_3_.refs_2_
  13.3 1.7 %collective-permute-done.5.refs_1_ = bf16[1,2,24,576]{3,2,1,0:T(8,128)(2,1)S(1)} collective-permute-done((bf16[1,2,24,576]{3,2,1,0:T(8,128)(2,1)S(1)}, bf16[1,2,24,576]{3,2,1,0:T(8,128)(2,1)S(1)}, u32[]{:S(2)}, u32[]{:S(2)}) %collective-permute-start.5) | collective-permute-done | bytes 55328 | tf_op jit(solution)/shard_map/ppermute | solution.py:388
  14.9 1.6 %shard_map.75 = (f32[1,2,24,576]{3,2,1,0:T(8,128)S(1)}, f32[1,2,24,576]{3,2,1,0:T(8,128)S(1)}) custom-call(bf16[1,2,24,576]{3,2,1,0:T(8,128)(2,1)S(1)} %shard_map.74.refs_0_, bf16[1,2,24,576]{3,2,1,0:T(8,128)(2,1)S(1)} %collective-permute-done.5.refs_1_, f32[1,2,24,576]{3,2,1,0:T(8,128)S(1)} %get-tuple-element.15.refs_2_, ...), custom_call_target="tpu_custom_call" | custom-call | tf_op jit(solution)/shard_map/pallas_call | solution.py:368
  16.5 0.2 collective-permute-done.4.refs_1_
  16.7 0.9 %collective-permute-done.3.refs_0_ = bf16[1,2,24,576]{3,2,1,0:T(8,128)(2,1)S(1)} collective-permute-done((bf16[1,2,24,576]{3,2,1,0:T(8,128)(2,1)S(1)}, bf16[1,2,24,576]{3,2,1,0:T(8,128)(2,1)S(1)}, u32[]{:S(2)}, u32[]{:S(2)}) %collective-permute-start.3) | collective-permute-done | bytes 55328 | tf_op jit(solution)/shard_map/ppermute | solution.py:388
  17.6 1.2 %shard_map.77 = f32[1,2,24,576]{3,2,1,0:T(8,128)S(1)} custom-call(bf16[1,2,24,576]{3,2,1,0:T(8,128)(2,1)S(1)} %collective-permute-done.3.refs_0_, bf16[1,2,24,576]{3,2,1,0:T(8,128)(2,1)S(1)} %collective-permute-done.4.refs_1_, f32[1,2,24,576]{3,2,1,0:T(8,128)S(1)} %collective-permute-done.6.refs_3_.refs_2_, ...), custom_call_target="tpu_custom_call" | custom-call | tf_op jit(solution)/shard_map/pallas_call | solution.py:368
  18.8 0.1 collective-permute-start.7
  18.9 1.2 %shard_map.76 = f32[1,2,24,576]{3,2,1,0:T(8,128)S(1)} custom-call(bf16[1,2,24,576]{3,2,1,0:T(8,128)(2,1)S(1)} %collective-permute-done.3.refs_0_, bf16[1,2,24,576]{3,2,1,0:T(8,128)(2,1)S(1)} %collective-permute-done.4.refs_1_, f32[1,2,24,576]{3,2,1,0:T(8,128)S(1)} %get-tuple-element.15.refs_2_, ...), custom_call_target="tpu_custom_call" | custom-call | tf_op jit(solution)/shard_map/pallas_call | solution.py:368
  20.0 0.1 collective-permute-done.7
  20.2 0.7 %add.3 = f32[1,2,24,576]{3,2,1,0:T(8,128)} add(f32[1,2,24,576]{3,2,1,0:T(8,128)S(1)} %shard_map.76, f32[1,2,24,576]{3,2,1,0:T(8,128)S(1)} %collective-permute-done.7) | non-fusion elementwise | flops 27648 | bytes 331776 | tf_op jit(solution)/shard_map/add | solution.py:409
  (1 shorter events, 0.0 us)
Async XLA Ops:
  0.0 6.5 %collective-permute-start = (bf16[1,2,24,576]{3,2,1,0:T(8,128)(2,1)}, bf16[1,2,24,576]{3,2,1,0:T(8,128)(2,1)S(1)}, u32[]{:S(2)}, u32[]{:S(2)}) collective-permute-start(bf16[1,2,24,576]{3,2,1,0:T(8,128)(2,1)} %refs_0_.1), channel_id=1, source_target_pairs={{24,0},{16,8},{8,16},{0,24},{25,1},{17,9},{9,17},{1,25},{26,2},{18... | collective-permute-start | bytes 165896 | tf_op jit(solution)/shard_map/ppermute | solution.py:398
  3.9 4.4 %collective-permute-start.2 = (bf16[1,2,24,576]{3,2,1,0:T(8,128)(2,1)}, bf16[1,2,24,576]{3,2,1,0:T(8,128)(2,1)S(1)}, u32[]{:S(2)}, u32[]{:S(2)}) collective-permute-start(bf16[1,2,24,576]{3,2,1,0:T(8,128)(2,1)} %refs_0_.1), channel_id=1, source_target_pairs={{8,0},{0,8},{24,16},{16,24},{9,1},{1,9},{25,17},{17,25},{10,2},{2,... | collective-permute-start | bytes 165896 | tf_op jit(solution)/shard_map/ppermute | solution.py:398
  4.4 4.4 %collective-permute-start.1 = (bf16[1,2,24,576]{3,2,1,0:T(8,128)(2,1)}, bf16[1,2,24,576]{3,2,1,0:T(8,128)(2,1)S(1)}, u32[]{:S(2)}, u32[]{:S(2)}) collective-permute-start(bf16[1,2,24,576]{3,2,1,0:T(8,128)(2,1)} %refs_0_.1), channel_id=1, source_target_pairs={{16,0},{24,8},{0,16},{8,24},{17,1},{25,9},{1,17},{9,25},{18,2},{26... | collective-permute-start | bytes 165896 | tf_op jit(solution)/shard_map/ppermute | solution.py:398
  4.5 8.8 %collective-permute-start.6 = (f32[1,2,24,576]{3,2,1,0:T(8,128)}, f32[1,2,24,576]{3,2,1,0:T(8,128)S(1)}, u32[]{:S(2)}, u32[]{:S(2)}) collective-permute-start(f32[1,2,24,576]{3,2,1,0:T(8,128)} %refs_1_.1), channel_id=1, source_target_pairs={{0,1},{1,0},{2,3},{3,2},{4,5},{5,4},{6,7},{7,6},{8,9},{9,8},{10,11... | collective-permute-start | bytes 331784 | tf_op jit(solution)/shard_map/ppermute | solution.py:388
  8.9 6.1 %collective-permute-start.5 = (bf16[1,2,24,576]{3,2,1,0:T(8,128)(2,1)S(1)}, bf16[1,2,24,576]{3,2,1,0:T(8,128)(2,1)S(1)}, u32[]{:S(2)}, u32[]{:S(2)}) collective-permute-start(bf16[1,2,24,576]{3,2,1,0:T(8,128)(2,1)S(1)} %shard_map.74.refs_0_), channel_id=1, source_target_pairs={{0,6},{1,7},{2,4},{3,5},{4,2},{5,3},{6,0},{7,1},{8,14},{9,15},{10,... | collective-permute-start | bytes 165896 | tf_op jit(solution)/shard_map/ppermute | solution.py:388
  12.5 4.2 %collective-permute-start.4 = (bf16[1,2,24,576]{3,2,1,0:T(8,128)(2,1)S(1)}, bf16[1,2,24,576]{3,2,1,0:T(8,128)(2,1)S(1)}, u32[]{:S(2)}, u32[]{:S(2)}) collective-permute-start(bf16[1,2,24,576]{3,2,1,0:T(8,128)(2,1)S(1)} %shard_map.74.refs_0_), channel_id=1, source_target_pairs={{0,2},{1,3},{2,0},{3,1},{4,6},{5,7},{6,4},{7,5},{8,10},{9,11},{10,... | collective-permute-start | bytes 165896 | tf_op jit(solution)/shard_map/ppermute | solution.py:388
  12.5 5.1 %collective-permute-start.3 = (bf16[1,2,24,576]{3,2,1,0:T(8,128)(2,1)S(1)}, bf16[1,2,24,576]{3,2,1,0:T(8,128)(2,1)S(1)}, u32[]{:S(2)}, u32[]{:S(2)}) collective-permute-start(bf16[1,2,24,576]{3,2,1,0:T(8,128)(2,1)S(1)} %shard_map.74.refs_0_), channel_id=1, source_target_pairs={{0,4},{1,5},{2,6},{3,7},{4,0},{5,1},{6,2},{7,3},{8,12},{9,13},{10,... | collective-permute-start | bytes 165896 | tf_op jit(solution)/shard_map/ppermute | solution.py:388
  18.8 1.4 %collective-permute-start.7 = (f32[1,2,24,576]{3,2,1,0:T(8,128)S(1)}, f32[1,2,24,576]{3,2,1,0:T(8,128)S(1)}, u32[]{:S(2)}, u32[]{:S(2)}) collective-permute-start(f32[1,2,24,576]{3,2,1,0:T(8,128)S(1)} %shard_map.77), channel_id=1, source_target_pairs={{0,1},{1,0},{2,3},{3,2},{4,5},{5,4},{6,7},{7,6},{8,9},{9,8},{10,11... | collective-permute-start | bytes 331784 | tf_op jit(solution)/shard_map/ppermute | solution.py:388
